TPU v7x, 32 devices: a whole 2x2x4 slice. The times are simulated.
32 devices in a mesh: nodes: 8 (over z, y), feat: 4 (over x, core).
Axes of the slice: x: 2, y: 2, z: 4, core: 2. Of those that a mesh axis runs over, the one named last changes fastest.
Arguments:
- features: bfloat16 [65536, 256], P('nodes', 'feat'), may hold values from -6 to 6
- degrees: int32 [65536], P('nodes'), may hold values from 1 to 16
- edge_weights: bfloat16 [2048, 128, 128], P('nodes'), may hold values from 0 to 0.099609375
- block_rows: int32 [2048], P('nodes'), may hold values from 0 to 63
- block_cols: int32 [2048], P('nodes'), may hold values from 0 to 111, as said below
- block_counts: int32 [8], P('nodes'), may hold values from 112 to 256, as said below
- send_lists: int32 [8, 3, 16], P('nodes'), may hold values from 0 to 63, as said below
- w_self: bfloat16 [256, 256], P(None, 'feat'), may hold values from -0.375 to 0.375
- w_neigh: bfloat16 [256, 256], P(None, 'feat'), may hold values from -0.375 to 0.375
- cotangent: bfloat16 [65536, 256], P('nodes', 'feat'), may hold values from -6 to 6
Outputs:
- mixed: bfloat16 [65536, 256], P('nodes', 'feat')
- grad_features: bfloat16 [65536, 256], P('nodes', 'feat')
- grad_self: float32 [256, 256], P(None, 'feat')
- grad_neigh: float32 [256, 256], P(None, 'feat')
Inputs may be any that keep to these rules, and one draw needn't show every extreme that they name: `block_cols`: on each device, slots 0 to 111 name every extended block once; the other slots name any. A device uses its first block_counts slots. `send_lists`: the 16 entries of one device and level are distinct.
All inputs are finite; a program needn't handle non-finite values.
Results may differ from a plain program's by a relative error of at most 0.0065.
Values may be sent and summed in bfloat16 or wider, within the bound.
A program may use at most 192 MiB of HBM per device.

v0:
```python
import jax
import jax.numpy as jnp
from jax import lax
from jax.sharding import PartitionSpec as P

gelu_scale = 0.7978845608028654
gelu_cubic = 0.044715


def partner(value, axis, apart):
    return lax.ppermute(value, axis, [(i, i ^ 1 << apart) for i in range(lax.axis_size(axis))])


def gelu_value(values):
    inner = gelu_scale * (values + gelu_cubic * values * values * values)
    return 0.5 * values * (1.0 + jnp.tanh(inner))


def gelu_slope(values):
    inner = gelu_scale * (values + gelu_cubic * values * values * values)
    tanh_inner = jnp.tanh(inner)
    return 0.5 * (1.0 + tanh_inner) + 0.5 * values * (
        1.0 - tanh_inner * tanh_inner
    ) * gelu_scale * (1.0 + 3.0 * gelu_cubic * values * values)


def selector(targets, active, total):
    match = targets[None, :] == lax.iota(jnp.int32, total)[:, None]
    return (match & active[None, :]).astype(jnp.float32)


def gather_sum(edge_weights, table, block_cols, block_rows, active, own_blocks):
    picked = jnp.take(table, block_cols, axis=0)
    product = jnp.einsum("sij,sjf->sif", edge_weights, picked, preferred_element_type=jnp.float32)
    onehot = selector(block_rows, active, own_blocks)
    return jnp.dot(onehot, product.reshape(product.shape[0], -1), precision=lax.Precision.HIGHEST)


def spread_back(edge_weights, table, block_rows, block_cols, active, extended_count):
    picked = jnp.take(table, block_rows, axis=0)
    product = jnp.einsum("sji,sjf->sif", edge_weights, picked, preferred_element_type=jnp.float32)
    onehot = selector(block_cols, active, extended_count)
    summed = jnp.dot(onehot, product.reshape(product.shape[0], -1), precision=lax.Precision.HIGHEST)
    return summed.reshape(extended_count, table.shape[1], table.shape[2])


def fetch_narrow(blocks, sends, levels):
    pieces = [blocks]
    for level in range(levels):
        pieces.append(partner(jnp.take(blocks, sends[level], axis=0), "nodes", level))
    return jnp.concatenate(pieces, axis=0)


def gradient_total(terms):
    return lax.psum((terms[0], terms[1]), "nodes")


def local(
    features,
    degrees,
    edge_weights,
    block_rows,
    block_cols,
    block_counts,
    send_lists,
    w_self,
    w_neigh,
    cotangent,
):
    row_count = features.shape[0]
    local_width = features.shape[1]
    slot_count = edge_weights.shape[0]
    block_size = edge_weights.shape[1]
    own_blocks = row_count // block_size
    border_size = send_lists.shape[2]
    levels = lax.axis_size("nodes").bit_length() - 1
    extended_count = own_blocks + levels * border_size
    active = lax.iota(jnp.int32, slot_count) < block_counts[0]
    inverse = 1.0 / degrees.astype(jnp.float32)[:, None]
    whole_self, whole_neigh = (
        lax.all_gather(w_self, "feat", axis=1, tiled=True),
        lax.all_gather(w_neigh, "feat", axis=1, tiled=True),
    )
    start_row = lax.axis_index("feat") * local_width
    rows_self = lax.dynamic_slice_in_dim(whole_self, start_row, local_width, 0)
    rows_neigh = lax.dynamic_slice_in_dim(whole_neigh, start_row, local_width, 0)
    table = fetch_narrow(
        features.reshape(own_blocks, block_size, local_width), send_lists[0], levels
    )
    summed = gather_sum(edge_weights, table, block_cols, block_rows, active, own_blocks)
    aggregated = (summed.reshape(row_count, local_width) * inverse).astype(jnp.bfloat16)
    whole_rows, whole_agg = (
        lax.all_gather(features, "feat", axis=1, tiled=True),
        lax.all_gather(aggregated, "feat", axis=1, tiled=True),
    )
    preact = jnp.dot(whole_rows, w_self, preferred_element_type=jnp.float32) + jnp.dot(
        whole_agg, w_neigh, preferred_element_type=jnp.float32
    )
    mixed = gelu_value(preact).astype(jnp.bfloat16)
    pre_grad = (cotangent.astype(jnp.float32) * gelu_slope(preact)).astype(jnp.bfloat16)
    whole_grad = lax.all_gather(pre_grad, "feat", axis=1, tiled=True)
    grad_self, grad_neigh = gradient_total(
        (
            jnp.dot(whole_rows.T, pre_grad, preferred_element_type=jnp.float32),
            jnp.dot(whole_agg.T, pre_grad, preferred_element_type=jnp.float32),
        )
    )
    direct = jnp.dot(whole_grad, rows_self.T, preferred_element_type=jnp.float32)
    scaled = (
        jnp.dot(whole_grad, rows_neigh.T, preferred_element_type=jnp.float32) * inverse
    ).astype(jnp.bfloat16)
    spread = spread_back(
        edge_weights,
        scaled.reshape(own_blocks, block_size, local_width),
        block_rows,
        block_cols,
        active,
        extended_count,
    )
    total = spread[:own_blocks]
    for level in range(levels):
        first = own_blocks + level * border_size
        piece = lax.slice_in_dim(spread, first, first + border_size, axis=0)
        returned = partner(piece.astype(jnp.bfloat16), "nodes", level).astype(piece.dtype)
        total = total.at[send_lists[0, level]].add(returned)
    grad_features = (direct + total.reshape(row_count, local_width)).astype(jnp.bfloat16)
    return (mixed, grad_features, grad_self, grad_neigh)


def solution(mesh):
    in_specs = (
        P("nodes", "feat"),
        P("nodes"),
        P("nodes", None, None),
        P("nodes"),
        P("nodes"),
        P("nodes"),
        P("nodes", None, None),
        P(None, "feat"),
        P(None, "feat"),
        P("nodes", "feat"),
    )
    out_specs = (P("nodes", "feat"), P("nodes", "feat"), P(None, "feat"), P(None, "feat"))
    return jax.shard_map(local, mesh=mesh, in_specs=in_specs, out_specs=out_specs, check_vma=False)
```

profile of v0, /device:TPU:0, one launch (start us, length us, event | category | flops | bytes accessed | tf_op | source)
XLA Modules:
  0.0 271.4 jit_solution(11895584444448632408)
XLA Ops:
  7.2 0.0 all-gather.4.cloned.1.call-start
  7.2 0.7 all-gather.4.cloned.1.call-update
  7.9 0.0 all-gather.6.cloned.1.call-start
  7.9 0.7 compare_and_fusion.2
  8.7 1.5 copy_bitcast_fusion.1
  10.2 0.6 gather_fusion.2
  10.8 0.1 broadcast_select_fusion.2
  10.9 3.0 %collective-permute-start = (bf16[16,128,64]{1,2,0:T(8,128)(2,1)S(1)}, bf16[16,128,64]{1,2,0:T(8,128)(2,1)S(1)}, u32[]{:S(2)}, u32[]{:S(2)}) collective-permute-start(bf16[16,128,64]{1,2,0:T(8,128)(2,1)S(1)} %broadcast_select_fusion.2), channel_id=1, source_target_pairs={{0,4},{4,0},{8,12},{12,8},{16,20},{20,16},{24,28},{28,24},{1,5},{5... | collective-permute-start | bytes 786440 | tf_op jit(solution)/shard_map/ppermute | solution.py:11
  13.9 0.6 gather_fusion.3
  14.5 0.1 broadcast_select_fusion.1
  14.6 1.6 collective-permute-start.1
  16.3 0.6 gather_fusion.4
  16.9 0.1 broadcast_select_fusion
  17.0 2.7 collective-permute-start.2
  20.4 6.8 %collective-permute-done.1 = bf16[16,128,64]{1,2,0:T(8,128)(2,1)S(1)} collective-permute-done((bf16[16,128,64]{1,2,0:T(8,128)(2,1)S(1)}, bf16[16,128,64]{1,2,0:T(8,128)(2,1)S(1)}, u32[]{:S(2)}, u32[]{:S(2)}) %collective-permute-start.1) | collective-permute-done | bytes 262176 | tf_op jit(solution)/shard_map/ppermute | solution.py:11
  27.2 3.9 %collective-permute-done.2 = bf16[16,128,64]{1,2,0:T(8,128)(2,1)S(1)} collective-permute-done((bf16[16,128,64]{1,2,0:T(8,128)(2,1)S(1)}, bf16[16,128,64]{1,2,0:T(8,128)(2,1)S(1)}, u32[]{:S(2)}, u32[]{:S(2)}) %collective-permute-start.2) | collective-permute-done | bytes 262176 | tf_op jit(solution)/shard_map/ppermute | solution.py:11
  31.1 0.3 pad_maximum_fusion
  31.4 3.1 %gather_fusion = bf16[256,128,64]{1,2,0:T(8,128)(2,1)} fusion(bf16[112,128,64]{1,2,0:T(8,128)(2,1)S(1)} %pad_maximum_fusion, s32[1024]{0:T(1024)S(1)} %pad_clamp_fusion.1), kind=kCustom, calls=%fused_computation.3 | custom fusion | bytes 8389632 | tf_op jit(solution)/shard_map/jit(_take)/gather | solution.py:33
  34.4 13.7 %fusion.7 = f32[256,128,64]{1,2,0:T(8,128)} fusion(bf16[256,128,128]{2,1,0:T(8,128)(2,1)} %param.14, bf16[256,128,64]{1,2,0:T(8,128)(2,1)} %gather_fusion, pred[256]{0:T(512)(128)(4,1)S(1)} %compare_and_fusion.4), kind=kOutput, calls=%fused_computation.17 | convolution fusion | flops 538968064 | bytes 20971776 | tf_op jit(solution)/shard_map/sij,sjf->sif/dot_general | solution.py:34
  48.1 9.3 %copy.46 = f32[256,128,64]{0,2,1:T(8,128)} copy(f32[256,128,64]{1,2,0:T(8,128)} %fusion.7) | data formatting | bytes 16777216 | tf_op jit(solution)/shard_map/sij,sjf->sif/dot_general | solution.py:34
  57.5 7.7 %fusion.33 = f32[64,8192]{1,0:T(8,128)S(1)} fusion(f32[256,8192]{0,1:T(8,128)} %bitcast.64, s32[256]{0:T(256)S(1)} %copy-done.5, pred[256]{0:T(512)(128)(4,1)S(1)} %iota_compare_fusion.2), kind=kOutput, calls=%fused_computation.50 | convolution fusion | flops 1610645504 | bytes 10487040 | tf_op jit(solution)/shard_map/dot_general | solution.py:36
  65.2 3.0 %reshape.149 = f32[8192,64]{1,0:T(8,128)} reshape(f32[64,8192]{1,0:T(8,128)S(1)} %fusion.33) | data formatting | bytes 4194304 | tf_op jit(solution)/shard_map/reshape | solution.py:91
  68.2 2.8 %copy.47 = f32[8192,64]{0,1:T(8,128)S(1)} copy(f32[8192,64]{1,0:T(8,128)} %reshape.149) | data formatting | bytes 4194304 | tf_op jit(solution)/shard_map/reshape | solution.py:91
  71.1 1.1 multiply_convert_fusion.1
  72.2 0.2 all-gather.8.cloned.1.call-start
  72.4 0.0 all-gather.4.cloned.1.call-done
  72.5 3.0 %fusion.49 = f32[8192,64]{0,1:T(8,128)S(1)} fusion(bf16[256,64]{0,1:T(8,128)(2,1)S(1)} %copy-done.1, bf16[8192,256]{0,1:T(8,128)(2,1)} %all-gather.4.cloned.1.call-done), kind=kOutput, calls=%fused_computation.85 | convolution fusion | flops 268435456 | bytes 6324224 | tf_op jit(solution)/shard_map/dot_general | solution.py:96
  75.5 30.5 %all-gather.6.cloned.1.call-done = bf16[8192,256]{0,1:T(8,128)(2,1)} async-done(((bf16[8192,64]{0,1:T(8,128)(2,1)}), bf16[8192,256]{0,1:T(8,128)(2,1)}) %all-gather.6.cloned.1.call-update) | async-done | bytes 4194320 | tf_op jit(solution)/shard_map/all_gather | solution.py:94
  106.0 5.8 %fusion.19 = (bf16[8192,64]{0,1:T(8,128)(2,1)}, bf16[8192,64]{0,1:T(8,128)(2,1)}) fusion(bf16[8192,64]{0,1:T(8,128)(2,1)} %param.21, f32[8192,64]{0,1:T(8,128)S(1)} %fusion.49, bf16[256,64]{0,1:T(8,128)(2,1)S(1)} %copy-done.2, bf16[8192,256]{0,1:T(8,128)(2,1)} %all-gather.6.cloned.1.call-done), kind=kOutput, calls=%fused_computation.27 | convolution fusion | flops 280494080 | bytes 9469952 | tf_op jit(solution)/shard_map/dot_general | solution.py:96
  111.8 0.0 all-gather.8.cloned.1.call-update
  111.8 0.0 all-reduce.3.cloned.1.call-start
  111.9 5.4 %all_gather.19 = bf16[256,256]{0,1:T(8,128)(2,1)S(1)} all-gather(bf16[256,64]{0,1:T(8,128)(2,1)S(1)} %copy-done.2), channel_id=1, replica_groups=mesh['nodes'=8,'feat'=4] {'feat'}, dimensions={1}, use_global_device_ids=true | all-gather | bytes 163840 | tf_op jit(solution)/shard_map/all_gather | solution.py:82
  117.3 5.4 %all_gather.18 = bf16[256,256]{0,1:T(8,128)(2,1)S(1)} all-gather(bf16[256,64]{0,1:T(8,128)(2,1)S(1)} %copy-done.1), channel_id=1, replica_groups=mesh['nodes'=8,'feat'=4] {'feat'}, dimensions={1}, use_global_device_ids=true | all-gather | bytes 163840 | tf_op jit(solution)/shard_map/all_gather | solution.py:81
  122.8 4.5 %fusion.48 = f32[256,64]{0,1:T(8,128)} fusion(bf16[8192,256]{0,1:T(8,128)(2,1)} %all-gather.6.cloned.1.call-done, bf16[8192,64]{0,1:T(8,128)(2,1)} %get-tuple-element.13), kind=kOutput, calls=%fused_computation.84 | convolution fusion | flops 268435456 | bytes 5308416 | tf_op jit(solution)/shard_map/dot_general | solution.py:105
  127.3 19.2 %all-gather.8.cloned.1.call-done = bf16[8192,256]{0,1:T(8,128)(2,1)} async-done(((bf16[8192,64]{0,1:T(8,128)(2,1)}), bf16[8192,256]{0,1:T(8,128)(2,1)}) %all-gather.8.cloned.1.call-update) | async-done | bytes 4194320 | tf_op jit(solution)/shard_map/all_gather | solution.py:101
  146.5 3.1 %fusion.23 = bf16[8,64,8,128]{3,2,1,0:T(8,128)(2,1)S(1)} fusion(bf16[8192,256]{0,1:T(8,128)(2,1)} %all-gather.8.cloned.1.call-done, f32[8192]{0:T(1024)S(1)} %convert_divide_fusion, bf16[256,256]{0,1:T(8,128)(2,1)S(1)} %all_gather.19, s32[]{:T(128)S(6)} %select_n.60), kind=kOutput, calls=%fused_computation.35 | convolution fusion | flops 269484032 | bytes 5341188 | tf_op jit(solution)/shard_map/dot_general | solution.py:110
  149.6 0.3 copy.61
  149.9 3.1 %gather_fusion.1 = bf16[256,128,64]{1,2,0:T(8,128)(2,1)} fusion(bf16[64,128,64]{1,2,0:T(8,128)(2,1)S(1)} %bitcast.62, s32[1024]{0:T(1024)S(1)} %pad_clamp_fusion), kind=kCustom, calls=%fused_computation.4 | custom fusion | bytes 8389632 | tf_op jit(solution)/shard_map/jit(_take)/gather | solution.py:40
  153.0 10.3 %fusion.10 = f32[256,128,64]{1,2,0:T(8,128)} fusion(bf16[256,128,128]{2,1,0:T(8,128)(2,1)} %param.14, bf16[256,128,64]{1,2,0:T(8,128)(2,1)} %gather_fusion.1, pred[256]{0:T(512)(128)(4,1)S(1)} %compare_and_fusion.3), kind=kOutput, calls=%fused_computation.18 | convolution fusion | flops 538968064 | bytes 20971776 | tf_op jit(solution)/shard_map/sji,sjf->sif/dot_general | solution.py:41
  163.2 9.3 %copy.49 = f32[256,128,64]{0,2,1:T(8,128)} copy(f32[256,128,64]{1,2,0:T(8,128)} %fusion.10) | data formatting | bytes 16777216 | tf_op jit(solution)/shard_map/sji,sjf->sif/dot_general | solution.py:41
  172.6 9.8 %fusion.47 = (bf16[112,8192]{1,0:T(8,128)(2,1)S(1)}, f32[112,8192]{1,0:T(8,128)}) fusion(f32[256,8192]{0,1:T(8,128)} %bitcast.63, s32[256]{0:T(256)S(1)} %copy-done.6, pred[256]{0:T(512)(128)(4,1)S(1)} %iota_compare_fusion.2), kind=kOutput, calls=%fused_computation.83 | convolution fusion | flops 2819547136 | bytes 13894912 | tf_op jit(solution)/shard_map/dot_general | solution.py:43
  182.4 0.1 fusion.46
  182.4 0.5 convert_element_type.50
  183.0 0.2 copy.50
  183.2 1.6 collective-permute-start.3
  184.8 0.5 convert_element_type.52
  185.3 0.2 copy.52
  185.5 1.5 collective-permute-start.4
  187.1 0.5 convert_element_type.54
  187.6 0.2 copy.53
  187.8 2.5 collective-permute-start.5
  190.3 4.2 %convolution_bitcast_fusion = f32[256,64]{0,1:T(8,128)} fusion(bf16[8192,64]{0,1:T(8,128)(2,1)S(1)} %copy-done, bf16[8192,256]{0,1:T(8,128)(2,1)} %all-gather.4.cloned.1.call-done), kind=kOutput, calls=%fused_computation.36 | convolution fusion | flops 268435456 | bytes 5308416 | tf_op jit(solution)/shard_map/dot_general | solution.py:104
  194.6 1.7 slice.54
  196.3 3.0 %slice.40 = f32[64,128,64]{2,1,0:T(8,128)} reshape(f32[64,8192]{1,0:T(8,128)S(1)} %slice.54) | data formatting | bytes 4194304 | tf_op jit(solution)/shard_map/slice | solution.py:120
  199.3 2.8 %copy.51 = f32[64,128,64]{1,2,0:T(8,128)S(1)} copy(f32[64,128,64]{2,1,0:T(8,128)} %slice.40) | data formatting | bytes 4194304 | tf_op jit(solution)/shard_map/slice | solution.py:120
  202.2 1.0 convert_element_type.51
  203.2 1.3 scatter_fusion
  204.5 1.0 convert_element_type.53
  205.5 1.3 scatter_fusion.1
  206.9 1.3 scatter_fusion.2
  208.2 4.1 %fusion.20 = bf16[8192,64]{0,1:T(8,128)(2,1)} fusion(bf16[8192,256]{0,1:T(8,128)(2,1)} %all-gather.8.cloned.1.call-done, bf16[256,256]{0,1:T(8,128)(2,1)S(1)} %all_gather.18, s32[]{:T(128)S(6)} %select_n.60, f32[64,128,64]{1,2,0:T(8,128)S(1)} %scatter_fusion.2), kind=kOutput, calls=%fused_computation.29 | convolution fusion | flops 269484032 | bytes 7405572 | tf_op jit(solution)/shard_map/dot_general | solution.py:108
  212.4 49.5 %all-reduce.3.cloned.1.call-done = (f32[256,64]{0,1:T(8,128)}, f32[256,64]{0,1:T(8,128)}) async-done(((f32[256,64]{0,1:T(8,128)}, f32[256,64]{0,1:T(8,128)}), (f32[256,64]{0,1:T(8,128)}, f32[256,64]{0,1:T(8,128)})) %all-reduce.3.cloned.1.call-update) | async-done | bytes 131088 | tf_op jit(solution)/shard_map/psum | solution.py:55
  261.9 1.5 copy.68
  263.4 1.5 copy.69
  (33 shorter events, 0.2 us)
Async XLA Ops:
  7.2 65.3 %all-gather.4.cloned.1.call-start = ((), (), s32[]{:S(2)}) async-start(), calls=%async_computation | async-start | bytes 5242880 | tf_op jit(solution)/shard_map/all_gather | solution.py:93
  7.9 98.1 %all-gather.6.cloned.1.call-start = ((), (), s32[]{:S(2)}) async-start(), calls=%async_computation.1 | async-start | bytes 5242880 | tf_op jit(solution)/shard_map/all_gather | solution.py:94
  10.8 9.5 %copy-start.6 = (s32[256]{0:T(256)S(1)}, s32[256]{0:T(256)}, u32[]{:S(2)}) copy-start(s32[256]{0:T(256)} %param.16) | copy-start | bytes 3076
  10.8 9.6 %copy-start.3 = (s32[8192]{0:T(1024)S(1)}, s32[8192]{0:T(1024)}, u32[]{:S(2)}) copy-start(s32[8192]{0:T(1024)} %param.13) | copy-start | bytes 98308
  10.9 9.5 %collective-permute-start = (bf16[16,128,64]{1,2,0:T(8,128)(2,1)S(1)}, bf16[16,128,64]{1,2,0:T(8,128)(2,1)S(1)}, u32[]{:S(2)}, u32[]{:S(2)}) collective-permute-start(bf16[16,128,64]{1,2,0:T(8,128)(2,1)S(1)} %broadcast_select_fusion.2), channel_id=1, source_target_pairs={{0,4},{4,0},{8,12},{12,8},{16,20},{20,16},{24,28},{28,24},{1,5},{5... | collective-permute-start | bytes 786440 | tf_op jit(solution)/shard_map/ppermute | solution.py:11
  14.6 12.6 %collective-permute-start.1 = (bf16[16,128,64]{1,2,0:T(8,128)(2,1)S(1)}, bf16[16,128,64]{1,2,0:T(8,128)(2,1)S(1)}, u32[]{:S(2)}, u32[]{:S(2)}) collective-permute-start(bf16[16,128,64]{1,2,0:T(8,128)(2,1)S(1)} %broadcast_select_fusion.1), channel_id=1, source_target_pairs={{0,8},{4,12},{8,0},{12,4},{16,24},{20,28},{24,16},{28,20},{1,9},{5... | collective-permute-start | bytes 786440 | tf_op jit(solution)/shard_map/ppermute | solution.py:11
  17.0 14.1 %collective-permute-start.2 = (bf16[16,128,64]{1,2,0:T(8,128)(2,1)S(1)}, bf16[16,128,64]{1,2,0:T(8,128)(2,1)S(1)}, u32[]{:S(2)}, u32[]{:S(2)}) collective-permute-start(bf16[16,128,64]{1,2,0:T(8,128)(2,1)S(1)} %broadcast_select_fusion), channel_id=1, source_target_pairs={{0,16},{4,20},{8,24},{12,28},{16,0},{20,4},{24,8},{28,12},{1,17},{... | collective-permute-start | bytes 786440 | tf_op jit(solution)/shard_map/ppermute | solution.py:11
  48.1 9.3 %copy-start.5 = (s32[256]{0:T(256)S(1)}, s32[256]{0:T(256)}, u32[]{:S(2)}) copy-start(s32[256]{0:T(256)} %param.15) | copy-start | bytes 3076
  71.0 1.4 copy-start.1
  72.2 33.8 %copy-start.2 = (bf16[256,64]{0,1:T(8,128)(2,1)S(1)}, bf16[256,64]{0,1:T(8,128)(2,1)}, u32[]{:S(2)}) copy-start(bf16[256,64]{0,1:T(8,128)(2,1)} %param.20) | copy-start | bytes 98308
  72.2 74.3 %all-gather.8.cloned.1.call-start = ((), (), s32[]{:S(2)}) async-start(), calls=%async_computation.2 | async-start | bytes 5242880 | tf_op jit(solution)/shard_map/all_gather | solution.py:101
  75.5 47.2 %copy-start.4 = (s32[1,3,16]{2,0,1:T(1,128)S(1)}, s32[1,3,16]{2,0,1:T(1,128)}, u32[]{:S(2)}) copy-start(s32[1,3,16]{2,0,1:T(1,128)} %param.18) | copy-start | bytes 580
  111.8 150.1 %all-reduce.3.cloned.1.call-start = ((), (), s32[]{:S(2)}) async-start(), calls=%async_computation.3 | async-start | bytes 262144 | tf_op jit(solution)/shard_map/psum | solution.py:55
  183.0 7.3 %copy-start = (bf16[8192,64]{0,1:T(8,128)(2,1)S(1)}, bf16[8192,64]{0,1:T(8,128)(2,1)}, u32[]{:S(2)}) copy-start(bf16[8192,64]{0,1:T(8,128)(2,1)} %get-tuple-element.13) | copy-start | bytes 3145732
  183.2 18.9 %collective-permute-start.3 = (bf16[16,128,64]{1,2,0:T(8,128)(2,1)S(1)}, bf16[16,128,64]{1,2,0:T(8,128)(2,1)}, u32[]{:S(2)}, u32[]{:S(2)}) collective-permute-start(bf16[16,128,64]{1,2,0:T(8,128)(2,1)S(1)} %copy.50), channel_id=1, source_target_pairs={{0,4},{4,0},{8,12},{12,8},{16,20},{20,16},{24,28},{28,24},{1,5},{5... | collective-permute-start | bytes 786440 | tf_op jit(solution)/shard_map/ppermute | solution.py:11
  185.5 19.0 %collective-permute-start.4 = (bf16[16,128,64]{1,2,0:T(8,128)(2,1)S(1)}, bf16[16,128,64]{1,2,0:T(8,128)(2,1)}, u32[]{:S(2)}, u32[]{:S(2)}) collective-permute-start(bf16[16,128,64]{1,2,0:T(8,128)(2,1)S(1)} %copy.52), channel_id=1, source_target_pairs={{0,8},{4,12},{8,0},{12,4},{16,24},{20,28},{24,16},{28,20},{1,9},{5... | collective-permute-start | bytes 786440 | tf_op jit(solution)/shard_map/ppermute | solution.py:11
  187.8 19.0 %collective-permute-start.5 = (bf16[16,128,64]{1,2,0:T(8,128)(2,1)S(1)}, bf16[16,128,64]{1,2,0:T(8,128)(2,1)S(1)}, u32[]{:S(2)}, u32[]{:S(2)}) collective-permute-start(bf16[16,128,64]{1,2,0:T(8,128)(2,1)S(1)} %copy.53), channel_id=1, source_target_pairs={{0,16},{4,20},{8,24},{12,28},{16,0},{20,4},{24,8},{28,12},{1,17},{... | collective-permute-start | bytes 786440 | tf_op jit(solution)/shard_map/ppermute | solution.py:11
Sparse Core Ops, SparseCore 0:
  9.6 37.1 all-gather.3
  72.3 33.6 all-gather.5
  111.9 34.4 all-gather.7
  194.7 67.2 all-reduce.2
where the time goes:
time: 272 us; the launch traced here: 271 us
  waiting for transfers between devices  111 us (41%)
  matrix products  66.4 us (24%)
  local copies, waits for them, and re-layouts  47.1 us (17%)
  between operations  14.8 us (5%)
  starting transfers between devices  13.2 us (5%)
  blocking collectives  10.8 us (4%)
  other arithmetic  8.45 us (3%)
    psum x1, waiting for transfers between devices, gradient_total(): return lax.psum((terms[0], terms[1]), 'nodes')  49.5 us
    all_gather x1, waiting for transfers between devices, local(): lax.all_gather(aggregated, 'feat', axis=1, tiled=True)  30.5 us
    all_gather x1, waiting for transfers between devices, local(): whole_grad = lax.all_gather(pre_grad, 'feat', axis=1, tiled=True)  19.2 us
    dot_general x1, matrix products, gather_sum(): jnp.einsum('sij,sjf->sif', edge_weights, picked, preferred_element_type=j...  13.7 us
    ppermute x6, starting transfers between devices, partner(): lax.ppermute(value, axis, [(i, i ^ 1 << apart) for i in range(lax.axis_si...  12.9 us
    ppermute x6, waiting for transfers between devices, partner(): lax.ppermute(value, axis, [(i, i ^ 1 << apart) for i in range(lax.axis_si...  10.7 us
    dot_general x1, matrix products, spread_back(): jnp.einsum('sji,sjf->sif', edge_weights, picked, preferred_element_type=j...  10.3 us
    dot_general x1, matrix products, spread_back(): jnp.dot(onehot, product.reshape(product.shape[0], -1), precision=lax.Prec...  9.82 us
  transfers between devices with their start and end apart: 10, of which 5 were waited for; matrix products, arithmetic and copies ran while one was open for 28% of the time, Pallas kernels for 0%

commit v1 on v0

v1 whole, which is shorter than its diff:
```python
import functools

import jax
import jax.numpy as jnp
from jax import lax
from jax.experimental import pallas as pl
from jax.experimental.pallas import tpu as pltpu
from jax.sharding import PartitionSpec as P

gelu_scale = 0.7978845608028654
gelu_cubic = 0.044715
GROUP = 4
SMEM = pl.BlockSpec(memory_space=pltpu.SMEM)
VMEM = pl.BlockSpec(memory_space=pltpu.VMEM)
PARAMS = pltpu.CompilerParams(vmem_limit_bytes=56 * 1024 * 1024)
NT = (((1,), (1,)), ((), ()))


def partner(value, axis, apart):
    return lax.ppermute(value, axis, [(i, i ^ 1 << apart) for i in range(lax.axis_size(axis))])


def lanes(index, size):
    return pl.ds(pl.multiple_of(index * size, size), size)


def for_slots(first, last, order_ref, product, store):
    groups = (last - first) // GROUP

    def several(step, carry):
        slots = [order_ref[first + step * GROUP + k] for k in range(GROUP)]
        values = [product(slot) for slot in slots]
        for slot, value in zip(slots, values):
            store(slot, value)
        return carry

    def single(step, carry):
        slot = order_ref[step]
        store(slot, product(slot))
        return carry

    lax.fori_loop(0, groups, several, 0)
    lax.fori_loop(first + groups * GROUP, last, single, 0)


def pack_kernel(own_blocks, cols_ref, count_ref, sends_ref, table_ref, order_ref, split_ref, *piece_refs):
    size = piece_refs[0].shape[2]
    for level, piece_ref in enumerate(piece_refs):
        for j in range(piece_ref.shape[0]):
            piece_ref[j] = table_ref[:, lanes(sends_ref[level, j], size)]
    count = count_ref[0]

    def place(slot, state):
        low, high = state
        own = cols_ref[slot] < own_blocks
        order_ref[jnp.where(own, low, high)] = slot
        return jnp.where(own, low + 1, low), jnp.where(own, high, high - 1)

    low, _ = lax.fori_loop(0, count, place, (jnp.int32(0), count - 1))
    split_ref[0] = low
    split_ref[1] = count


def gather_own_kernel(rows_ref, cols_ref, order_ref, split_ref, weight_ref, table_ref, total_ref):
    size = weight_ref.shape[1]
    total_ref[...] = jnp.zeros_like(total_ref)

    def product(slot):
        block = table_ref[:, lanes(cols_ref[slot], size)]
        return lax.dot_general(block, weight_ref[slot], NT, preferred_element_type=jnp.float32)

    def store(slot, value):
        total_ref[:, lanes(rows_ref[slot], size)] += value

    for_slots(0, split_ref[0], order_ref, product, store)


def gather_border_kernel(
    own_blocks, rows_ref, cols_ref, order_ref, split_ref, weight_ref, total_ref, inverse_ref, *rest
):
    piece_refs, out_ref, border_ref, sum_ref = rest[:-3], rest[-3], rest[-2], rest[-1]
    size = weight_ref.shape[1]
    border_size = piece_refs[0].shape[0]
    for level, piece_ref in enumerate(piece_refs):
        border_ref[level * border_size : (level + 1) * border_size] = piece_ref[...]
    sum_ref[...] = total_ref[...]

    def product(slot):
        block = border_ref[cols_ref[slot] - own_blocks]
        return lax.dot_general(block, weight_ref[slot], NT, preferred_element_type=jnp.float32)

    def store(slot, value):
        sum_ref[:, lanes(rows_ref[slot], size)] += value

    for_slots(split_ref[0], split_ref[1], order_ref, product, store)
    out_ref[...] = (sum_ref[...] * inverse_ref[...]).astype(jnp.bfloat16)


def dense_kernel(
    own_ref, agg_ref, self_ref, neigh_ref, cot_ref, mixed_ref, grad_ref, grad_self_ref, grad_neigh_ref
):
    @pl.when(pl.program_id(0) == 0)
    def _():
        grad_self_ref[...] = jnp.zeros_like(grad_self_ref)
        grad_neigh_ref[...] = jnp.zeros_like(grad_neigh_ref)

    rows, agg = own_ref[...], agg_ref[...]
    values = jnp.dot(self_ref[...], rows, preferred_element_type=jnp.float32) + jnp.dot(
        neigh_ref[...], agg, preferred_element_type=jnp.float32
    )
    square = values * values
    tanh_inner = jnp.tanh(gelu_scale * (values + gelu_cubic * square * values))
    half = 0.5 * (1.0 + tanh_inner)
    mixed_ref[...] = (values * half).astype(jnp.bfloat16)
    slope = half + 0.5 * values * (1.0 - tanh_inner * tanh_inner) * gelu_scale * (
        1.0 + 3.0 * gelu_cubic * square
    )
    grad = (cot_ref[...].astype(jnp.float32) * slope).astype(jnp.bfloat16)
    grad_ref[...] = grad
    grad_self_ref[...] += lax.dot_general(grad, rows, NT, preferred_element_type=jnp.float32)
    grad_neigh_ref[...] += lax.dot_general(grad, agg, NT, preferred_element_type=jnp.float32)


def spread_border_kernel(
    own_blocks, rows_ref, cols_ref, order_ref, split_ref, weight_ref, whole_ref, self_ref, neigh_ref,
    inverse_ref, direct_ref, scaled_ref, *rest
):
    piece_refs, border_ref = rest[:-1], rest[-1]
    size = weight_ref.shape[1]
    chunk = 8 * size

    def dense(step, carry):
        part = lanes(step, chunk)
        grad = whole_ref[:, part]
        direct_ref[:, part] = jnp.dot(self_ref[...], grad, preferred_element_type=jnp.float32)
        scaled = jnp.dot(neigh_ref[...], grad, preferred_element_type=jnp.float32)
        scaled_ref[:, part] = (scaled * inverse_ref[:, part]).astype(jnp.bfloat16)
        return carry

    lax.fori_loop(0, whole_ref.shape[1] // chunk, dense, 0)
    border_ref[...] = jnp.zeros_like(border_ref)

    def product(slot):
        block = scaled_ref[:, lanes(rows_ref[slot], size)]
        return jnp.dot(block, weight_ref[slot], preferred_element_type=jnp.float32)

    def store(slot, value):
        border_ref[cols_ref[slot] - own_blocks] += value

    for_slots(split_ref[0], split_ref[1], order_ref, product, store)
    border_size = piece_refs[0].shape[0]
    for level, piece_ref in enumerate(piece_refs):
        piece_ref[...] = border_ref[level * border_size : (level + 1) * border_size].astype(jnp.bfloat16)


def spread_own_kernel(
    rows_ref, cols_ref, order_ref, split_ref, weight_ref, scaled_ref, direct_ref, total_ref
):
    size = weight_ref.shape[1]
    total_ref[...] = direct_ref[...]

    def product(slot):
        block = scaled_ref[:, lanes(rows_ref[slot], size)]
        return jnp.dot(block, weight_ref[slot], preferred_element_type=jnp.float32)

    def store(slot, value):
        total_ref[:, lanes(cols_ref[slot], size)] += value

    for_slots(0, split_ref[0], order_ref, product, store)


def collect_kernel(sends_ref, total_ref, *rest):
    piece_refs, out_ref, sum_ref = rest[:-2], rest[-2], rest[-1]
    size = piece_refs[0].shape[2]
    sum_ref[...] = total_ref[...]
    for level, piece_ref in enumerate(piece_refs):
        for j in range(piece_ref.shape[0]):
            sum_ref[:, lanes(sends_ref[level, j], size)] += piece_ref[j].astype(jnp.float32)
    out_ref[...] = sum_ref[...].astype(jnp.bfloat16)


def local(
    features,
    degrees,
    edge_weights,
    block_rows,
    block_cols,
    block_counts,
    send_lists,
    w_self,
    w_neigh,
    cotangent,
):
    row_count, width = features.shape
    slot_count, size, _ = edge_weights.shape
    own_blocks = row_count // size
    border_size = send_lists.shape[2]
    levels = send_lists.shape[1]
    hidden = w_self.shape[0]
    shape = jax.ShapeDtypeStruct
    bf16, f32, i32 = jnp.bfloat16, jnp.float32, jnp.int32
    piece = shape((border_size, width, size), bf16)
    inverse = (1.0 / degrees.astype(f32))[None, :]
    own = features.T
    whole_rows = lax.all_gather(own, "feat", axis=0, tiled=True)
    both = jnp.concatenate([w_self.T, w_neigh.T], axis=1)
    whole_both = lax.all_gather(both, "feat", axis=0, tiled=True)
    start_row = lax.axis_index("feat") * width
    rows_self = lax.dynamic_slice_in_dim(whole_both, start_row, width, 1).T
    rows_neigh = lax.dynamic_slice_in_dim(whole_both, hidden + start_row, width, 1).T
    sends = send_lists[0]

    order, split, *pieces = pl.pallas_call(
        functools.partial(pack_kernel, own_blocks),
        out_shape=[shape((slot_count,), i32), shape((2,), i32)] + [piece] * levels,
        in_specs=[SMEM, SMEM, SMEM, VMEM],
        out_specs=[SMEM, SMEM] + [VMEM] * levels,
        compiler_params=PARAMS,
        name="pack",
    )(block_cols, block_counts, sends, own)
    tables = (block_rows, block_cols, order, split)
    arrived = [partner(value, "nodes", level) for level, value in enumerate(pieces)]
    total = pl.pallas_call(
        gather_own_kernel,
        out_shape=shape((width, row_count), f32),
        in_specs=[SMEM] * 4 + [VMEM] * 2,
        out_specs=VMEM,
        compiler_params=PARAMS,
        cost_estimate=pl.CostEstimate(flops=4 * 10**9, bytes_accessed=12 * 10**6, transcendentals=0),
        name="gather_own",
    )(*tables, edge_weights, own)
    aggregated = pl.pallas_call(
        functools.partial(gather_border_kernel, own_blocks),
        out_shape=shape((width, row_count), bf16),
        in_specs=[SMEM] * 4 + [VMEM] * (3 + levels),
        out_specs=VMEM,
        scratch_shapes=[
            pltpu.VMEM((levels * border_size, width, size), bf16),
            pltpu.VMEM((width, row_count), f32),
        ],
        compiler_params=PARAMS,
        name="gather_border",
    )(*tables, edge_weights, total, inverse, *arrived)
    whole_agg = lax.all_gather(aggregated, "feat", axis=0, tiled=True)

    chunk = 8 * size
    steps = row_count // chunk
    column = pl.BlockSpec((width, chunk), lambda i: (0, i))
    tall = pl.BlockSpec((hidden, chunk), lambda i: (0, i))
    fixed = pl.BlockSpec((width, hidden), lambda i: (0, 0))
    mixed, pre_grad, grad_self, grad_neigh = pl.pallas_call(
        dense_kernel,
        grid=(steps,),
        out_shape=[shape((width, row_count), bf16)] * 2 + [shape((width, hidden), f32)] * 2,
        in_specs=[tall, tall, fixed, fixed, column],
        out_specs=[column, column, fixed, fixed],
        compiler_params=PARAMS,
        name="dense",
    )(whole_rows, whole_agg, w_self.T, w_neigh.T, cotangent.T)
    whole_grad = lax.all_gather(pre_grad, "feat", axis=0, tiled=True)
    grad_self, grad_neigh = lax.psum((grad_self, grad_neigh), "nodes")

    direct, scaled, *pieces = pl.pallas_call(
        functools.partial(spread_border_kernel, own_blocks),
        out_shape=[shape((width, row_count), f32), shape((width, row_count), bf16)] + [piece] * levels,
        in_specs=[SMEM] * 4 + [VMEM] * 5,
        out_specs=[VMEM] * (2 + levels),
        scratch_shapes=[pltpu.VMEM((levels * border_size, width, size), f32)],
        compiler_params=PARAMS,
        name="spread_border",
    )(*tables, edge_weights, whole_grad, rows_self, rows_neigh, inverse)
    returned = [partner(value, "nodes", level) for level, value in enumerate(pieces)]
    total = pl.pallas_call(
        spread_own_kernel,
        out_shape=shape((width, row_count), f32),
        in_specs=[SMEM] * 4 + [VMEM] * 3,
        out_specs=VMEM,
        compiler_params=PARAMS,
        cost_estimate=pl.CostEstimate(flops=4 * 10**9, bytes_accessed=12 * 10**6, transcendentals=0),
        name="spread_own",
    )(*tables, edge_weights, scaled, direct)
    grad_features = pl.pallas_call(
        collect_kernel,
        out_shape=shape((width, row_count), bf16),
        in_specs=[SMEM] + [VMEM] * (1 + levels),
        out_specs=VMEM,
        scratch_shapes=[pltpu.VMEM((width, row_count), f32)],
        compiler_params=PARAMS,
        name="collect",
    )(sends, total, *returned)
    return (mixed.T, grad_features.T, grad_self.T, grad_neigh.T)


def solution(mesh):
    in_specs = (
        P("nodes", "feat"),
        P("nodes"),
        P("nodes", None, None),
        P("nodes"),
        P("nodes"),
        P("nodes"),
        P("nodes", None, None),
        P(None, "feat"),
        P(None, "feat"),
        P("nodes", "feat"),
    )
    out_specs = (P("nodes", "feat"), P("nodes", "feat"), P(None, "feat"), P(None, "feat"))
    return jax.shard_map(local, mesh=mesh, in_specs=in_specs, out_specs=out_specs, check_vma=False)
```

time: 272 us -> 216 us (0.79)
  Pallas kernels: 0 us -> 68.2 us
  matrix products: 66.4 us -> 0 us
  local copies, waits for them, and re-layouts: 47.1 us -> 8.06 us
  other arithmetic: 8.45 us -> 0.63 us
  blocking collectives: 10.8 us -> 5.79 us
  starting transfers between devices: 13.2 us -> 10.1 us
  waiting for transfers between devices: 111 us -> 108 us
    pallas_call x0 -> x7, Pallas kernels: none -> 68.2 us  [the longest x1 13.7 us: local(): pl.pallas_call(functools.partial(spread_border_kernel, own_blocks), out_s...]
    dot_general x10 -> x0, matrix products: 66.4 us -> none  [the longest x1 13.7 us: gather_sum(): jnp.einsum('sij,sjf->sif', edge_weights, picked, preferred_element_type=j...]
    dot_general x2 -> x0, local copies, waits for them, and re-layouts: 18.6 us -> none  [the longest x1 9.32 us: gather_sum(): jnp.einsum('sij,sjf->sif', edge_weights, picked, preferred_element_type=j...]
    all_gather x3, waiting for transfers between devices: 49.7 us -> 63.9 us  [the longest x1 36.7 us: local(): whole_agg = lax.all_gather(aggregated, 'feat', axis=0, tiled=True)]
    ppermute x6, waiting for transfers between devices: 10.7 us -> 0.02 us  [partner(): lax.ppermute(value, axis, [(i, i ^ 1 << apart) for i in range(lax.axis_si...]
    gather x5 -> x0, local copies, waits for them, and re-layouts: 7.92 us -> none  [the longest x1 3.07 us: spread_back(): picked = jnp.take(table, block_rows, axis=0)]
    reshape x4 -> x0, local copies, waits for them, and re-layouts: 7.63 us -> none  [the longest x2 5.83 us: local(): summed.reshape(row_count, local_width) * inverse]
    slice x4 -> x0, local copies, waits for them, and re-layouts: 7.63 us -> none  [the longest x3 7.58 us: local(): total = spread[:own_blocks]]
  transfers between devices with their start and end apart: 10 -> 10, of which waited for: 5 -> 3; matrix products, arithmetic and copies ran while one was open for 28% -> 2% of each run, Pallas kernels for 0% -> 27%
where the time goes in v1:
time: 216 us; the launch traced here: 215 us
  waiting for transfers between devices  108 us (50%)
  Pallas kernels  68.2 us (32%)
  between operations  14.5 us (7%)
  starting transfers between devices  10.1 us (5%)
  local copies, waits for them, and re-layouts  8.06 us (4%)
  blocking collectives  5.79 us (3%)
    psum x1, waiting for transfers between devices, local(): grad_self, grad_neigh = lax.psum((grad_self, grad_neigh), 'nodes')  43.3 us
    all_gather x1, waiting for transfers between devices, local(): whole_agg = lax.all_gather(aggregated, 'feat', axis=0, tiled=True)  36.7 us
    all_gather x1, waiting for transfers between devices, local(): whole_grad = lax.all_gather(pre_grad, 'feat', axis=0, tiled=True)  27.2 us
    pallas_call x1, Pallas kernels, local(): pl.pallas_call(functools.partial(spread_border_kernel, own_blocks), out_s...  13.7 us
    pallas_call x1, Pallas kernels, local(): pl.pallas_call(gather_own_kernel, out_shape=shape((width, row_count), f32...  12.9 us
    pallas_call x1, Pallas kernels, local(): pl.pallas_call(spread_own_kernel, out_shape=shape((width, row_count), f32...  12.3 us
    pallas_call x1, Pallas kernels, local(): pl.pallas_call(functools.partial(gather_border_kernel, own_blocks), out_s...  11 us
    ppermute x6, starting transfers between devices, partner(): lax.ppermute(value, axis, [(i, i ^ 1 << apart) for i in range(lax.axis_si...  9.91 us
  transfers between devices with their start and end apart: 10, of which 3 were waited for; matrix products, arithmetic and copies ran while one was open for 2% of the time, Pallas kernels for 27%

profile of v1, /device:TPU:0, one launch (start us, length us, event | category | flops | bytes accessed | tf_op | source)
XLA Modules:
  0.0 215.3 jit_solution(4824989523391652432)
XLA Ops:
  7.2 0.0 all-gather.4.cloned.1.call-start
  7.2 0.7 all-gather.4.cloned.1.call-update
  7.9 0.0 all-gather.6.cloned.1.call-start
  7.9 1.2 copy.24
  9.8 5.3 %pack.1 = (s32[256]{0:T(256)}, s32[2]{0:T(128)}, bf16[16,64,128]{2,1,0:T(8,128)(2,1)}, bf16[16,64,128]{2,1,0:T(8,128)(2,1)}, bf16[16,64,128]{2,1,0:T(8,128)(2,1)}) custom-call(s32[256]{0:T(256)} %cols_ref.9, s32[1]{0:T(128)S(6)} %copy.27.count_ref, s32[3,16]{1,0:T(4,128)} %bitcast.29, bf16[64,8192]{1,0:T(8,128)(2,1)} %bitcast.15), custom_call_target="tpu_custom_call" | custom-call | tf_op jit(solution)/shard_map/pack/pallas_call | solution.py:213
  15.1 2.9 %collective-permute-start = (bf16[16,64,128]{2,1,0:T(8,128)(2,1)}, bf16[16,64,128]{2,1,0:T(8,128)(2,1)S(1)}, u32[]{:S(2)}, u32[]{:S(2)}) collective-permute-start(bf16[16,64,128]{2,1,0:T(8,128)(2,1)} %get-tuple-element.20), channel_id=1, source_target_pairs={{0,4},{4,0},{8,12},{12,8},{16,20},{20,16},{24,28},{28,24},{1,5},{5... | collective-permute-start | bytes 786440 | tf_op jit(solution)/shard_map/ppermute | solution.py:20
  18.0 1.2 collective-permute-start.1
  19.3 2.0 collective-permute-start.2
  21.3 0.0 copy-start.8
  21.3 12.9 %gather_own.1.total_ref = f32[64,8192]{1,0:T(8,128)} custom-call(s32[256]{0:T(256)} %rows_ref.7, s32[256]{0:T(256)} %cols_ref.9, s32[256]{0:T(256)} %get-tuple-element.18.order_ref, s32[2]{0:T(128)} %get-tuple-element.19.split_ref, bf16[256,128,128]{2,1,0:T(8,128)(2,1)} %weight_ref.7, bf16[64,8192]{1,0:T(8,128)(2,1)} %bitcast.16), custom_call_target="tpu_custom_call" | custom-call | flops 4000000000 | bytes 12000000 | tf_op jit(solution)/shard_map/gather_own/pallas_call | solution.py:223
  34.1 0.0 copy-done.8
  34.1 0.6 convert_divide_fusion
  34.7 0.0 collective-permute-done.rest_0_
  34.7 0.0 copy-start.2
  34.7 0.0 collective-permute-done.1.rest_1_
  34.7 0.0 copy-start.4
  34.8 0.0 collective-permute-done.2.rest_2_
  34.8 0.0 copy-start.5
  34.8 0.7 copy-done.2
  35.5 0.1 copy-done.4
  35.5 0.1 copy-done.5
  35.6 11.0 %gather_border.1 = bf16[64,8192]{1,0:T(8,128)(2,1)} custom-call(s32[256]{0:T(256)} %rows_ref.7, s32[256]{0:T(256)} %cols_ref.9, s32[256]{0:T(256)} %get-tuple-element.18.order_ref, s32[2]{0:T(128)} %get-tuple-element.19.split_ref, bf16[256,128,128]{2,1,0:T(8,128)(2,1)} %weight_ref.7, f32[64,8192]{1,0:T(8,128)} %gather_own.1.total_ref, f32[1,8192]{1,0:T(1,128)} %bitcast.19, ...), custom_call_target="tpu_custom_call" | custom-call | tf_op jit(solution)/shard_map/gather_border/pallas_call | solution.py:232
  46.7 0.0 all-gather.6.cloned.1.call-update
  46.7 0.0 all-gather.8.cloned.1.call-start
  46.7 0.0 all-gather.4.cloned.1.call-done.own_ref
  46.8 36.7 %all-gather.6.cloned.1.call-done.agg_ref = bf16[256,8192]{1,0:T(8,128)(2,1)} async-done(((bf16[64,8192]{1,0:T(8,128)(2,1)}), bf16[256,8192]{1,0:T(8,128)(2,1)}) %all-gather.6.cloned.1.call-update) | async-done | bytes 4194320 | tf_op jit(solution)/shard_map/all_gather | solution.py:244
  83.4 0.0 copy-start.6
  83.4 0.0 copy-start.7
  83.4 9.7 %dense.1 = (bf16[64,8192]{1,0:T(8,128)(2,1)}, bf16[64,8192]{1,0:T(8,128)(2,1)}, f32[64,256]{1,0:T(8,128)}, f32[64,256]{1,0:T(8,128)}) custom-call(bf16[256,8192]{1,0:T(8,128)(2,1)} %all-gather.4.cloned.1.call-done.own_ref, bf16[256,8192]{1,0:T(8,128)(2,1)} %all-gather.6.cloned.1.call-done.agg_ref, bf16[64,256]{1,0:T(8,128)(2,1)} %bitcast.23, ...), custom_call_target="tpu_custom_call" | custom-call | tf_op jit(solution)/shard_map/dense/pallas_call | solution.py:251
  93.2 0.0 all-gather.8.cloned.1.call-update
  93.2 0.0 all-reduce.3.cloned.1.call-start
  93.2 0.0 copy-done.6
  93.3 0.0 copy-done.7
  93.3 5.8 %all_gather.15 = bf16[256,512]{1,0:T(8,128)(2,1)S(1)} all-gather(bf16[64,512]{1,0:T(8,128)(2,1)S(1)} %pad_maximum_fusion), channel_id=1, replica_groups=mesh['nodes'=8,'feat'=4] {'feat'}, dimensions={0}, use_global_device_ids=true | all-gather | bytes 327680 | tf_op jit(solution)/shard_map/all_gather | solution.py:207
  99.1 0.1 constant_dynamic-slice_fusion
  99.2 0.7 copy.21
  99.9 0.7 copy.22
  100.6 0.0 all-reduce.3.cloned.1.call-update
  100.6 27.2 %all-gather.8.cloned.1.call-done.whole_ref = bf16[256,8192]{1,0:T(8,128)(2,1)} async-done(((bf16[64,8192]{1,0:T(8,128)(2,1)}), bf16[256,8192]{1,0:T(8,128)(2,1)}) %all-gather.8.cloned.1.call-update) | async-done | bytes 4194320 | tf_op jit(solution)/shard_map/all_gather | solution.py:260
  127.8 13.7 %spread_border.1 = (f32[64,8192]{1,0:T(8,128)}, bf16[64,8192]{1,0:T(8,128)(2,1)}, bf16[16,64,128]{2,1,0:T(8,128)(2,1)}, bf16[16,64,128]{2,1,0:T(8,128)(2,1)}, bf16[16,64,128]{2,1,0:T(8,128)(2,1)}) custom-call(s32[256]{0:T(256)} %rows_ref.7, s32[256]{0:T(256)} %cols_ref.9, s32[256]{0:T(256)} %get-tuple-element.18.order_ref, s32[2]{0:T(128)} %get-tuple-element.19.split_ref, ...), custom_call_target="tpu_custom_call" | custom-call | tf_op jit(solution)/shard_map/spread_border/pallas_call | solution.py:263
  141.6 1.6 collective-permute-start.3
  143.1 0.4 collective-permute-start.4
  143.5 1.9 collective-permute-start.5
  145.4 12.3 %spread_own.1.total_ref = f32[64,8192]{1,0:T(8,128)} custom-call(s32[256]{0:T(256)} %rows_ref.7, s32[256]{0:T(256)} %cols_ref.9, s32[256]{0:T(256)} %get-tuple-element.18.order_ref, s32[2]{0:T(128)} %get-tuple-element.19.split_ref, bf16[256,128,128]{2,1,0:T(8,128)(2,1)} %weight_ref.7, bf16[64,8192]{1,0:T(8,128)(2,1)} %get-tuple-element.25.scaled_ref, ...), custom_call_target="tpu_custom_call" | custom-call | flops 4000000000 | bytes 12000000 | tf_op jit(solution)/shard_map/spread_own/pallas_call | solution.py:273
  157.6 0.0 collective-permute-done.3.rest_0_
  157.6 0.0 copy-start
  157.6 0.0 collective-permute-done.4.rest_1_
  157.6 0.0 copy-start.1
  157.7 0.0 collective-permute-done.5.rest_2_
  157.7 0.7 copy-done
  158.3 0.1 copy-done.1
  158.4 0.0 copy-start.3
  158.5 0.7 copy-done.3
  159.2 3.3 %collect.1 = bf16[64,8192]{1,0:T(8,128)(2,1)} custom-call(s32[3,16]{1,0:T(4,128)} %bitcast.30, f32[64,8192]{1,0:T(8,128)} %spread_own.1.total_ref, bf16[16,64,128]{2,1,0:T(8,128)(2,1)} %copy-done, bf16[16,64,128]{2,1,0:T(8,128)(2,1)} %copy-done.1, bf16[16,64,128]{2,1,0:T(8,128)(2,1)} %copy-done.3), custom_call_target="tpu_custom_call" | custom-call | tf_op jit(solution)/shard_map/collect/pallas_call | solution.py:282
  162.4 43.3 %all-reduce.3.cloned.1.call-done = (f32[256,64]{0,1:T(8,128)}, f32[256,64]{0,1:T(8,128)}) async-done(((f32[256,64]{0,1:T(8,128)}, f32[256,64]{0,1:T(8,128)}), (f32[256,64]{0,1:T(8,128)}, f32[256,64]{0,1:T(8,128)})) %all-reduce.3.cloned.1.call-update) | async-done | bytes 131088 | tf_op jit(solution)/shard_map/psum | solution.py:261
  205.8 1.5 copy.28
  207.2 1.5 copy.29
  (1 shorter events, 0.0 us)
Async XLA Ops:
  7.2 39.6 %all-gather.4.cloned.1.call-start = ((), (), s32[]{:S(2)}) async-start(), calls=%async_computation | async-start | bytes 5242880 | tf_op jit(solution)/shard_map/all_gather | solution.py:205
  7.9 75.5 %all-gather.6.cloned.1.call-start = ((), (), s32[]{:S(2)}) async-start(), calls=%async_computation.1 | async-start | bytes 5242880 | tf_op jit(solution)/shard_map/all_gather | solution.py:244
  15.1 19.6 %collective-permute-start = (bf16[16,64,128]{2,1,0:T(8,128)(2,1)}, bf16[16,64,128]{2,1,0:T(8,128)(2,1)S(1)}, u32[]{:S(2)}, u32[]{:S(2)}) collective-permute-start(bf16[16,64,128]{2,1,0:T(8,128)(2,1)} %get-tuple-element.20), channel_id=1, source_target_pairs={{0,4},{4,0},{8,12},{12,8},{16,20},{20,16},{24,28},{28,24},{1,5},{5... | collective-permute-start | bytes 786440 | tf_op jit(solution)/shard_map/ppermute | solution.py:20
  18.0 16.7 %collective-permute-start.1 = (bf16[16,64,128]{2,1,0:T(8,128)(2,1)}, bf16[16,64,128]{2,1,0:T(8,128)(2,1)S(1)}, u32[]{:S(2)}, u32[]{:S(2)}) collective-permute-start(bf16[16,64,128]{2,1,0:T(8,128)(2,1)} %get-tuple-element.21), channel_id=1, source_target_pairs={{0,8},{4,12},{8,0},{12,4},{16,24},{20,28},{24,16},{28,20},{1,9},{5... | collective-permute-start | bytes 786440 | tf_op jit(solution)/shard_map/ppermute | solution.py:20
  19.3 15.5 %collective-permute-start.2 = (bf16[16,64,128]{2,1,0:T(8,128)(2,1)}, bf16[16,64,128]{2,1,0:T(8,128)(2,1)S(1)}, u32[]{:S(2)}, u32[]{:S(2)}) collective-permute-start(bf16[16,64,128]{2,1,0:T(8,128)(2,1)} %get-tuple-element.22), channel_id=1, source_target_pairs={{0,16},{4,20},{8,24},{12,28},{16,0},{20,4},{24,8},{28,12},{1,17},{... | collective-permute-start | bytes 786440 | tf_op jit(solution)/shard_map/ppermute | solution.py:20
  21.3 12.9 %copy-start.8 = (s32[8192]{0:T(1024)S(1)}, s32[8192]{0:T(1024)}, u32[]{:S(2)}) copy-start(s32[8192]{0:T(1024)} %param.11) | copy-start | bytes 98308
  34.7 0.7 copy-start.2
  34.7 0.8 copy-start.4
  34.8 0.8 copy-start.5
  46.7 81.1 %all-gather.8.cloned.1.call-start = ((), (), s32[]{:S(2)}) async-start(), calls=%async_computation.2 | async-start | bytes 5242880 | tf_op jit(solution)/shard_map/all_gather | solution.py:260
  83.4 9.8 %copy-start.6 = (bf16[256,64]{0,1:T(8,128)(2,1)S(1)}, bf16[256,64]{0,1:T(8,128)(2,1)}, u32[]{:S(2)}) copy-start(bf16[256,64]{0,1:T(8,128)(2,1)} %param.17) | copy-start | bytes 98308
  83.4 9.8 %copy-start.7 = (bf16[256,64]{0,1:T(8,128)(2,1)S(1)}, bf16[256,64]{0,1:T(8,128)(2,1)}, u32[]{:S(2)}) copy-start(bf16[256,64]{0,1:T(8,128)(2,1)} %param.18) | copy-start | bytes 98308
  93.2 112.6 %all-reduce.3.cloned.1.call-start = ((), (), s32[]{:S(2)}) async-start(), calls=%async_computation.3 | async-start | bytes 262144 | tf_op jit(solution)/shard_map/psum | solution.py:261
  141.6 16.1 %collective-permute-start.3 = (bf16[16,64,128]{2,1,0:T(8,128)(2,1)}, bf16[16,64,128]{2,1,0:T(8,128)(2,1)S(1)}, u32[]{:S(2)}, u32[]{:S(2)}) collective-permute-start(bf16[16,64,128]{2,1,0:T(8,128)(2,1)} %get-tuple-element.27), channel_id=1, source_target_pairs={{0,4},{4,0},{8,12},{12,8},{16,20},{20,16},{24,28},{28,24},{1,5},{5... | collective-permute-start | bytes 786440 | tf_op jit(solution)/shard_map/ppermute | solution.py:20
  143.1 14.5 %collective-permute-start.4 = (bf16[16,64,128]{2,1,0:T(8,128)(2,1)}, bf16[16,64,128]{2,1,0:T(8,128)(2,1)S(1)}, u32[]{:S(2)}, u32[]{:S(2)}) collective-permute-start(bf16[16,64,128]{2,1,0:T(8,128)(2,1)} %get-tuple-element.28), channel_id=1, source_target_pairs={{0,8},{4,12},{8,0},{12,4},{16,24},{20,28},{24,16},{28,20},{1,9},{5... | collective-permute-start | bytes 786440 | tf_op jit(solution)/shard_map/ppermute | solution.py:20
  143.5 14.2 %collective-permute-start.5 = (bf16[16,64,128]{2,1,0:T(8,128)(2,1)}, bf16[16,64,128]{2,1,0:T(8,128)(2,1)S(1)}, u32[]{:S(2)}, u32[]{:S(2)}) collective-permute-start(bf16[16,64,128]{2,1,0:T(8,128)(2,1)} %get-tuple-element.29), channel_id=1, source_target_pairs={{0,16},{4,20},{8,24},{12,28},{16,0},{20,4},{24,8},{28,12},{1,17},{... | collective-permute-start | bytes 786440 | tf_op jit(solution)/shard_map/ppermute | solution.py:20
  157.6 0.7 copy-start
  157.6 0.8 copy-start.1
  158.4 0.7 copy-start.3
Sparse Core Ops, SparseCore 0:
  9.6 37.1 all-gather.3
  48.9 34.4 all-gather.5
  93.3 34.4 all-gather.7
  131.7 74.0 all-reduce.2

commit v2 on v1

--- a/solution.py
+++ b/solution.py
@@ -9,7 +9,7 @@
 
 gelu_scale = 0.7978845608028654
 gelu_cubic = 0.044715
-GROUP = 4
+GROUP = 8
 SMEM = pl.BlockSpec(memory_space=pltpu.SMEM)
 VMEM = pl.BlockSpec(memory_space=pltpu.VMEM)
 PARAMS = pltpu.CompilerParams(vmem_limit_bytes=56 * 1024 * 1024)
@@ -96,48 +96,163 @@
     out_ref[...] = (sum_ref[...] * inverse_ref[...]).astype(jnp.bfloat16)
 
 
-def dense_kernel(
-    own_ref, agg_ref, self_ref, neigh_ref, cot_ref, mixed_ref, grad_ref, grad_self_ref, grad_neigh_ref
+def middle_kernel(
+    levels, chunk, whole_ref, agg_ref, self_ref, neigh_ref, slab_ref, cot_ref, inverse_ref,
+    mixed_ref, direct_ref, scaled_ref, sums_ref,
+    all_agg, all_grad, slabs, back_ref, partial_ref, arrived_ref,
+    gather_send, gather_recv, slab_send, slab_recv, sum_send, sum_recv,
 ):
-    @pl.when(pl.program_id(0) == 0)
-    def _():
-        grad_self_ref[...] = jnp.zeros_like(grad_self_ref)
-        grad_neigh_ref[...] = jnp.zeros_like(grad_neigh_ref)
-
-    rows, agg = own_ref[...], agg_ref[...]
-    values = jnp.dot(self_ref[...], rows, preferred_element_type=jnp.float32) + jnp.dot(
-        neigh_ref[...], agg, preferred_element_type=jnp.float32
-    )
-    square = values * values
-    tanh_inner = jnp.tanh(gelu_scale * (values + gelu_cubic * square * values))
-    half = 0.5 * (1.0 + tanh_inner)
-    mixed_ref[...] = (values * half).astype(jnp.bfloat16)
-    slope = half + 0.5 * values * (1.0 - tanh_inner * tanh_inner) * gelu_scale * (
-        1.0 + 3.0 * gelu_cubic * square
-    )
-    grad = (cot_ref[...].astype(jnp.float32) * slope).astype(jnp.bfloat16)
-    grad_ref[...] = grad
-    grad_self_ref[...] += lax.dot_general(grad, rows, NT, preferred_element_type=jnp.float32)
-    grad_neigh_ref[...] += lax.dot_general(grad, agg, NT, preferred_element_type=jnp.float32)
+    width, nodes = agg_ref.shape
+    steps = nodes // chunk
+    me, node = lax.axis_index("feat"), lax.axis_index("nodes")
+    near = me + 1 - 2 * (me % 2)
+    cross = (me + 2) % 4
+    far = 3 - me
+    mates = [node + (1 << level) * (1 - 2 * ((node // (1 << level)) % 2)) for level in range(levels)]
+
+    def rows(owner):
+        return pl.ds(pl.multiple_of(owner * width, width), width)
+
+    def moved(table, phase, kind, owner, step, target):
+        view = table.at[rows(owner), lanes(step, chunk)]
+        return pltpu.make_async_remote_copy(
+            src_ref=view,
+            dst_ref=view,
+            send_sem=gather_send.at[phase, kind, step],
+            recv_sem=gather_recv.at[phase, kind, step],
+            device_id={"feat": target},
+            device_id_type=pl.DeviceIdType.MESH,
+        )
+
+    def slab(kind, target):
+        return pltpu.make_async_remote_copy(
+            src_ref=slab_ref.at[target],
+            dst_ref=slabs.at[me],
+            send_sem=slab_send.at[kind],
+            recv_sem=slab_recv.at[kind],
+            device_id={"feat": target},
+            device_id_type=pl.DeviceIdType.MESH,
+        )
+
+    def summed(level):
+        return pltpu.make_async_remote_copy(
+            src_ref=partial_ref.at[level],
+            dst_ref=arrived_ref.at[level],
+            send_sem=sum_send.at[level],
+            recv_sem=sum_recv.at[level],
+            device_id={"nodes": mates[level]},
+            device_id_type=pl.DeviceIdType.MESH,
+        )
+
+    def share(table, phase, step):
+        moved(table, phase, 0, me, step, cross).start()
+        moved(table, phase, 1, me, step, near).start()
+
+    def forward(table, phase, step):
+        moved(table, phase, 0, cross, step, cross).wait_recv()
+        moved(table, phase, 2, cross, step, near).start()
+
+    def complete(table, phase, step):
+        moved(table, phase, 1, near, step, near).wait_recv()
+        moved(table, phase, 2, far, step, near).wait_recv()
+
+    barrier = pltpu.get_barrier_semaphore()
+    for target in (near, cross, far):
+        pl.semaphore_signal(
+            barrier, inc=1, device_id={"feat": target}, device_id_type=pl.DeviceIdType.MESH
+        )
+    for mate in mates:
+        pl.semaphore_signal(
+            barrier, inc=1, device_id={"nodes": mate}, device_id_type=pl.DeviceIdType.MESH
+        )
+    all_agg[rows(me), :] = agg_ref[...]
+    slabs[me] = slab_ref[me]
+    partial_ref[0] = jnp.zeros(partial_ref.shape[1:], jnp.float32)
+    pl.semaphore_wait(barrier, 3 + levels)
+
+    def share_agg(step, carry):
+        share(all_agg, 0, step)
+        return carry
+
+    lax.fori_loop(0, steps, share_agg, 0)
+    for kind, target in enumerate((near, cross, far)):
+        slab(kind, target).start()
+
+    def dense(step):
+        complete(all_agg, 0, step)
+        part = lanes(step, chunk)
+        whole, agg = whole_ref[:, part], all_agg[:, part]
+        values = jnp.dot(self_ref[...], whole, preferred_element_type=jnp.float32) + jnp.dot(
+            neigh_ref[...], agg, preferred_element_type=jnp.float32
+        )
+        square = values * values
+        tanh_inner = jnp.tanh(gelu_scale * (values + gelu_cubic * square * values))
+        half = 0.5 * (1.0 + tanh_inner)
+        mixed_ref[:, part] = (values * half).astype(jnp.bfloat16)
+        slope = half + 0.5 * values * (1.0 - tanh_inner * tanh_inner) * gelu_scale * (
+            1.0 + 3.0 * gelu_cubic * square
+        )
+        grad = (cot_ref[:, part].astype(jnp.float32) * slope).astype(jnp.bfloat16)
+        all_grad[rows(me), part] = grad
+        share(all_grad, 1, step)
+        partial_ref[0, 0] += lax.dot_general(grad, whole, NT, preferred_element_type=jnp.float32)
+        partial_ref[0, 1] += lax.dot_general(grad, agg, NT, preferred_element_type=jnp.float32)
+
+    def dense_step(step, carry):
+        forward(all_agg, 0, step + 1)
+        dense(step)
+        return carry
+
+    forward(all_agg, 0, 0)
+    lax.fori_loop(0, steps - 1, dense_step, 0)
+    dense(steps - 1)
+
+    for kind, target in enumerate((near, cross, far)):
+        slab(kind, target).wait_recv()
+    back_ref[...] = slabs[...].reshape(back_ref.shape[1], back_ref.shape[0]).T
+
+    def project(step):
+        complete(all_grad, 1, step)
+        part = lanes(step, chunk)
+        both = jnp.dot(back_ref[...], all_grad[:, part], preferred_element_type=jnp.float32)
+        direct_ref[:, part] = both[:width]
+        scaled_ref[:, part] = (both[width:] * inverse_ref[:, part]).astype(jnp.bfloat16)
+
+    def project_step(step, carry):
+        forward(all_grad, 1, step + 1)
+        project(step)
+        return carry
+
+    forward(all_grad, 1, 0)
+    for level in range(levels):
+        summed(level).start()
+        lax.fori_loop(
+            level * (steps - 1) // levels, (level + 1) * (steps - 1) // levels, project_step, 0
+        )
+        summed(level).wait_recv()
+        partial_ref[level + 1] = partial_ref[level] + arrived_ref[level]
+    sums_ref[...] = partial_ref[levels]
+    project(steps - 1)
+
+    def finish(step, carry):
+        for phase, table in enumerate((all_agg, all_grad)):
+            moved(table, phase, 0, me, step, cross).wait_send()
+            moved(table, phase, 1, me, step, near).wait_send()
+            moved(table, phase, 2, cross, step, near).wait_send()
+        return carry
+
+    lax.fori_loop(0, steps, finish, 0)
+    for kind, target in enumerate((near, cross, far)):
+        slab(kind, target).wait_send()
+    for level in range(levels):
+        summed(level).wait_send()
 
 
 def spread_border_kernel(
-    own_blocks, rows_ref, cols_ref, order_ref, split_ref, weight_ref, whole_ref, self_ref, neigh_ref,
-    inverse_ref, direct_ref, scaled_ref, *rest
+    own_blocks, rows_ref, cols_ref, order_ref, split_ref, weight_ref, scaled_ref, *rest
 ):
     piece_refs, border_ref = rest[:-1], rest[-1]
     size = weight_ref.shape[1]
-    chunk = 8 * size
-
-    def dense(step, carry):
-        part = lanes(step, chunk)
-        grad = whole_ref[:, part]
-        direct_ref[:, part] = jnp.dot(self_ref[...], grad, preferred_element_type=jnp.float32)
-        scaled = jnp.dot(neigh_ref[...], grad, preferred_element_type=jnp.float32)
-        scaled_ref[:, part] = (scaled * inverse_ref[:, part]).astype(jnp.bfloat16)
-        return carry
-
-    lax.fori_loop(0, whole_ref.shape[1] // chunk, dense, 0)
     border_ref[...] = jnp.zeros_like(border_ref)
 
     def product(slot):
@@ -203,11 +318,10 @@
     inverse = (1.0 / degrees.astype(f32))[None, :]
     own = features.T
     whole_rows = lax.all_gather(own, "feat", axis=0, tiled=True)
-    both = jnp.concatenate([w_self.T, w_neigh.T], axis=1)
-    whole_both = lax.all_gather(both, "feat", axis=0, tiled=True)
-    start_row = lax.axis_index("feat") * width
-    rows_self = lax.dynamic_slice_in_dim(whole_both, start_row, width, 1).T
-    rows_neigh = lax.dynamic_slice_in_dim(whole_both, hidden + start_row, width, 1).T
+    groups = hidden // width
+    slab = jnp.concatenate(
+        [w.T.reshape(width, groups, width).transpose(1, 0, 2) for w in (w_self, w_neigh)], axis=2
+    )
     sends = send_lists[0]
 
     order, split, *pieces = pl.pallas_call(
@@ -241,34 +355,50 @@
         compiler_params=PARAMS,
         name="gather_border",
     )(*tables, edge_weights, total, inverse, *arrived)
-    whole_agg = lax.all_gather(aggregated, "feat", axis=0, tiled=True)
 
     chunk = 8 * size
     steps = row_count // chunk
-    column = pl.BlockSpec((width, chunk), lambda i: (0, i))
-    tall = pl.BlockSpec((hidden, chunk), lambda i: (0, i))
-    fixed = pl.BlockSpec((width, hidden), lambda i: (0, 0))
-    mixed, pre_grad, grad_self, grad_neigh = pl.pallas_call(
-        dense_kernel,
-        grid=(steps,),
-        out_shape=[shape((width, row_count), bf16)] * 2 + [shape((width, hidden), f32)] * 2,
-        in_specs=[tall, tall, fixed, fixed, column],
-        out_specs=[column, column, fixed, fixed],
-        compiler_params=PARAMS,
-        name="dense",
-    )(whole_rows, whole_agg, w_self.T, w_neigh.T, cotangent.T)
-    whole_grad = lax.all_gather(pre_grad, "feat", axis=0, tiled=True)
-    grad_self, grad_neigh = lax.psum((grad_self, grad_neigh), "nodes")
-
-    direct, scaled, *pieces = pl.pallas_call(
+    dma = pltpu.SemaphoreType.DMA
+    mixed, direct, scaled, sums = pl.pallas_call(
+        functools.partial(middle_kernel, levels, chunk),
+        out_shape=[
+            shape((width, row_count), bf16),
+            shape((width, row_count), f32),
+            shape((width, row_count), bf16),
+            shape((2, width, hidden), f32),
+        ],
+        in_specs=[VMEM] * 7,
+        out_specs=[VMEM] * 4,
+        scratch_shapes=[
+            pltpu.VMEM((hidden, row_count), bf16),
+            pltpu.VMEM((hidden, row_count), bf16),
+            pltpu.VMEM((groups, width, 2 * width), bf16),
+            pltpu.VMEM((2 * width, hidden), bf16),
+            pltpu.VMEM((levels + 1, 2, width, hidden), f32),
+            pltpu.VMEM((levels, 2, width, hidden), f32),
+            dma((2, 3, steps)),
+            dma((2, 3, steps)),
+            dma((3,)),
+            dma((3,)),
+            dma((levels,)),
+            dma((levels,)),
+        ],
+        compiler_params=pltpu.CompilerParams(
+            vmem_limit_bytes=56 * 1024 * 1024, collective_id=0, has_side_effects=True
+        ),
+        name="middle",
+    )(whole_rows, aggregated, w_self.T, w_neigh.T, slab, cotangent.T, inverse)
+    grad_self, grad_neigh = sums[0], sums[1]
+
+    pieces = pl.pallas_call(
         functools.partial(spread_border_kernel, own_blocks),
-        out_shape=[shape((width, row_count), f32), shape((width, row_count), bf16)] + [piece] * levels,
-        in_specs=[SMEM] * 4 + [VMEM] * 5,
-        out_specs=[VMEM] * (2 + levels),
+        out_shape=[piece] * levels,
+        in_specs=[SMEM] * 4 + [VMEM] * 2,
+        out_specs=[VMEM] * levels,
         scratch_shapes=[pltpu.VMEM((levels * border_size, width, size), f32)],
         compiler_params=PARAMS,
         name="spread_border",
-    )(*tables, edge_weights, whole_grad, rows_self, rows_neigh, inverse)
+    )(*tables, edge_weights, scaled)
     returned = [partner(value, "nodes", level) for level, value in enumerate(pieces)]
     total = pl.pallas_call(
         spread_own_kernel,

time: 216 us -> 141 us (0.65)
  waiting for transfers between devices: 108 us -> 6.12 us
  Pallas kernels: 68.2 us -> 102 us
  blocking collectives: 5.79 us -> 0 us
  local copies, waits for them, and re-layouts: 8.06 us -> 4.66 us
    all_gather x2 -> x0, waiting for transfers between devices: 63.9 us -> none  [the longest x1 36.7 us: local(): whole_agg = lax.all_gather(aggregated, 'feat', axis=0, tiled=True)]
    pallas_call x1, Pallas kernels: 9.74 us -> 56.3 us  [local(): pl.pallas_call(functools.partial(middle_kernel, levels, chunk), out_shape...]
    psum x1 -> x0, waiting for transfers between devices: 43.3 us -> none  [local(): grad_self, grad_neigh = lax.psum((grad_self, grad_neigh), 'nodes')]
    pallas_call x1, Pallas kernels: 13.7 us -> 7.3 us  [local(): pl.pallas_call(functools.partial(spread_border_kernel, own_blocks), out_s...]
    all_gather x1 -> x0, blocking collectives: 5.79 us -> none  [local(): whole_both = lax.all_gather(both, 'feat', axis=0, tiled=True)]
    unnamed x23 -> x24, local copies, waits for them, and re-layouts: 7.96 us -> 3.79 us
    ppermute x6, waiting for transfers between devices: 0.02 us -> 2.85 us  [partner(): lax.ppermute(value, axis, [(i, i ^ 1 << apart) for i in range(lax.axis_si...]
    all_gather x1, waiting for transfers between devices: 0.03 us -> 2.59 us  [local(): whole_rows = lax.all_gather(own, 'feat', axis=0, tiled=True)]
  transfers between devices with their start and end apart: 10 -> 7, of which waited for: 3 -> 3; matrix products, arithmetic and copies ran while one was open for 2% -> 2% of each run, Pallas kernels for 27% -> 25%
where the time goes in v2:
time: 141 us; the launch traced here: 140 us
  Pallas kernels  102 us (72%)
  between operations  14.8 us (10%)
  starting transfers between devices  11.5 us (8%)
  waiting for transfers between devices  6.12 us (4%)
  local copies, waits for them, and re-layouts  4.66 us (3%)
    pallas_call x1, Pallas kernels, local(): pl.pallas_call(functools.partial(middle_kernel, levels, chunk), out_shape...  56.3 us
    ppermute x6, starting transfers between devices, partner(): lax.ppermute(value, axis, [(i, i ^ 1 << apart) for i in range(lax.axis_si...  11.5 us
    pallas_call x1, Pallas kernels, local(): pl.pallas_call(gather_own_kernel, out_shape=shape((width, row_count), f32...  10.6 us
    pallas_call x1, Pallas kernels, local(): pl.pallas_call(spread_own_kernel, out_shape=shape((width, row_count), f32...  10 us
    pallas_call x1, Pallas kernels, local(): pl.pallas_call(functools.partial(gather_border_kernel, own_blocks), out_s...  9.11 us
    pallas_call x1, Pallas kernels, local(): pl.pallas_call(functools.partial(spread_border_kernel, own_blocks), out_s...  7.3 us
    pallas_call x1, Pallas kernels, local(): pl.pallas_call(functools.partial(pack_kernel, own_blocks), out_shape=[sha...  5.14 us
    unnamed x24, local copies, waits for them, and re-layouts  3.79 us
  transfers between devices with their start and end apart: 7, of which 3 were waited for; matrix products, arithmetic and copies ran while one was open for 2% of the time, Pallas kernels for 25%

profile of v2, /device:TPU:0, one launch (start us, length us, event | category | flops | bytes accessed | tf_op | source)
XLA Modules:
  0.0 140.2 jit_solution(5859385647564399382)
XLA Ops:
  7.2 0.0 copy-start.7
  7.2 0.0 copy-start.8
  7.2 0.0 all-gather.2.cloned.1.call-start
  7.2 0.7 all-gather.2.cloned.1.call-update
  8.6 1.2 copy.20
  9.8 5.1 %pack.1 = (s32[256]{0:T(256)}, s32[2]{0:T(128)}, bf16[16,64,128]{2,1,0:T(8,128)(2,1)}, bf16[16,64,128]{2,1,0:T(8,128)(2,1)}, bf16[16,64,128]{2,1,0:T(8,128)(2,1)}) custom-call(s32[256]{0:T(256)} %cols_ref.9, s32[1]{0:T(128)S(6)} %copy.22.count_ref, s32[3,16]{1,0:T(4,128)} %bitcast.34, bf16[64,8192]{1,0:T(8,128)(2,1)} %bitcast.23), custom_call_target="tpu_custom_call" | custom-call | tf_op jit(solution)/shard_map/pack/pallas_call | solution.py:327
  15.0 3.2 %collective-permute-start = (bf16[16,64,128]{2,1,0:T(8,128)(2,1)}, bf16[16,64,128]{2,1,0:T(8,128)(2,1)S(1)}, u32[]{:S(2)}, u32[]{:S(2)}) collective-permute-start(bf16[16,64,128]{2,1,0:T(8,128)(2,1)} %get-tuple-element.18), channel_id=1, source_target_pairs={{0,4},{4,0},{8,12},{12,8},{16,20},{20,16},{24,28},{28,24},{1,5},{5... | collective-permute-start | bytes 786440 | tf_op jit(solution)/shard_map/ppermute | solution.py:20
  18.1 0.2 collective-permute-start.1
  18.3 3.7 %collective-permute-start.2 = (bf16[16,64,128]{2,1,0:T(8,128)(2,1)}, bf16[16,64,128]{2,1,0:T(8,128)(2,1)S(1)}, u32[]{:S(2)}, u32[]{:S(2)}) collective-permute-start(bf16[16,64,128]{2,1,0:T(8,128)(2,1)} %get-tuple-element.20), channel_id=1, source_target_pairs={{0,16},{4,20},{8,24},{12,28},{16,0},{20,4},{24,8},{28,12},{1,17},{... | collective-permute-start | bytes 786440 | tf_op jit(solution)/shard_map/ppermute | solution.py:20
  22.0 0.0 copy-done.7
  22.0 0.1 reshape.14
  22.1 0.0 copy-done.8
  22.1 0.1 reshape.15
  22.2 0.0 copy-start.10
  22.2 10.6 %gather_own.1.total_ref = f32[64,8192]{1,0:T(8,128)} custom-call(s32[256]{0:T(256)} %rows_ref.7, s32[256]{0:T(256)} %cols_ref.9, s32[256]{0:T(256)} %get-tuple-element.16.order_ref, s32[2]{0:T(128)} %get-tuple-element.17.split_ref, bf16[256,128,128]{2,1,0:T(8,128)(2,1)} %weight_ref.7, bf16[64,8192]{1,0:T(8,128)(2,1)} %bitcast.24), custom_call_target="tpu_custom_call" | custom-call | flops 4000000000 | bytes 12000000 | tf_op jit(solution)/shard_map/gather_own/pallas_call | solution.py:337
  32.9 0.7 pad_maximum_fusion.slab_ref
  33.6 0.0 copy-done.10
  33.6 0.6 convert_divide_fusion
  34.2 0.0 collective-permute-done.rest_0_
  34.2 0.0 copy-start.1
  34.2 0.0 collective-permute-done.1.rest_1_
  34.2 0.0 copy-start.3
  34.2 0.0 collective-permute-done.2.rest_2_
  34.2 0.0 copy-start.5
  34.3 0.7 copy-done.1
  34.9 0.1 copy-done.3
  35.0 0.1 copy-done.5
  35.1 9.1 %gather_border.1.agg_ref = bf16[64,8192]{1,0:T(8,128)(2,1)} custom-call(s32[256]{0:T(256)} %rows_ref.7, s32[256]{0:T(256)} %cols_ref.9, s32[256]{0:T(256)} %get-tuple-element.16.order_ref, s32[2]{0:T(128)} %get-tuple-element.17.split_ref, bf16[256,128,128]{2,1,0:T(8,128)(2,1)} %weight_ref.7, f32[64,8192]{1,0:T(8,128)} %gather_own.1.total_ref, ...), custom_call_target="tpu_custom_call" | custom-call | tf_op jit(solution)/shard_map/gather_border/pallas_call | solution.py:346
  44.2 2.6 %all-gather.2.cloned.1.call-done.whole_ref = bf16[256,8192]{1,0:T(8,128)(2,1)} async-done(((bf16[64,8192]{1,0:T(8,128)(2,1)}), bf16[256,8192]{1,0:T(8,128)(2,1)}) %all-gather.2.cloned.1.call-update) | async-done | bytes 4194320 | tf_op jit(solution)/shard_map/all_gather | solution.py:320
  46.8 56.3 %middle.1 = (bf16[64,8192]{1,0:T(8,128)(2,1)}, f32[64,8192]{1,0:T(8,128)}, bf16[64,8192]{1,0:T(8,128)(2,1)}, f32[2,64,256]{2,1,0:T(8,128)}) custom-call(bf16[256,8192]{1,0:T(8,128)(2,1)} %all-gather.2.cloned.1.call-done.whole_ref, bf16[64,8192]{1,0:T(8,128)(2,1)} %gather_border.1.agg_ref, bf16[64,256]{1,0:T(8,128)(2,1)} %bitcast.30, ...), custom_call_target="tpu_custom_call" | custom-call | tf_op jit(solution)/shard_map/middle/pallas_call | solution.py:362
  103.1 7.3 %spread_border.1 = (bf16[16,64,128]{2,1,0:T(8,128)(2,1)}, bf16[16,64,128]{2,1,0:T(8,128)(2,1)}, bf16[16,64,128]{2,1,0:T(8,128)(2,1)}) custom-call(s32[256]{0:T(256)} %rows_ref.7, s32[256]{0:T(256)} %cols_ref.9, s32[256]{0:T(256)} %get-tuple-element.16.order_ref, s32[2]{0:T(128)} %get-tuple-element.17.split_ref, bf16[256,128,128]{2,1,0:T(8,128)(2,1)} %weight_ref.7, ...), custom_call_target="tpu_custom_call" | custom-call | tf_op jit(solution)/shard_map/spread_border/pallas_call | solution.py:393
  110.4 2.6 %collective-permute-start.3 = (bf16[16,64,128]{2,1,0:T(8,128)(2,1)}, bf16[16,64,128]{2,1,0:T(8,128)(2,1)S(1)}, u32[]{:S(2)}, u32[]{:S(2)}) collective-permute-start(bf16[16,64,128]{2,1,0:T(8,128)(2,1)} %get-tuple-element.24), channel_id=1, source_target_pairs={{0,4},{4,0},{8,12},{12,8},{16,20},{20,16},{24,28},{28,24},{1,5},{5... | collective-permute-start | bytes 786440 | tf_op jit(solution)/shard_map/ppermute | solution.py:20
  113.0 0.0 collective-permute-start.4
  113.0 1.9 %collective-permute-start.5 = (bf16[16,64,128]{2,1,0:T(8,128)(2,1)}, bf16[16,64,128]{2,1,0:T(8,128)(2,1)S(1)}, u32[]{:S(2)}, u32[]{:S(2)}) collective-permute-start(bf16[16,64,128]{2,1,0:T(8,128)(2,1)} %get-tuple-element.26), channel_id=1, source_target_pairs={{0,16},{4,20},{8,24},{12,28},{16,0},{20,4},{24,8},{28,12},{1,17},{... | collective-permute-start | bytes 786440 | tf_op jit(solution)/shard_map/ppermute | solution.py:20
  114.9 0.0 copy-start.9
  114.9 10.0 %spread_own.1.total_ref = f32[64,8192]{1,0:T(8,128)} custom-call(s32[256]{0:T(256)} %rows_ref.7, s32[256]{0:T(256)} %cols_ref.9, s32[256]{0:T(256)} %get-tuple-element.16.order_ref, s32[2]{0:T(128)} %get-tuple-element.17.split_ref, bf16[256,128,128]{2,1,0:T(8,128)(2,1)} %weight_ref.7, bf16[64,8192]{1,0:T(8,128)(2,1)} %get-tuple-element.22.scaled_ref, ...), custom_call_target="tpu_custom_call" | custom-call | flops 4000000000 | bytes 12000000 | tf_op jit(solution)/shard_map/spread_own/pallas_call | solution.py:403
  124.9 0.0 copy-done.9
  124.9 0.0 copy-start
  124.9 0.7 slice_bitcast_fusion
  125.5 0.0 collective-permute-done.3.rest_0_
  125.5 0.0 copy-start.2
  125.5 1.3 collective-permute-done.4.rest_1_
  126.9 0.0 copy-start.4
  126.9 1.5 %collective-permute-done.5.rest_2_ = bf16[16,64,128]{2,1,0:T(8,128)(2,1)S(1)} collective-permute-done((bf16[16,64,128]{2,1,0:T(8,128)(2,1)}, bf16[16,64,128]{2,1,0:T(8,128)(2,1)S(1)}, u32[]{:S(2)}, u32[]{:S(2)}) %collective-permute-start.5) | collective-permute-done | bytes 262176 | tf_op jit(solution)/shard_map/ppermute | solution.py:20
  128.4 0.0 copy-done.2
  128.4 0.0 copy-done.4
  128.4 0.0 copy-start.6
  128.4 0.7 copy-done.6
  129.1 3.3 %collect.1 = bf16[64,8192]{1,0:T(8,128)(2,1)} custom-call(s32[3,16]{1,0:T(4,128)} %bitcast.35, f32[64,8192]{1,0:T(8,128)} %spread_own.1.total_ref, bf16[16,64,128]{2,1,0:T(8,128)(2,1)} %copy-done.2, bf16[16,64,128]{2,1,0:T(8,128)(2,1)} %copy-done.4, bf16[16,64,128]{2,1,0:T(8,128)(2,1)} %copy-done.6), custom_call_target="tpu_custom_call" | custom-call | tf_op jit(solution)/shard_map/collect/pallas_call | solution.py:412
  132.4 0.0 copy-done
  132.4 1.0 copy.23
  (1 shorter events, 0.0 us)
Async XLA Ops:
  7.2 14.8 %copy-start.7 = (bf16[256,64]{0,1:T(8,128)(2,1)S(1)}, bf16[256,64]{0,1:T(8,128)(2,1)}, u32[]{:S(2)}) copy-start(bf16[256,64]{0,1:T(8,128)(2,1)} %param.17) | copy-start | bytes 98308
  7.2 14.9 %copy-start.8 = (bf16[256,64]{0,1:T(8,128)(2,1)S(1)}, bf16[256,64]{0,1:T(8,128)(2,1)}, u32[]{:S(2)}) copy-start(bf16[256,64]{0,1:T(8,128)(2,1)} %param.18) | copy-start | bytes 98308
  7.2 39.6 %all-gather.2.cloned.1.call-start = ((), (), s32[]{:S(2)}) async-start(), calls=%async_computation | async-start | bytes 5242880 | tf_op jit(solution)/shard_map/all_gather | solution.py:320
  15.0 19.3 %collective-permute-start = (bf16[16,64,128]{2,1,0:T(8,128)(2,1)}, bf16[16,64,128]{2,1,0:T(8,128)(2,1)S(1)}, u32[]{:S(2)}, u32[]{:S(2)}) collective-permute-start(bf16[16,64,128]{2,1,0:T(8,128)(2,1)} %get-tuple-element.18), channel_id=1, source_target_pairs={{0,4},{4,0},{8,12},{12,8},{16,20},{20,16},{24,28},{28,24},{1,5},{5... | collective-permute-start | bytes 786440 | tf_op jit(solution)/shard_map/ppermute | solution.py:20
  18.1 16.1 %collective-permute-start.1 = (bf16[16,64,128]{2,1,0:T(8,128)(2,1)}, bf16[16,64,128]{2,1,0:T(8,128)(2,1)S(1)}, u32[]{:S(2)}, u32[]{:S(2)}) collective-permute-start(bf16[16,64,128]{2,1,0:T(8,128)(2,1)} %get-tuple-element.19), channel_id=1, source_target_pairs={{0,8},{4,12},{8,0},{12,4},{16,24},{20,28},{24,16},{28,20},{1,9},{5... | collective-permute-start | bytes 786440 | tf_op jit(solution)/shard_map/ppermute | solution.py:20
  18.3 15.9 %collective-permute-start.2 = (bf16[16,64,128]{2,1,0:T(8,128)(2,1)}, bf16[16,64,128]{2,1,0:T(8,128)(2,1)S(1)}, u32[]{:S(2)}, u32[]{:S(2)}) collective-permute-start(bf16[16,64,128]{2,1,0:T(8,128)(2,1)} %get-tuple-element.20), channel_id=1, source_target_pairs={{0,16},{4,20},{8,24},{12,28},{16,0},{20,4},{24,8},{28,12},{1,17},{... | collective-permute-start | bytes 786440 | tf_op jit(solution)/shard_map/ppermute | solution.py:20
  22.2 11.4 %copy-start.10 = (s32[8192]{0:T(1024)S(1)}, s32[8192]{0:T(1024)}, u32[]{:S(2)}) copy-start(s32[8192]{0:T(1024)} %param.11) | copy-start | bytes 98308
  34.2 0.7 copy-start.1
  34.2 0.8 copy-start.3
  34.2 0.8 copy-start.5
  110.4 15.1 %collective-permute-start.3 = (bf16[16,64,128]{2,1,0:T(8,128)(2,1)}, bf16[16,64,128]{2,1,0:T(8,128)(2,1)S(1)}, u32[]{:S(2)}, u32[]{:S(2)}) collective-permute-start(bf16[16,64,128]{2,1,0:T(8,128)(2,1)} %get-tuple-element.24), channel_id=1, source_target_pairs={{0,4},{4,0},{8,12},{12,8},{16,20},{20,16},{24,28},{28,24},{1,5},{5... | collective-permute-start | bytes 786440 | tf_op jit(solution)/shard_map/ppermute | solution.py:20
  113.0 13.9 %collective-permute-start.4 = (bf16[16,64,128]{2,1,0:T(8,128)(2,1)}, bf16[16,64,128]{2,1,0:T(8,128)(2,1)S(1)}, u32[]{:S(2)}, u32[]{:S(2)}) collective-permute-start(bf16[16,64,128]{2,1,0:T(8,128)(2,1)} %get-tuple-element.25), channel_id=1, source_target_pairs={{0,8},{4,12},{8,0},{12,4},{16,24},{20,28},{24,16},{28,20},{1,9},{5... | collective-permute-start | bytes 786440 | tf_op jit(solution)/shard_map/ppermute | solution.py:20
  113.0 15.4 %collective-permute-start.5 = (bf16[16,64,128]{2,1,0:T(8,128)(2,1)}, bf16[16,64,128]{2,1,0:T(8,128)(2,1)S(1)}, u32[]{:S(2)}, u32[]{:S(2)}) collective-permute-start(bf16[16,64,128]{2,1,0:T(8,128)(2,1)} %get-tuple-element.26), channel_id=1, source_target_pairs={{0,16},{4,20},{8,24},{12,28},{16,0},{20,4},{24,8},{28,12},{1,17},{... | collective-permute-start | bytes 786440 | tf_op jit(solution)/shard_map/ppermute | solution.py:20
  114.9 10.0 %copy-start.9 = (f32[2,64,256]{2,1,0:T(8,128)S(1)}, f32[2,64,256]{2,1,0:T(8,128)}, u32[]{:S(2)}) copy-start(f32[2,64,256]{2,1,0:T(8,128)} %get-tuple-element.27) | copy-start | bytes 393220
  124.9 7.5 %copy-start = (bf16[64,8192]{1,0:T(8,128)(2,1)S(1)}, bf16[64,8192]{1,0:T(8,128)(2,1)}, u32[]{:S(2)}) copy-start(bf16[64,8192]{1,0:T(8,128)(2,1)} %get-tuple-element.21) | copy-start | bytes 3145732
  125.5 2.8 %copy-start.2 = (bf16[16,64,128]{2,1,0:T(8,128)(2,1)}, bf16[16,64,128]{2,1,0:T(8,128)(2,1)S(1)}, u32[]{:S(2)}) copy-start(bf16[16,64,128]{2,1,0:T(8,128)(2,1)S(1)} %collective-permute-done.3.rest_0_) | copy-start | bytes 786436
  126.9 1.5 %copy-start.4 = (bf16[16,64,128]{2,1,0:T(8,128)(2,1)}, bf16[16,64,128]{2,1,0:T(8,128)(2,1)S(1)}, u32[]{:S(2)}) copy-start(bf16[16,64,128]{2,1,0:T(8,128)(2,1)S(1)} %collective-permute-done.4.rest_1_) | copy-start | bytes 786436
  128.4 0.7 copy-start.6
Sparse Core Ops, SparseCore 0:
  9.6 37.1 all-gather.1

commit v3 on v2

--- a/solution.py
+++ b/solution.py
@@ -9,9 +9,12 @@
 
 gelu_scale = 0.7978845608028654
 gelu_cubic = 0.044715
-GROUP = 8
+GROUP = 16
+TAIL = 4
+PARTS = 4
 SMEM = pl.BlockSpec(memory_space=pltpu.SMEM)
 VMEM = pl.BlockSpec(memory_space=pltpu.VMEM)
+ANY = pl.BlockSpec(memory_space=pl.ANY)
 PARAMS = pltpu.CompilerParams(vmem_limit_bytes=56 * 1024 * 1024)
 NT = (((1,), (1,)), ((), ()))
 
@@ -24,82 +27,124 @@
     return pl.ds(pl.multiple_of(index * size, size), size)
 
 
-def for_slots(first, last, order_ref, product, store):
+def for_slots(bounds, tables, product, store):
+    def batch(width, start):
+        def body(step, carry):
+            first = start + step * width
+            entries = [tuple(table[first + k] for table in tables) for k in range(width)]
+            values = [product(*entry) for entry in entries]
+            for entry, value in zip(entries, values):
+                store(*entry, value)
+            return carry
+
+        return body
+
+    first, last = bounds
     groups = (last - first) // GROUP
-
-    def several(step, carry):
-        slots = [order_ref[first + step * GROUP + k] for k in range(GROUP)]
-        values = [product(slot) for slot in slots]
-        for slot, value in zip(slots, values):
-            store(slot, value)
-        return carry
-
-    def single(step, carry):
-        slot = order_ref[step]
-        store(slot, product(slot))
-        return carry
-
-    lax.fori_loop(0, groups, several, 0)
-    lax.fori_loop(first + groups * GROUP, last, single, 0)
-
-
-def pack_kernel(own_blocks, cols_ref, count_ref, sends_ref, table_ref, order_ref, split_ref, *piece_refs):
+    middle = first + groups * GROUP
+    lax.fori_loop(0, groups, batch(GROUP, first), 0)
+    lax.fori_loop(0, (last - middle) // TAIL, batch(TAIL, middle), 0)
+
+
+def fetch(source_ref, weight_ref, sem):
+    slots = source_ref.shape[0]
+    share = slots // PARTS
+    copies = [
+        pltpu.make_async_copy(
+            source_ref.at[pl.ds(k * share, share)], weight_ref.at[pl.ds(k * share, share)], sem.at[k]
+        )
+        for k in range(PARTS)
+    ]
+    for copy in copies:
+        copy.start()
+    weight_ref[slots] = jnp.zeros(weight_ref.shape[1:], weight_ref.dtype)
+    return copies
+
+
+def pack_kernel(sends_ref, table_ref, *piece_refs):
     size = piece_refs[0].shape[2]
     for level, piece_ref in enumerate(piece_refs):
         for j in range(piece_ref.shape[0]):
             piece_ref[j] = table_ref[:, lanes(sends_ref[level, j], size)]
+
+
+def gather_own_kernel(
+    own_blocks, rows_ref, cols_ref, count_ref, source_ref, table_ref,
+    total_ref, slot_list, row_list, col_list, bound_ref, weight_ref, sem,
+):
+    copies = fetch(source_ref, weight_ref, sem)
+    slots, size, _ = source_ref.shape
+    share = slots // PARTS
     count = count_ref[0]
+    total_ref[...] = jnp.zeros_like(total_ref)
 
     def place(slot, state):
-        low, high = state
-        own = cols_ref[slot] < own_blocks
-        order_ref[jnp.where(own, low, high)] = slot
-        return jnp.where(own, low + 1, low), jnp.where(own, high, high - 1)
-
-    low, _ = lax.fori_loop(0, count, place, (jnp.int32(0), count - 1))
-    split_ref[0] = low
-    split_ref[1] = count
-
-
-def gather_own_kernel(rows_ref, cols_ref, order_ref, split_ref, weight_ref, table_ref, total_ref):
-    size = weight_ref.shape[1]
-    total_ref[...] = jnp.zeros_like(total_ref)
-
-    def product(slot):
-        block = table_ref[:, lanes(cols_ref[slot], size)]
+        own_at, border_at = state
+        col = cols_ref[slot]
+        own = col < own_blocks
+        at = jnp.where(own, own_at, border_at)
+        slot_list[at] = slot
+        row_list[at] = rows_ref[slot]
+        col_list[at] = jnp.where(own, col, col - own_blocks)
+        return jnp.where(own, own_at + 1, own_at), jnp.where(own, border_at, border_at + 1)
+
+    def pad(at):
+        for k in range(TAIL - 1):
+            slot_list[at + k] = slots
+            row_list[at + k] = 0
+            col_list[at + k] = 0
+        return (at + TAIL - 1) // TAIL * TAIL
+
+    state = (jnp.int32(0), jnp.int32(slots + PARTS * TAIL))
+    bound_ref[0, 0], bound_ref[1, 0] = state
+    for k in range(PARTS):
+        state = lax.fori_loop(
+            jnp.minimum(k * share, count), jnp.minimum((k + 1) * share, count), place, state
+        )
+        state = pad(state[0]), pad(state[1])
+        bound_ref[0, k + 1], bound_ref[1, k + 1] = state
+
+    def product(slot, row, col):
+        block = table_ref[:, lanes(col, size)]
         return lax.dot_general(block, weight_ref[slot], NT, preferred_element_type=jnp.float32)
 
-    def store(slot, value):
-        total_ref[:, lanes(rows_ref[slot], size)] += value
-
-    for_slots(0, split_ref[0], order_ref, product, store)
+    def store(slot, row, col, value):
+        total_ref[:, lanes(row, size)] += value
+
+    for k, copy in enumerate(copies):
+        copy.wait()
+        for_slots((bound_ref[0, k], bound_ref[0, k + 1]), (slot_list, row_list, col_list), product, store)
 
 
 def gather_border_kernel(
-    own_blocks, rows_ref, cols_ref, order_ref, split_ref, weight_ref, total_ref, inverse_ref, *rest
+    slot_list, row_list, col_list, bound_ref, source_ref, total_ref, inverse_ref, *rest
 ):
-    piece_refs, out_ref, border_ref, sum_ref = rest[:-3], rest[-3], rest[-2], rest[-1]
-    size = weight_ref.shape[1]
+    *piece_refs, out_ref, weight_ref, border_ref, sum_ref, sem = rest
+    copies = fetch(source_ref, weight_ref, sem)
+    size = source_ref.shape[1]
     border_size = piece_refs[0].shape[0]
     for level, piece_ref in enumerate(piece_refs):
         border_ref[level * border_size : (level + 1) * border_size] = piece_ref[...]
     sum_ref[...] = total_ref[...]
 
-    def product(slot):
-        block = border_ref[cols_ref[slot] - own_blocks]
-        return lax.dot_general(block, weight_ref[slot], NT, preferred_element_type=jnp.float32)
-
-    def store(slot, value):
-        sum_ref[:, lanes(rows_ref[slot], size)] += value
-
-    for_slots(split_ref[0], split_ref[1], order_ref, product, store)
+    def product(slot, row, col):
+        return lax.dot_general(
+            border_ref[col], weight_ref[slot], NT, preferred_element_type=jnp.float32
+        )
+
+    def store(slot, row, col, value):
+        sum_ref[:, lanes(row, size)] += value
+
+    for k, copy in enumerate(copies):
+        copy.wait()
+        for_slots((bound_ref[1, k], bound_ref[1, k + 1]), (slot_list, row_list, col_list), product, store)
     out_ref[...] = (sum_ref[...] * inverse_ref[...]).astype(jnp.bfloat16)
 
 
 def middle_kernel(
-    levels, chunk, whole_ref, agg_ref, self_ref, neigh_ref, slab_ref, cot_ref, inverse_ref,
+    levels, chunk, own_ref, cross_ref, agg_ref, self_ref, neigh_ref, slab_ref, cot_ref, inverse_ref,
     mixed_ref, direct_ref, scaled_ref, sums_ref,
-    all_agg, all_grad, slabs, back_ref, partial_ref, arrived_ref,
+    all_agg, all_grad, whole_ref, slabs, back_ref, partial_ref, arrived_ref,
     gather_send, gather_recv, slab_send, slab_recv, sum_send, sum_recv,
 ):
     width, nodes = agg_ref.shape
@@ -166,12 +211,16 @@
             barrier, inc=1, device_id={"nodes": mate}, device_id_type=pl.DeviceIdType.MESH
         )
     all_agg[rows(me), :] = agg_ref[...]
+    whole_ref[rows(me), :] = own_ref[...]
+    whole_ref[rows(cross), :] = cross_ref[...]
     slabs[me] = slab_ref[me]
     partial_ref[0] = jnp.zeros(partial_ref.shape[1:], jnp.float32)
     pl.semaphore_wait(barrier, 3 + levels)
 
     def share_agg(step, carry):
         share(all_agg, 0, step)
+        moved(whole_ref, 2, 1, me, step, near).start()
+        moved(whole_ref, 2, 2, cross, step, near).start()
         return carry
 
     lax.fori_loop(0, steps, share_agg, 0)
@@ -179,6 +228,7 @@
         slab(kind, target).start()
 
     def dense(step):
+        complete(whole_ref, 2, step)
         complete(all_agg, 0, step)
         part = lanes(step, chunk)
         whole, agg = whole_ref[:, part], all_agg[:, part]
@@ -239,6 +289,8 @@
             moved(table, phase, 0, me, step, cross).wait_send()
             moved(table, phase, 1, me, step, near).wait_send()
             moved(table, phase, 2, cross, step, near).wait_send()
+        moved(whole_ref, 2, 1, me, step, near).wait_send()
+        moved(whole_ref, 2, 2, cross, step, near).wait_send()
         return carry
 
     lax.fori_loop(0, steps, finish, 0)
@@ -248,40 +300,44 @@
         summed(level).wait_send()
 
 
-def spread_border_kernel(
-    own_blocks, rows_ref, cols_ref, order_ref, split_ref, weight_ref, scaled_ref, *rest
-):
-    piece_refs, border_ref = rest[:-1], rest[-1]
-    size = weight_ref.shape[1]
+def spread_border_kernel(slot_list, row_list, col_list, bound_ref, source_ref, scaled_ref, *rest):
+    *piece_refs, weight_ref, border_ref, sem = rest
+    copies = fetch(source_ref, weight_ref, sem)
+    size = source_ref.shape[1]
     border_ref[...] = jnp.zeros_like(border_ref)
 
-    def product(slot):
-        block = scaled_ref[:, lanes(rows_ref[slot], size)]
+    def product(slot, row, col):
+        block = scaled_ref[:, lanes(row, size)]
         return jnp.dot(block, weight_ref[slot], preferred_element_type=jnp.float32)
 
-    def store(slot, value):
-        border_ref[cols_ref[slot] - own_blocks] += value
-
-    for_slots(split_ref[0], split_ref[1], order_ref, product, store)
+    def store(slot, row, col, value):
+        border_ref[col] += value
+
+    for k, copy in enumerate(copies):
+        copy.wait()
+        for_slots((bound_ref[1, k], bound_ref[1, k + 1]), (slot_list, row_list, col_list), product, store)
     border_size = piece_refs[0].shape[0]
     for level, piece_ref in enumerate(piece_refs):
         piece_ref[...] = border_ref[level * border_size : (level + 1) * border_size].astype(jnp.bfloat16)
 
 
 def spread_own_kernel(
-    rows_ref, cols_ref, order_ref, split_ref, weight_ref, scaled_ref, direct_ref, total_ref
+    slot_list, row_list, col_list, bound_ref, source_ref, scaled_ref, direct_ref, total_ref, weight_ref, sem
 ):
-    size = weight_ref.shape[1]
+    copies = fetch(source_ref, weight_ref, sem)
+    size = source_ref.shape[1]
     total_ref[...] = direct_ref[...]
 
-    def product(slot):
-        block = scaled_ref[:, lanes(rows_ref[slot], size)]
+    def product(slot, row, col):
+        block = scaled_ref[:, lanes(row, size)]
         return jnp.dot(block, weight_ref[slot], preferred_element_type=jnp.float32)
 
-    def store(slot, value):
-        total_ref[:, lanes(cols_ref[slot], size)] += value
-
-    for_slots(0, split_ref[0], order_ref, product, store)
+    def store(slot, row, col, value):
+        total_ref[:, lanes(col, size)] += value
+
+    for k, copy in enumerate(copies):
+        copy.wait()
+        for_slots((bound_ref[0, k], bound_ref[0, k + 1]), (slot_list, row_list, col_list), product, store)
 
 
 def collect_kernel(sends_ref, total_ref, *rest):
@@ -317,40 +373,45 @@
     piece = shape((border_size, width, size), bf16)
     inverse = (1.0 / degrees.astype(f32))[None, :]
     own = features.T
-    whole_rows = lax.all_gather(own, "feat", axis=0, tiled=True)
+    cross = partner(own, "feat", 1)
     groups = hidden // width
     slab = jnp.concatenate(
         [w.T.reshape(width, groups, width).transpose(1, 0, 2) for w in (w_self, w_neigh)], axis=2
     )
     sends = send_lists[0]
 
-    order, split, *pieces = pl.pallas_call(
-        functools.partial(pack_kernel, own_blocks),
-        out_shape=[shape((slot_count,), i32), shape((2,), i32)] + [piece] * levels,
-        in_specs=[SMEM, SMEM, SMEM, VMEM],
-        out_specs=[SMEM, SMEM] + [VMEM] * levels,
+    pieces = pl.pallas_call(
+        pack_kernel,
+        out_shape=[piece] * levels,
+        in_specs=[SMEM, VMEM],
+        out_specs=[VMEM] * levels,
         compiler_params=PARAMS,
         name="pack",
-    )(block_cols, block_counts, sends, own)
-    tables = (block_rows, block_cols, order, split)
+    )(sends, own)
     arrived = [partner(value, "nodes", level) for level, value in enumerate(pieces)]
-    total = pl.pallas_call(
-        gather_own_kernel,
-        out_shape=shape((width, row_count), f32),
-        in_specs=[SMEM] * 4 + [VMEM] * 2,
-        out_specs=VMEM,
+    listed = shape((2 * (slot_count + PARTS * TAIL),), i32)
+    weight = pltpu.VMEM((slot_count + 1, size, size), bf16)
+    sem = pltpu.SemaphoreType.DMA((PARTS,))
+    total, *tables = pl.pallas_call(
+        functools.partial(gather_own_kernel, own_blocks),
+        out_shape=[shape((width, row_count), f32), listed, listed, listed, shape((2, PARTS + 1), i32)],
+        in_specs=[SMEM] * 3 + [ANY, VMEM],
+        out_specs=[VMEM] + [SMEM] * 4,
+        scratch_shapes=[weight, sem],
         compiler_params=PARAMS,
         cost_estimate=pl.CostEstimate(flops=4 * 10**9, bytes_accessed=12 * 10**6, transcendentals=0),
         name="gather_own",
-    )(*tables, edge_weights, own)
+    )(block_rows, block_cols, block_counts, edge_weights, own)
     aggregated = pl.pallas_call(
-        functools.partial(gather_border_kernel, own_blocks),
+        gather_border_kernel,
         out_shape=shape((width, row_count), bf16),
-        in_specs=[SMEM] * 4 + [VMEM] * (3 + levels),
+        in_specs=[SMEM] * 4 + [ANY] + [VMEM] * (2 + levels),
         out_specs=VMEM,
         scratch_shapes=[
+            weight,
             pltpu.VMEM((levels * border_size, width, size), bf16),
             pltpu.VMEM((width, row_count), f32),
+            sem,
         ],
         compiler_params=PARAMS,
         name="gather_border",
@@ -367,17 +428,18 @@
             shape((width, row_count), bf16),
             shape((2, width, hidden), f32),
         ],
-        in_specs=[VMEM] * 7,
+        in_specs=[VMEM] * 8,
         out_specs=[VMEM] * 4,
         scratch_shapes=[
+            pltpu.VMEM((hidden, row_count), bf16),
             pltpu.VMEM((hidden, row_count), bf16),
             pltpu.VMEM((hidden, row_count), bf16),
             pltpu.VMEM((groups, width, 2 * width), bf16),
             pltpu.VMEM((2 * width, hidden), bf16),
             pltpu.VMEM((levels + 1, 2, width, hidden), f32),
             pltpu.VMEM((levels, 2, width, hidden), f32),
-            dma((2, 3, steps)),
-            dma((2, 3, steps)),
+            dma((3, 3, steps)),
+            dma((3, 3, steps)),
             dma((3,)),
             dma((3,)),
             dma((levels,)),
@@ -387,15 +449,15 @@
             vmem_limit_bytes=56 * 1024 * 1024, collective_id=0, has_side_effects=True
         ),
         name="middle",
-    )(whole_rows, aggregated, w_self.T, w_neigh.T, slab, cotangent.T, inverse)
+    )(own, cross, aggregated, w_self.T, w_neigh.T, slab, cotangent.T, inverse)
     grad_self, grad_neigh = sums[0], sums[1]
 
     pieces = pl.pallas_call(
-        functools.partial(spread_border_kernel, own_blocks),
+        spread_border_kernel,
         out_shape=[piece] * levels,
-        in_specs=[SMEM] * 4 + [VMEM] * 2,
+        in_specs=[SMEM] * 4 + [ANY, VMEM],
         out_specs=[VMEM] * levels,
-        scratch_shapes=[pltpu.VMEM((levels * border_size, width, size), f32)],
+        scratch_shapes=[weight, pltpu.VMEM((levels * border_size, width, size), f32), sem],
         compiler_params=PARAMS,
         name="spread_border",
     )(*tables, edge_weights, scaled)
@@ -403,8 +465,9 @@
     total = pl.pallas_call(
         spread_own_kernel,
         out_shape=shape((width, row_count), f32),
-        in_specs=[SMEM] * 4 + [VMEM] * 3,
+        in_specs=[SMEM] * 4 + [ANY] + [VMEM] * 2,
         out_specs=VMEM,
+        scratch_shapes=[weight, sem],
         compiler_params=PARAMS,
         cost_estimate=pl.CostEstimate(flops=4 * 10**9, bytes_accessed=12 * 10**6, transcendentals=0),
         name="spread_own",

time: 141 us -> 121 us (0.86)
  between operations: 14.8 us -> 1.42 us
  Pallas kernels: 102 us -> 93.4 us
  local copies, waits for them, and re-layouts: 4.66 us -> 7.18 us
    pallas_call x4, Pallas kernels: 32.2 us -> 26.8 us  [the longest x1 9.89 us: local(): pl.pallas_call(functools.partial(gather_own_kernel, own_blocks), out_shap...]
    ppermute x6 -> x7, waiting for transfers between devices: 2.85 us -> 6.27 us  [partner(): lax.ppermute(value, axis, [(i, i ^ 1 << apart) for i in range(lax.axis_si...]
    all_gather x1 -> x0, waiting for transfers between devices: 2.59 us -> none  [local(): whole_rows = lax.all_gather(own, 'feat', axis=0, tiled=True)]
    pallas_call x1, Pallas kernels: 10 us -> 7.94 us  [local(): pl.pallas_call(spread_own_kernel, out_shape=shape((width, row_count), f32...]
    reshape x2, local copies, waits for them, and re-layouts: 0.2 us -> 1.72 us  [local(): w.T.reshape(width, groups, width).transpose(1, 0, 2)]
    unnamed x24 -> x22, local copies, waits for them, and re-layouts: 3.79 us -> 4.78 us
    ppermute x6 -> x7, starting transfers between devices: 11.5 us -> 11 us  [partner(): lax.ppermute(value, axis, [(i, i ^ 1 << apart) for i in range(lax.axis_si...]
  transfers between devices with their start and end apart: 7 -> 7, of which waited for: 3 -> 2; matrix products, arithmetic and copies ran while one was open for 2% -> 4% of each run, Pallas kernels for 25% -> 24%
where the time goes in v3:
time: 121 us
  Pallas kernels  93.4 us (77%)
  starting transfers between devices  11 us (9%)
  local copies, waits for them, and re-layouts  7.18 us (6%)
  waiting for transfers between devices  6.27 us (5%)
  between operations  1.42 us (1%)
  other arithmetic  1.35 us (1%)
    pallas_call x1, Pallas kernels, local(): pl.pallas_call(functools.partial(middle_kernel, levels, chunk), out_shape...  55.4 us
    ppermute x7, starting transfers between devices, partner(): lax.ppermute(value, axis, [(i, i ^ 1 << apart) for i in range(lax.axis_si...  11 us
    pallas_call x1, Pallas kernels, local(): pl.pallas_call(functools.partial(gather_own_kernel, own_blocks), out_shap...  9.89 us
    pallas_call x1, Pallas kernels, local(): pl.pallas_call(gather_border_kernel, out_shape=shape((width, row_count),...  8.2 us
    pallas_call x1, Pallas kernels, local(): pl.pallas_call(spread_own_kernel, out_shape=shape((width, row_count), f32...  7.94 us
    pallas_call x1, Pallas kernels, local(): pl.pallas_call(spread_border_kernel, out_shape=[piece] * levels, in_specs...  6.35 us
    ppermute x7, waiting for transfers between devices, partner(): lax.ppermute(value, axis, [(i, i ^ 1 << apart) for i in range(lax.axis_si...  6.27 us
    unnamed x22, local copies, waits for them, and re-layouts  4.78 us
  transfers between devices with their start and end apart: 7, of which 2 were waited for; matrix products, arithmetic and copies ran while one was open for 4% of the time, Pallas kernels for 24%

profile of v3, /device:TPU:0, one launch (start us, length us, event | category | flops | bytes accessed | tf_op | source)
XLA Modules:
  0.0 120.6 jit_solution(8388311200147752122)
XLA Ops:
  0.6 3.0 %collective-permute-start = (bf16[64,8192]{1,0:T(8,128)(2,1)}, bf16[64,8192]{1,0:T(8,128)(2,1)S(1)}, u32[]{:S(2)}, u32[]{:S(2)}) collective-permute-start(bf16[64,8192]{1,0:T(8,128)(2,1)} %bitcast.22), channel_id=1, source_target_pairs={{0,2},{1,3},{2,0},{3,1},{4,6},{5,7},{6,4},{7,5},{8,10},{9,11},{10,... | collective-permute-start | bytes 3145736 | tf_op jit(solution)/shard_map/ppermute | solution.py:23
  3.6 1.3 %copy.20 = s32[1,3,16]{2,1,0:T(4,128)} copy(s32[1,3,16]{2,0,1:T(1,128)} %param.16) | data formatting | bytes 384
  4.9 2.3 %pack.1 = (bf16[16,64,128]{2,1,0:T(8,128)(2,1)}, bf16[16,64,128]{2,1,0:T(8,128)(2,1)}, bf16[16,64,128]{2,1,0:T(8,128)(2,1)}) custom-call(s32[3,16]{1,0:T(4,128)} %bitcast.35, bf16[64,8192]{1,0:T(8,128)(2,1)} %bitcast.23), custom_call_target="tpu_custom_call" | custom-call | tf_op jit(solution)/shard_map/pack/pallas_call | solution.py:383
  7.2 1.5 %collective-permute-start.1 = (bf16[16,64,128]{2,1,0:T(8,128)(2,1)}, bf16[16,64,128]{2,1,0:T(8,128)(2,1)S(1)}, u32[]{:S(2)}, u32[]{:S(2)}) collective-permute-start(bf16[16,64,128]{2,1,0:T(8,128)(2,1)} %get-tuple-element.24), channel_id=1, source_target_pairs={{0,4},{4,0},{8,12},{12,8},{16,20},{20,16},{24,28},{28,24},{1,5},{5... | collective-permute-start | bytes 786440 | tf_op jit(solution)/shard_map/ppermute | solution.py:23
  8.7 1.6 %collective-permute-start.2 = (bf16[16,64,128]{2,1,0:T(8,128)(2,1)}, bf16[16,64,128]{2,1,0:T(8,128)(2,1)S(1)}, u32[]{:S(2)}, u32[]{:S(2)}) collective-permute-start(bf16[16,64,128]{2,1,0:T(8,128)(2,1)} %get-tuple-element.25), channel_id=1, source_target_pairs={{0,8},{4,12},{8,0},{12,4},{16,24},{20,28},{24,16},{28,20},{1,9},{5... | collective-permute-start | bytes 786440 | tf_op jit(solution)/shard_map/ppermute | solution.py:23
  10.3 2.6 %collective-permute-start.3 = (bf16[16,64,128]{2,1,0:T(8,128)(2,1)}, bf16[16,64,128]{2,1,0:T(8,128)(2,1)S(1)}, u32[]{:S(2)}, u32[]{:S(2)}) collective-permute-start(bf16[16,64,128]{2,1,0:T(8,128)(2,1)} %get-tuple-element.26), channel_id=1, source_target_pairs={{0,16},{4,20},{8,24},{12,28},{16,0},{20,4},{24,8},{28,12},{1,17},{... | collective-permute-start | bytes 786440 | tf_op jit(solution)/shard_map/ppermute | solution.py:23
  13.6 0.9 reshape.15
  14.4 0.9 reshape.14
  15.3 0.0 copy-start.9
  15.3 9.9 %gather_own.1 = (f32[64,8192]{1,0:T(8,128)}, s32[544]{0:T(1024)}, s32[544]{0:T(1024)}, s32[544]{0:T(1024)}, s32[2,5]{1,0:T(2,128)}) custom-call(s32[256]{0:T(256)} %rows_ref.1, s32[256]{0:T(256)} %cols_ref.1, s32[1]{0:T(128)S(6)} %copy.22.count_ref, bf16[256,128,128]{2,1,0:T(8,128)(2,1)} %source_ref.7, bf16[64,8192]{1,0:T(8,128)(2,1)} %bitcast.24), custom_call_target="tpu_custom_call" | custom-call | flops 4000000000 | bytes 12000000 | tf_op jit(solution)/shard_map/gather_own/pallas_call | solution.py:395
  25.2 0.7 pad_maximum_fusion.slab_ref
  26.0 0.0 copy-done.9
  26.0 0.6 convert_divide_fusion
  26.6 0.0 collective-permute-done.1.rest_0_
  26.6 0.0 copy-start.5
  26.6 0.0 collective-permute-done.2.rest_1_
  26.6 0.0 copy-start.6
  26.6 0.0 collective-permute-done.3.rest_2_
  26.6 0.0 copy-start.7
  26.6 0.7 copy-done.5
  27.3 0.1 copy-done.6
  27.4 0.1 copy-done.7
  27.5 8.2 %gather_border.1.agg_ref = bf16[64,8192]{1,0:T(8,128)(2,1)} custom-call(s32[544]{0:T(1024)} %get-tuple-element.19.slot_list, s32[544]{0:T(1024)} %get-tuple-element.20.row_list, s32[544]{0:T(1024)} %get-tuple-element.21.col_list, s32[2,5]{1,0:T(2,128)} %get-tuple-element.22.bound_ref, bf16[256,128,128]{2,1,0:T(8,128)(2,1)} %source_ref.7, ...), custom_call_target="tpu_custom_call" | custom-call | tf_op jit(solution)/shard_map/gather_border/pallas_call | solution.py:405
  35.7 0.0 collective-permute-done.cross_ref
  35.7 0.0 copy-start.1
  35.7 1.0 copy-done.1
  36.7 55.4 %middle.1 = (bf16[64,8192]{1,0:T(8,128)(2,1)}, f32[64,8192]{1,0:T(8,128)}, bf16[64,8192]{1,0:T(8,128)(2,1)}, f32[2,64,256]{2,1,0:T(8,128)}) custom-call(bf16[64,8192]{1,0:T(8,128)(2,1)} %bitcast.25, bf16[64,8192]{1,0:T(8,128)(2,1)} %copy-done.1, bf16[64,8192]{1,0:T(8,128)(2,1)} %gather_border.1.agg_ref, bf16[64,256]{1,0:T(8,128)(2,1)} %bitcast.32, ...), custom_call_target="tpu_custom_call" | custom-call | tf_op jit(solution)/shard_map/middle/pallas_call | solution.py:423
  92.1 6.3 %spread_border.1 = (bf16[16,64,128]{2,1,0:T(8,128)(2,1)}, bf16[16,64,128]{2,1,0:T(8,128)(2,1)}, bf16[16,64,128]{2,1,0:T(8,128)(2,1)}) custom-call(s32[544]{0:T(1024)} %get-tuple-element.19.slot_list, s32[544]{0:T(1024)} %get-tuple-element.20.row_list, s32[544]{0:T(1024)} %get-tuple-element.21.col_list, s32[2,5]{1,0:T(2,128)} %get-tuple-element.22.bound_ref, ...), custom_call_target="tpu_custom_call" | custom-call | tf_op jit(solution)/shard_map/spread_border/pallas_call | solution.py:455
  98.5 1.8 %collective-permute-start.4 = (bf16[16,64,128]{2,1,0:T(8,128)(2,1)}, bf16[16,64,128]{2,1,0:T(8,128)(2,1)S(1)}, u32[]{:S(2)}, u32[]{:S(2)}) collective-permute-start(bf16[16,64,128]{2,1,0:T(8,128)(2,1)} %get-tuple-element.30), channel_id=1, source_target_pairs={{0,4},{4,0},{8,12},{12,8},{16,20},{20,16},{24,28},{28,24},{1,5},{5... | collective-permute-start | bytes 786440 | tf_op jit(solution)/shard_map/ppermute | solution.py:23
  100.2 0.0 collective-permute-start.5
  100.2 0.5 collective-permute-start.6
  100.8 0.0 copy-start.8
  100.8 7.9 %spread_own.1.total_ref = f32[64,8192]{1,0:T(8,128)} custom-call(s32[544]{0:T(1024)} %get-tuple-element.19.slot_list, s32[544]{0:T(1024)} %get-tuple-element.20.row_list, s32[544]{0:T(1024)} %get-tuple-element.21.col_list, s32[2,5]{1,0:T(2,128)} %get-tuple-element.22.bound_ref, bf16[256,128,128]{2,1,0:T(8,128)(2,1)} %source_ref.7, ...), custom_call_target="tpu_custom_call" | custom-call | flops 4000000000 | bytes 12000000 | tf_op jit(solution)/shard_map/spread_own/pallas_call | solution.py:465
  108.7 0.0 copy-done.8
  108.7 0.0 copy-start
  108.7 0.7 slice_bitcast_fusion
  109.4 0.0 collective-permute-done.4.rest_0_
  109.4 0.0 copy-start.2
  109.4 3.5 %collective-permute-done.5.rest_1_ = bf16[16,64,128]{2,1,0:T(8,128)(2,1)S(1)} collective-permute-done((bf16[16,64,128]{2,1,0:T(8,128)(2,1)}, bf16[16,64,128]{2,1,0:T(8,128)(2,1)S(1)}, u32[]{:S(2)}, u32[]{:S(2)}) %collective-permute-start.5) | collective-permute-done | bytes 262176 | tf_op jit(solution)/shard_map/ppermute | solution.py:23
  112.8 0.0 copy-start.3
  112.8 2.8 %collective-permute-done.6.rest_2_ = bf16[16,64,128]{2,1,0:T(8,128)(2,1)S(1)} collective-permute-done((bf16[16,64,128]{2,1,0:T(8,128)(2,1)}, bf16[16,64,128]{2,1,0:T(8,128)(2,1)S(1)}, u32[]{:S(2)}, u32[]{:S(2)}) %collective-permute-start.6) | collective-permute-done | bytes 262176 | tf_op jit(solution)/shard_map/ppermute | solution.py:23
  115.7 0.0 copy-done.2
  115.7 0.0 copy-done.3
  115.7 0.0 copy-start.4
  115.7 0.7 copy-done.4
  116.4 3.3 %collect.1 = bf16[64,8192]{1,0:T(8,128)(2,1)} custom-call(s32[3,16]{1,0:T(4,128)} %bitcast.36, f32[64,8192]{1,0:T(8,128)} %spread_own.1.total_ref, bf16[16,64,128]{2,1,0:T(8,128)(2,1)} %copy-done.2, bf16[16,64,128]{2,1,0:T(8,128)(2,1)} %copy-done.3, bf16[16,64,128]{2,1,0:T(8,128)(2,1)} %copy-done.4), custom_call_target="tpu_custom_call" | custom-call | tf_op jit(solution)/shard_map/collect/pallas_call | solution.py:475
  119.6 0.0 copy-done
  119.6 1.0 copy.23
  (1 shorter events, 0.0 us)
Async XLA Ops:
  0.6 35.1 %collective-permute-start = (bf16[64,8192]{1,0:T(8,128)(2,1)}, bf16[64,8192]{1,0:T(8,128)(2,1)S(1)}, u32[]{:S(2)}, u32[]{:S(2)}) collective-permute-start(bf16[64,8192]{1,0:T(8,128)(2,1)} %bitcast.22), channel_id=1, source_target_pairs={{0,2},{1,3},{2,0},{3,1},{4,6},{5,7},{6,4},{7,5},{8,10},{9,11},{10,... | collective-permute-start | bytes 3145736 | tf_op jit(solution)/shard_map/ppermute | solution.py:23
  7.2 19.4 %collective-permute-start.1 = (bf16[16,64,128]{2,1,0:T(8,128)(2,1)}, bf16[16,64,128]{2,1,0:T(8,128)(2,1)S(1)}, u32[]{:S(2)}, u32[]{:S(2)}) collective-permute-start(bf16[16,64,128]{2,1,0:T(8,128)(2,1)} %get-tuple-element.24), channel_id=1, source_target_pairs={{0,4},{4,0},{8,12},{12,8},{16,20},{20,16},{24,28},{28,24},{1,5},{5... | collective-permute-start | bytes 786440 | tf_op jit(solution)/shard_map/ppermute | solution.py:23
  8.7 17.8 %collective-permute-start.2 = (bf16[16,64,128]{2,1,0:T(8,128)(2,1)}, bf16[16,64,128]{2,1,0:T(8,128)(2,1)S(1)}, u32[]{:S(2)}, u32[]{:S(2)}) collective-permute-start(bf16[16,64,128]{2,1,0:T(8,128)(2,1)} %get-tuple-element.25), channel_id=1, source_target_pairs={{0,8},{4,12},{8,0},{12,4},{16,24},{20,28},{24,16},{28,20},{1,9},{5... | collective-permute-start | bytes 786440 | tf_op jit(solution)/shard_map/ppermute | solution.py:23
  10.3 16.3 %collective-permute-start.3 = (bf16[16,64,128]{2,1,0:T(8,128)(2,1)}, bf16[16,64,128]{2,1,0:T(8,128)(2,1)S(1)}, u32[]{:S(2)}, u32[]{:S(2)}) collective-permute-start(bf16[16,64,128]{2,1,0:T(8,128)(2,1)} %get-tuple-element.26), channel_id=1, source_target_pairs={{0,16},{4,20},{8,24},{12,28},{16,0},{20,4},{24,8},{28,12},{1,17},{... | collective-permute-start | bytes 786440 | tf_op jit(solution)/shard_map/ppermute | solution.py:23
  15.3 10.6 %copy-start.9 = (s32[8192]{0:T(1024)S(1)}, s32[8192]{0:T(1024)}, u32[]{:S(2)}) copy-start(s32[8192]{0:T(1024)} %param.11) | copy-start | bytes 98308
  26.6 0.7 copy-start.5
  26.6 0.8 copy-start.6
  26.6 0.9 copy-start.7
  35.7 1.0 copy-start.1
  98.5 10.9 %collective-permute-start.4 = (bf16[16,64,128]{2,1,0:T(8,128)(2,1)}, bf16[16,64,128]{2,1,0:T(8,128)(2,1)S(1)}, u32[]{:S(2)}, u32[]{:S(2)}) collective-permute-start(bf16[16,64,128]{2,1,0:T(8,128)(2,1)} %get-tuple-element.30), channel_id=1, source_target_pairs={{0,4},{4,0},{8,12},{12,8},{16,20},{20,16},{24,28},{28,24},{1,5},{5... | collective-permute-start | bytes 786440 | tf_op jit(solution)/shard_map/ppermute | solution.py:23
  100.2 12.6 %collective-permute-start.5 = (bf16[16,64,128]{2,1,0:T(8,128)(2,1)}, bf16[16,64,128]{2,1,0:T(8,128)(2,1)S(1)}, u32[]{:S(2)}, u32[]{:S(2)}) collective-permute-start(bf16[16,64,128]{2,1,0:T(8,128)(2,1)} %get-tuple-element.31), channel_id=1, source_target_pairs={{0,8},{4,12},{8,0},{12,4},{16,24},{20,28},{24,16},{28,20},{1,9},{5... | collective-permute-start | bytes 786440 | tf_op jit(solution)/shard_map/ppermute | solution.py:23
  100.2 15.4 %collective-permute-start.6 = (bf16[16,64,128]{2,1,0:T(8,128)(2,1)}, bf16[16,64,128]{2,1,0:T(8,128)(2,1)S(1)}, u32[]{:S(2)}, u32[]{:S(2)}) collective-permute-start(bf16[16,64,128]{2,1,0:T(8,128)(2,1)} %get-tuple-element.32), channel_id=1, source_target_pairs={{0,16},{4,20},{8,24},{12,28},{16,0},{20,4},{24,8},{28,12},{1,17},{... | collective-permute-start | bytes 786440 | tf_op jit(solution)/shard_map/ppermute | solution.py:23
  100.8 8.0 %copy-start.8 = (f32[2,64,256]{2,1,0:T(8,128)S(1)}, f32[2,64,256]{2,1,0:T(8,128)}, u32[]{:S(2)}) copy-start(f32[2,64,256]{2,1,0:T(8,128)} %get-tuple-element.33) | copy-start | bytes 393220
  108.7 10.9 %copy-start = (bf16[64,8192]{1,0:T(8,128)(2,1)S(1)}, bf16[64,8192]{1,0:T(8,128)(2,1)}, u32[]{:S(2)}) copy-start(bf16[64,8192]{1,0:T(8,128)(2,1)} %get-tuple-element.27) | copy-start | bytes 3145732
  109.4 6.3 %copy-start.2 = (bf16[16,64,128]{2,1,0:T(8,128)(2,1)}, bf16[16,64,128]{2,1,0:T(8,128)(2,1)S(1)}, u32[]{:S(2)}) copy-start(bf16[16,64,128]{2,1,0:T(8,128)(2,1)S(1)} %collective-permute-done.4.rest_0_) | copy-start | bytes 786436
  112.8 2.8 %copy-start.3 = (bf16[16,64,128]{2,1,0:T(8,128)(2,1)}, bf16[16,64,128]{2,1,0:T(8,128)(2,1)S(1)}, u32[]{:S(2)}) copy-start(bf16[16,64,128]{2,1,0:T(8,128)(2,1)S(1)} %collective-permute-done.5.rest_1_) | copy-start | bytes 786436
  115.7 0.7 copy-start.4

commit v4 on v3

--- a/solution.py
+++ b/solution.py
@@ -15,7 +15,7 @@
 SMEM = pl.BlockSpec(memory_space=pltpu.SMEM)
 VMEM = pl.BlockSpec(memory_space=pltpu.VMEM)
 ANY = pl.BlockSpec(memory_space=pl.ANY)
-PARAMS = pltpu.CompilerParams(vmem_limit_bytes=56 * 1024 * 1024)
+PARAMS = pltpu.CompilerParams(vmem_limit_bytes=24 * 1024 * 1024)
 NT = (((1,), (1,)), ((), ()))
 
 
@@ -61,11 +61,22 @@
     return copies
 
 
+def load_pieces(total_ref, sum_ref, piece_refs, border_ref, sem):
+    border_size = piece_refs[0].shape[0]
+    loads = [pltpu.make_async_copy(total_ref, sum_ref, sem.at[len(piece_refs)])]
+    for level, piece_ref in enumerate(piece_refs):
+        part = border_ref.at[pl.ds(level * border_size, border_size)]
+        loads.append(pltpu.make_async_copy(piece_ref, part, sem.at[level]))
+    for load in loads:
+        load.start()
+    return loads
+
+
 def pack_kernel(sends_ref, table_ref, *piece_refs):
     size = piece_refs[0].shape[2]
     for level, piece_ref in enumerate(piece_refs):
         for j in range(piece_ref.shape[0]):
-            piece_ref[j] = table_ref[:, lanes(sends_ref[level, j], size)]
+            piece_ref[j] = table_ref[:, lanes(sends_ref[level, 0, j], size)]
 
 
 def gather_own_kernel(
@@ -117,15 +128,14 @@
 
 
 def gather_border_kernel(
-    slot_list, row_list, col_list, bound_ref, source_ref, total_ref, inverse_ref, *rest
+    slot_list, row_list, col_list, bound_ref, source_ref, total_ref, degree_ref, *rest
 ):
-    *piece_refs, out_ref, weight_ref, border_ref, sum_ref, sem = rest
+    *piece_refs, out_ref, weight_ref, border_ref, sum_ref, sem, load_sem = rest
+    loads = load_pieces(total_ref, sum_ref, piece_refs, border_ref, load_sem)
     copies = fetch(source_ref, weight_ref, sem)
     size = source_ref.shape[1]
-    border_size = piece_refs[0].shape[0]
-    for level, piece_ref in enumerate(piece_refs):
-        border_ref[level * border_size : (level + 1) * border_size] = piece_ref[...]
-    sum_ref[...] = total_ref[...]
+    for load in loads:
+        load.wait()
 
     def product(slot, row, col):
         return lax.dot_general(
@@ -138,14 +148,15 @@
     for k, copy in enumerate(copies):
         copy.wait()
         for_slots((bound_ref[1, k], bound_ref[1, k + 1]), (slot_list, row_list, col_list), product, store)
-    out_ref[...] = (sum_ref[...] * inverse_ref[...]).astype(jnp.bfloat16)
+    inverse = 1.0 / degree_ref[...].astype(jnp.float32)
+    out_ref[...] = (sum_ref[...] * inverse).astype(jnp.bfloat16)
 
 
 def middle_kernel(
-    levels, chunk, own_ref, cross_ref, agg_ref, self_ref, neigh_ref, slab_ref, cot_ref, inverse_ref,
+    levels, chunk, own_ref, cross_ref, agg_ref, self_ref, neigh_ref, cot_source, degree_ref,
     mixed_ref, direct_ref, scaled_ref, sums_ref,
-    all_agg, all_grad, whole_ref, slabs, back_ref, partial_ref, arrived_ref,
-    gather_send, gather_recv, slab_send, slab_recv, sum_send, sum_recv,
+    all_agg, all_grad, whole_ref, cot_ref, slab_ref, slabs, back_ref, partial_ref, arrived_ref,
+    gather_send, gather_recv, load_sem, slab_send, slab_recv, sum_send, sum_recv,
 ):
     width, nodes = agg_ref.shape
     steps = nodes // chunk
@@ -201,6 +212,18 @@
         moved(table, phase, 1, near, step, near).wait_recv()
         moved(table, phase, 2, far, step, near).wait_recv()
 
+    loads = [
+        pltpu.make_async_copy(source, target, load_sem.at[k])
+        for k, (source, target) in enumerate(
+            (
+                (own_ref, whole_ref.at[rows(me), :]),
+                (cross_ref, whole_ref.at[rows(cross), :]),
+                (cot_source, cot_ref),
+            )
+        )
+    ]
+    for load in loads:
+        load.start()
     barrier = pltpu.get_barrier_semaphore()
     for target in (near, cross, far):
         pl.semaphore_signal(
@@ -211,19 +234,27 @@
             barrier, inc=1, device_id={"nodes": mate}, device_id_type=pl.DeviceIdType.MESH
         )
     all_agg[rows(me), :] = agg_ref[...]
-    whole_ref[rows(me), :] = own_ref[...]
-    whole_ref[rows(cross), :] = cross_ref[...]
+    for group in range(slab_ref.shape[0]):
+        part = slice(group * width, (group + 1) * width)
+        slab_ref[group, :, :width] = self_ref[:, part]
+        slab_ref[group, :, width:] = neigh_ref[:, part]
     slabs[me] = slab_ref[me]
     partial_ref[0] = jnp.zeros(partial_ref.shape[1:], jnp.float32)
     pl.semaphore_wait(barrier, 3 + levels)
 
     def share_agg(step, carry):
         share(all_agg, 0, step)
+        return carry
+
+    def share_rows(step, carry):
         moved(whole_ref, 2, 1, me, step, near).start()
         moved(whole_ref, 2, 2, cross, step, near).start()
         return carry
 
     lax.fori_loop(0, steps, share_agg, 0)
+    for load in loads:
+        load.wait()
+    lax.fori_loop(0, steps, share_rows, 0)
     for kind, target in enumerate((near, cross, far)):
         slab(kind, target).start()
 
@@ -266,7 +297,8 @@
         part = lanes(step, chunk)
         both = jnp.dot(back_ref[...], all_grad[:, part], preferred_element_type=jnp.float32)
         direct_ref[:, part] = both[:width]
-        scaled_ref[:, part] = (both[width:] * inverse_ref[:, part]).astype(jnp.bfloat16)
+        inverse = 1.0 / degree_ref[:, part].astype(jnp.float32)
+        scaled_ref[:, part] = (both[width:] * inverse).astype(jnp.bfloat16)
 
     def project_step(step, carry):
         forward(all_grad, 1, step + 1)
@@ -322,11 +354,13 @@
 
 
 def spread_own_kernel(
-    slot_list, row_list, col_list, bound_ref, source_ref, scaled_ref, direct_ref, total_ref, weight_ref, sem
+    slot_list, row_list, col_list, bound_ref, source_ref, scaled_ref, direct_ref, total_ref, weight_ref, sem, load_sem
 ):
+    load = pltpu.make_async_copy(direct_ref, total_ref, load_sem.at[0])
+    load.start()
     copies = fetch(source_ref, weight_ref, sem)
     size = source_ref.shape[1]
-    total_ref[...] = direct_ref[...]
+    load.wait()
 
     def product(slot, row, col):
         block = scaled_ref[:, lanes(row, size)]
@@ -341,12 +375,14 @@
 
 
 def collect_kernel(sends_ref, total_ref, *rest):
-    piece_refs, out_ref, sum_ref = rest[:-2], rest[-2], rest[-1]
-    size = piece_refs[0].shape[2]
-    sum_ref[...] = total_ref[...]
-    for level, piece_ref in enumerate(piece_refs):
-        for j in range(piece_ref.shape[0]):
-            sum_ref[:, lanes(sends_ref[level, j], size)] += piece_ref[j].astype(jnp.float32)
+    *piece_refs, out_ref, sum_ref, border_ref, load_sem = rest
+    border_size, _, size = piece_refs[0].shape
+    for load in load_pieces(total_ref, sum_ref, piece_refs, border_ref, load_sem):
+        load.wait()
+    for level in range(len(piece_refs)):
+        for j in range(border_size):
+            block = border_ref[level * border_size + j].astype(jnp.float32)
+            sum_ref[:, lanes(sends_ref[level, 0, j], size)] += block
     out_ref[...] = sum_ref[...].astype(jnp.bfloat16)
 
 
@@ -371,14 +407,11 @@
     shape = jax.ShapeDtypeStruct
     bf16, f32, i32 = jnp.bfloat16, jnp.float32, jnp.int32
     piece = shape((border_size, width, size), bf16)
-    inverse = (1.0 / degrees.astype(f32))[None, :]
+    degree = degrees[None, :]
     own = features.T
     cross = partner(own, "feat", 1)
     groups = hidden // width
-    slab = jnp.concatenate(
-        [w.T.reshape(width, groups, width).transpose(1, 0, 2) for w in (w_self, w_neigh)], axis=2
-    )
-    sends = send_lists[0]
+    sends = send_lists.transpose(1, 0, 2)
 
     pieces = pl.pallas_call(
         pack_kernel,
@@ -388,10 +421,11 @@
         compiler_params=PARAMS,
         name="pack",
     )(sends, own)
-    arrived = [partner(value, "nodes", level) for level, value in enumerate(pieces)]
+    arrived = [partner(pieces[level], "nodes", level) for level in reversed(range(levels))][::-1]
     listed = shape((2 * (slot_count + PARTS * TAIL),), i32)
     weight = pltpu.VMEM((slot_count + 1, size, size), bf16)
     sem = pltpu.SemaphoreType.DMA((PARTS,))
+    load_sem = pltpu.SemaphoreType.DMA((levels + 1,))
     total, *tables = pl.pallas_call(
         functools.partial(gather_own_kernel, own_blocks),
         out_shape=[shape((width, row_count), f32), listed, listed, listed, shape((2, PARTS + 1), i32)],
@@ -405,19 +439,20 @@
     aggregated = pl.pallas_call(
         gather_border_kernel,
         out_shape=shape((width, row_count), bf16),
-        in_specs=[SMEM] * 4 + [ANY] + [VMEM] * (2 + levels),
+        in_specs=[SMEM] * 4 + [ANY, ANY, VMEM] + [ANY] * levels,
         out_specs=VMEM,
         scratch_shapes=[
             weight,
             pltpu.VMEM((levels * border_size, width, size), bf16),
             pltpu.VMEM((width, row_count), f32),
             sem,
+            load_sem,
         ],
         compiler_params=PARAMS,
         name="gather_border",
-    )(*tables, edge_weights, total, inverse, *arrived)
-
-    chunk = 8 * size
+    )(*tables, edge_weights, total, degree, *arrived)
+
+    chunk = 4 * size
     steps = row_count // chunk
     dma = pltpu.SemaphoreType.DMA
     mixed, direct, scaled, sums = pl.pallas_call(
@@ -428,12 +463,14 @@
             shape((width, row_count), bf16),
             shape((2, width, hidden), f32),
         ],
-        in_specs=[VMEM] * 8,
+        in_specs=[ANY, ANY, VMEM, VMEM, VMEM, ANY, VMEM],
         out_specs=[VMEM] * 4,
         scratch_shapes=[
             pltpu.VMEM((hidden, row_count), bf16),
             pltpu.VMEM((hidden, row_count), bf16),
             pltpu.VMEM((hidden, row_count), bf16),
+            pltpu.VMEM((width, row_count), bf16),
+            pltpu.VMEM((groups, width, 2 * width), bf16),
             pltpu.VMEM((groups, width, 2 * width), bf16),
             pltpu.VMEM((2 * width, hidden), bf16),
             pltpu.VMEM((levels + 1, 2, width, hidden), f32),
@@ -442,14 +479,15 @@
             dma((3, 3, steps)),
             dma((3,)),
             dma((3,)),
+            dma((3,)),
             dma((levels,)),
             dma((levels,)),
         ],
         compiler_params=pltpu.CompilerParams(
-            vmem_limit_bytes=56 * 1024 * 1024, collective_id=0, has_side_effects=True
+            vmem_limit_bytes=40 * 1024 * 1024, collective_id=0, has_side_effects=True
         ),
         name="middle",
-    )(own, cross, aggregated, w_self.T, w_neigh.T, slab, cotangent.T, inverse)
+    )(own, cross, aggregated, w_self.T, w_neigh.T, cotangent.T, degree)
     grad_self, grad_neigh = sums[0], sums[1]
 
     pieces = pl.pallas_call(
@@ -461,13 +499,13 @@
         compiler_params=PARAMS,
         name="spread_border",
     )(*tables, edge_weights, scaled)
-    returned = [partner(value, "nodes", level) for level, value in enumerate(pieces)]
+    returned = [partner(pieces[level], "nodes", level) for level in reversed(range(levels))][::-1]
     total = pl.pallas_call(
         spread_own_kernel,
         out_shape=shape((width, row_count), f32),
-        in_specs=[SMEM] * 4 + [ANY] + [VMEM] * 2,
+        in_specs=[SMEM] * 4 + [ANY, VMEM, ANY],
         out_specs=VMEM,
-        scratch_shapes=[weight, sem],
+        scratch_shapes=[weight, sem, load_sem],
         compiler_params=PARAMS,
         cost_estimate=pl.CostEstimate(flops=4 * 10**9, bytes_accessed=12 * 10**6, transcendentals=0),
         name="spread_own",
@@ -475,9 +513,13 @@
     grad_features = pl.pallas_call(
         collect_kernel,
         out_shape=shape((width, row_count), bf16),
-        in_specs=[SMEM] + [VMEM] * (1 + levels),
+        in_specs=[SMEM] + [ANY] * (1 + levels),
         out_specs=VMEM,
-        scratch_shapes=[pltpu.VMEM((width, row_count), f32)],
+        scratch_shapes=[
+            pltpu.VMEM((width, row_count), f32),
+            pltpu.VMEM((levels * border_size, width, size), bf16),
+            load_sem,
+        ],
         compiler_params=PARAMS,
         name="collect",
     )(sends, total, *returned)

time: 121 us -> 109 us (0.901)
  Pallas kernels: 93.4 us -> 78.5 us
  local copies, waits for them, and re-layouts: 7.18 us -> 9.56 us
  starting transfers between devices: 11 us -> 12.5 us
  other arithmetic: 1.35 us -> 0 us
    unnamed x22 -> x27, local copies, waits for them, and re-layouts: 4.78 us -> 8.9 us
    pallas_call x1, Pallas kernels: 7.94 us -> 3.91 us  [local(): pl.pallas_call(spread_own_kernel, out_shape=shape((width, row_count), f32...]
    pallas_call x1, Pallas kernels: 8.2 us -> 4.42 us  [local(): pl.pallas_call(gather_border_kernel, out_shape=shape((width, row_count),...]
    pallas_call x1, Pallas kernels: 6.35 us -> 3.46 us  [local(): pl.pallas_call(spread_border_kernel, out_shape=[piece] * levels, in_specs...]
    pallas_call x1, Pallas kernels: 9.89 us -> 7.49 us  [local(): pl.pallas_call(functools.partial(gather_own_kernel, own_blocks), out_shap...]
    reshape x2 -> x0, local copies, waits for them, and re-layouts: 1.72 us -> none  [local(): w.T.reshape(width, groups, width).transpose(1, 0, 2)]
    pallas_call x1, Pallas kernels: 2.32 us -> 0.76 us  [local(): pl.pallas_call(pack_kernel, out_shape=[piece] * levels, in_specs=[SMEM, V...]
    ppermute x7, starting transfers between devices: 11 us -> 12.5 us  [partner(): lax.ppermute(value, axis, [(i, i ^ 1 << apart) for i in range(lax.axis_si...]
  transfers between devices with their start and end apart: 7 -> 7, of which waited for: 2 -> 1; matrix products, arithmetic and copies ran while one was open for 4% -> 1% of each run, Pallas kernels for 24% -> 15%
where the time goes in v4:
time: 109 us; the launch traced here: 108 us
  Pallas kernels  78.5 us (72%)
  starting transfers between devices  12.5 us (11%)
  local copies, waits for them, and re-layouts  9.56 us (9%)
  waiting for transfers between devices  5.89 us (5%)
  between operations  1.47 us (1%)
    pallas_call x1, Pallas kernels, local(): pl.pallas_call(functools.partial(middle_kernel, levels, chunk), out_shape...  56.3 us
    ppermute x7, starting transfers between devices, partner(): lax.ppermute(value, axis, [(i, i ^ 1 << apart) for i in range(lax.axis_si...  12.5 us
    unnamed x27, local copies, waits for them, and re-layouts  8.9 us
    pallas_call x1, Pallas kernels, local(): pl.pallas_call(functools.partial(gather_own_kernel, own_blocks), out_shap...  7.49 us
    ppermute x7, waiting for transfers between devices, partner(): lax.ppermute(value, axis, [(i, i ^ 1 << apart) for i in range(lax.axis_si...  5.89 us
    pallas_call x1, Pallas kernels, local(): pl.pallas_call(gather_border_kernel, out_shape=shape((width, row_count),...  4.42 us
    pallas_call x1, Pallas kernels, local(): pl.pallas_call(spread_own_kernel, out_shape=shape((width, row_count), f32...  3.91 us
    pallas_call x1, Pallas kernels, local(): pl.pallas_call(spread_border_kernel, out_shape=[piece] * levels, in_specs...  3.46 us
  transfers between devices with their start and end apart: 7, of which 1 were waited for; matrix products, arithmetic and copies ran while one was open for 1% of the time, Pallas kernels for 15%

profile of v4, /device:TPU:0, one launch (start us, length us, event | category | flops | bytes accessed | tf_op | source)
XLA Modules:
  0.0 107.9 jit_solution(18061005517402934270)
XLA Ops:
  0.6 3.0 %collective-permute-start = (bf16[64,8192]{1,0:T(8,128)(2,1)}, bf16[64,8192]{1,0:T(8,128)(2,1)S(1)}, u32[]{:S(2)}, u32[]{:S(2)}) collective-permute-start(bf16[64,8192]{1,0:T(8,128)(2,1)} %bitcast.16), channel_id=1, source_target_pairs={{0,2},{1,3},{2,0},{3,1},{4,6},{5,7},{6,4},{7,5},{8,10},{9,11},{10,... | collective-permute-start | bytes 3145736 | tf_op jit(solution)/shard_map/ppermute | solution.py:23
  3.6 0.0 copy-start.2
  3.6 1.3 %copy-done.2 = bf16[8192,64]{0,1:T(8,128)(2,1)S(1)} copy-done((bf16[8192,64]{0,1:T(8,128)(2,1)S(1)}, bf16[8192,64]{0,1:T(8,128)(2,1)}, u32[]{:S(2)}) %copy-start.2) | copy-done | bytes 1048600
  4.9 0.0 copy-start.9
  4.9 0.7 copy-done.9
  5.6 0.8 pack.1
  6.3 1.6 %collective-permute-start.1 = (bf16[16,64,128]{2,1,0:T(8,128)(2,1)S(1)}, bf16[16,64,128]{2,1,0:T(8,128)(2,1)S(1)}, u32[]{:S(2)}, u32[]{:S(2)}) collective-permute-start(bf16[16,64,128]{2,1,0:T(8,128)(2,1)S(1)} %get-tuple-element.24), channel_id=1, source_target_pairs={{0,4},{4,0},{8,12},{12,8},{16,20},{20,16},{24,28},{28,24},{1,5},{5... | collective-permute-start | bytes 786440 | tf_op jit(solution)/shard_map/ppermute | solution.py:23
  7.9 1.6 %collective-permute-start.2 = (bf16[16,64,128]{2,1,0:T(8,128)(2,1)S(1)}, bf16[16,64,128]{2,1,0:T(8,128)(2,1)S(1)}, u32[]{:S(2)}, u32[]{:S(2)}) collective-permute-start(bf16[16,64,128]{2,1,0:T(8,128)(2,1)S(1)} %get-tuple-element.25), channel_id=1, source_target_pairs={{0,8},{4,12},{8,0},{12,4},{16,24},{20,28},{24,16},{28,20},{1,9},{5... | collective-permute-start | bytes 786440 | tf_op jit(solution)/shard_map/ppermute | solution.py:23
  9.5 2.6 %collective-permute-start.3 = (bf16[16,64,128]{2,1,0:T(8,128)(2,1)S(1)}, bf16[16,64,128]{2,1,0:T(8,128)(2,1)S(1)}, u32[]{:S(2)}, u32[]{:S(2)}) collective-permute-start(bf16[16,64,128]{2,1,0:T(8,128)(2,1)S(1)} %get-tuple-element.26), channel_id=1, source_target_pairs={{0,16},{4,20},{8,24},{12,28},{16,0},{20,4},{24,8},{28,12},{1,17},{... | collective-permute-start | bytes 786440 | tf_op jit(solution)/shard_map/ppermute | solution.py:23
  12.7 0.0 copy-start
  12.8 3.4 %copy-done = bf16[256,128,128]{2,1,0:T(8,128)(2,1)S(1)} copy-done((bf16[256,128,128]{2,1,0:T(8,128)(2,1)S(1)}, bf16[256,128,128]{2,1,0:T(8,128)(2,1)}, u32[]{:S(2)}) %copy-start) | copy-done | bytes 8388632
  16.1 0.0 copy-start.3
  16.1 1.2 %copy-done.3 = bf16[8192,64]{0,1:T(8,128)(2,1)S(1)} copy-done((bf16[8192,64]{0,1:T(8,128)(2,1)S(1)}, bf16[8192,64]{0,1:T(8,128)(2,1)}, u32[]{:S(2)}) %copy-start.3) | copy-done | bytes 1048600
  17.4 0.0 copy-start.11
  17.4 0.7 copy-done.11
  18.0 0.0 copy-start.12
  18.0 0.7 copy-done.12
  18.7 0.0 copy-start.1
  18.7 0.0 copy-start.6
  18.7 7.5 %gather_own.1 = (f32[64,8192]{1,0:T(8,128)S(1)}, s32[544]{0:T(1024)S(1)}, s32[544]{0:T(1024)S(1)}, s32[544]{0:T(1024)S(1)}, s32[2,5]{1,0:T(2,128)S(1)}) custom-call(s32[256]{0:T(256)S(1)} %copy-done.11, s32[256]{0:T(256)S(1)} %copy-done.12, s32[1]{0:T(128)S(6)} %copy.15.count_ref, bf16[256,128,128]{2,1,0:T(8,128)(2,1)S(1)} %copy-done, ...), custom_call_target="tpu_custom_call" | custom-call | flops 4000000000 | bytes 12000000 | tf_op jit(solution)/shard_map/gather_own/pallas_call | solution.py:429
  26.2 0.0 collective-permute-done.1.rest_0_
  26.2 0.0 collective-permute-done.2.rest_1_
  26.2 0.0 collective-permute-done.3.rest_2_
  26.3 0.0 copy-done.1
  26.3 0.0 copy-done.6
  26.3 0.0 copy-start.4
  26.3 0.0 copy-start.5
  26.3 0.0 copy-start.7
  26.3 0.0 copy-start.8
  26.3 4.4 %gather_border.1.agg_ref = bf16[64,8192]{1,0:T(8,128)(2,1)S(1)} custom-call(s32[544]{0:T(1024)S(1)} %get-tuple-element.19.slot_list, s32[544]{0:T(1024)S(1)} %get-tuple-element.20.row_list, s32[544]{0:T(1024)S(1)} %get-tuple-element.21.col_list, s32[2,5]{1,0:T(2,128)S(1)} %get-tuple-element.22.bound_ref, bf16[256,128,128]{2,1,0:T(8,128)(2,1)S(1)} %copy-done.1, ...), custom_call_target="tpu_custom_call" | custom-call | tf_op jit(solution)/shard_map/gather_border/pallas_call | solution.py:439
  30.8 0.0 collective-permute-done.cross_ref
  30.8 0.0 copy-done.4
  30.8 0.0 copy-done.5
  30.8 0.0 copy-done.7
  30.8 0.0 copy-done.8
  30.8 56.3 %middle.1 = (bf16[64,8192]{1,0:T(8,128)(2,1)S(1)}, f32[64,8192]{1,0:T(8,128)S(1)}, bf16[64,8192]{1,0:T(8,128)(2,1)S(1)}, f32[2,64,256]{2,1,0:T(8,128)S(1)}) custom-call(bf16[64,8192]{1,0:T(8,128)(2,1)S(1)} %bitcast.19, bf16[64,8192]{1,0:T(8,128)(2,1)S(1)} %collective-permute-done.cross_ref, bf16[64,8192]{1,0:T(8,128)(2,1)S(1)} %gather_border.1.agg_ref, ...), custom_call_target="tpu_custom_call" | custom-call | tf_op jit(solution)/shard_map/middle/pallas_call | solution.py:458
  87.1 3.5 %spread_border.1 = (bf16[16,64,128]{2,1,0:T(8,128)(2,1)S(1)}, bf16[16,64,128]{2,1,0:T(8,128)(2,1)S(1)}, bf16[16,64,128]{2,1,0:T(8,128)(2,1)S(1)}) custom-call(s32[544]{0:T(1024)S(1)} %get-tuple-element.19.slot_list, s32[544]{0:T(1024)S(1)} %get-tuple-element.20.row_list, s32[544]{0:T(1024)S(1)} %get-tuple-element.21.col_list, ...), custom_call_target="tpu_custom_call" | custom-call | tf_op jit(solution)/shard_map/spread_border/pallas_call | solution.py:493
  90.5 1.2 %collective-permute-start.4 = (bf16[16,64,128]{2,1,0:T(8,128)(2,1)S(1)}, bf16[16,64,128]{2,1,0:T(8,128)(2,1)S(1)}, u32[]{:S(2)}, u32[]{:S(2)}) collective-permute-start(bf16[16,64,128]{2,1,0:T(8,128)(2,1)S(1)} %get-tuple-element.30), channel_id=1, source_target_pairs={{0,4},{4,0},{8,12},{12,8},{16,20},{20,16},{24,28},{28,24},{1,5},{5... | collective-permute-start | bytes 786440 | tf_op jit(solution)/shard_map/ppermute | solution.py:23
  91.7 0.0 collective-permute-start.5
  91.7 2.5 %collective-permute-start.6 = (bf16[16,64,128]{2,1,0:T(8,128)(2,1)S(1)}, bf16[16,64,128]{2,1,0:T(8,128)(2,1)S(1)}, u32[]{:S(2)}, u32[]{:S(2)}) collective-permute-start(bf16[16,64,128]{2,1,0:T(8,128)(2,1)S(1)} %get-tuple-element.32), channel_id=1, source_target_pairs={{0,16},{4,20},{8,24},{12,28},{16,0},{20,4},{24,8},{28,12},{1,17},{... | collective-permute-start | bytes 786440 | tf_op jit(solution)/shard_map/ppermute | solution.py:23
  94.3 0.0 copy-start.10
  94.3 3.9 %spread_own.1.total_ref = f32[64,8192]{1,0:T(8,128)S(1)} custom-call(s32[544]{0:T(1024)S(1)} %get-tuple-element.19.slot_list, s32[544]{0:T(1024)S(1)} %get-tuple-element.20.row_list, s32[544]{0:T(1024)S(1)} %get-tuple-element.21.col_list, s32[2,5]{1,0:T(2,128)S(1)} %get-tuple-element.22.bound_ref, bf16[256,128,128]{2,1,0:T(8,128)(2,1)S(1)} %copy-done.1, ...), custom_call_target="tpu_custom_call" | custom-call | flops 4000000000 | bytes 12000000 | tf_op jit(solution)/shard_map/spread_own/pallas_call | solution.py:503
  98.2 0.7 slice_bitcast_fusion
  98.8 0.0 collective-permute-done.4.rest_0_
  98.8 5.9 %collective-permute-done.5.rest_1_ = bf16[16,64,128]{2,1,0:T(8,128)(2,1)S(1)} collective-permute-done((bf16[16,64,128]{2,1,0:T(8,128)(2,1)S(1)}, bf16[16,64,128]{2,1,0:T(8,128)(2,1)S(1)}, u32[]{:S(2)}, u32[]{:S(2)}) %collective-permute-start.5) | collective-permute-done | bytes 262176 | tf_op jit(solution)/shard_map/ppermute | solution.py:23
  104.7 0.0 collective-permute-done.6.rest_2_
  104.7 0.0 copy-done.10
  104.7 2.2 %collect.1 = bf16[64,8192]{1,0:T(8,128)(2,1)} custom-call(s32[3,1,16]{2,1,0:T(1,128)S(1)} %bitcast.27, f32[64,8192]{1,0:T(8,128)S(1)} %spread_own.1.total_ref, bf16[16,64,128]{2,1,0:T(8,128)(2,1)S(1)} %collective-permute-done.4.rest_0_, bf16[16,64,128]{2,1,0:T(8,128)(2,1)S(1)} %collective-permute-done.5.rest_1_, ...), custom_call_target="tpu_custom_call" | custom-call | tf_op jit(solution)/shard_map/collect/pallas_call | solution.py:513
  106.9 1.0 copy.16
Async XLA Ops:
  0.6 30.1 %collective-permute-start = (bf16[64,8192]{1,0:T(8,128)(2,1)}, bf16[64,8192]{1,0:T(8,128)(2,1)S(1)}, u32[]{:S(2)}, u32[]{:S(2)}) collective-permute-start(bf16[64,8192]{1,0:T(8,128)(2,1)} %bitcast.16), channel_id=1, source_target_pairs={{0,2},{1,3},{2,0},{3,1},{4,6},{5,7},{6,4},{7,5},{8,10},{9,11},{10,... | collective-permute-start | bytes 3145736 | tf_op jit(solution)/shard_map/ppermute | solution.py:23
  3.6 1.3 %copy-start.2 = (bf16[8192,64]{0,1:T(8,128)(2,1)S(1)}, bf16[8192,64]{0,1:T(8,128)(2,1)}, u32[]{:S(2)}) copy-start(bf16[8192,64]{0,1:T(8,128)(2,1)} %param.10) | copy-start | bytes 3145732
  4.9 0.7 copy-start.9
  6.3 19.9 %collective-permute-start.1 = (bf16[16,64,128]{2,1,0:T(8,128)(2,1)S(1)}, bf16[16,64,128]{2,1,0:T(8,128)(2,1)S(1)}, u32[]{:S(2)}, u32[]{:S(2)}) collective-permute-start(bf16[16,64,128]{2,1,0:T(8,128)(2,1)S(1)} %get-tuple-element.24), channel_id=1, source_target_pairs={{0,4},{4,0},{8,12},{12,8},{16,20},{20,16},{24,28},{28,24},{1,5},{5... | collective-permute-start | bytes 786440 | tf_op jit(solution)/shard_map/ppermute | solution.py:23
  7.9 18.3 %collective-permute-start.2 = (bf16[16,64,128]{2,1,0:T(8,128)(2,1)S(1)}, bf16[16,64,128]{2,1,0:T(8,128)(2,1)S(1)}, u32[]{:S(2)}, u32[]{:S(2)}) collective-permute-start(bf16[16,64,128]{2,1,0:T(8,128)(2,1)S(1)} %get-tuple-element.25), channel_id=1, source_target_pairs={{0,8},{4,12},{8,0},{12,4},{16,24},{20,28},{24,16},{28,20},{1,9},{5... | collective-permute-start | bytes 786440 | tf_op jit(solution)/shard_map/ppermute | solution.py:23
  9.5 16.7 %collective-permute-start.3 = (bf16[16,64,128]{2,1,0:T(8,128)(2,1)S(1)}, bf16[16,64,128]{2,1,0:T(8,128)(2,1)S(1)}, u32[]{:S(2)}, u32[]{:S(2)}) collective-permute-start(bf16[16,64,128]{2,1,0:T(8,128)(2,1)S(1)} %get-tuple-element.26), channel_id=1, source_target_pairs={{0,16},{4,20},{8,24},{12,28},{16,0},{20,4},{24,8},{28,12},{1,17},{... | collective-permute-start | bytes 786440 | tf_op jit(solution)/shard_map/ppermute | solution.py:23
  12.7 3.4 %copy-start = (bf16[256,128,128]{2,1,0:T(8,128)(2,1)S(1)}, bf16[256,128,128]{2,1,0:T(8,128)(2,1)}, u32[]{:S(2)}) copy-start(bf16[256,128,128]{2,1,0:T(8,128)(2,1)} %source_ref.7) | copy-start | bytes 25165828
  16.1 1.2 %copy-start.3 = (bf16[8192,64]{0,1:T(8,128)(2,1)S(1)}, bf16[8192,64]{0,1:T(8,128)(2,1)}, u32[]{:S(2)}) copy-start(bf16[8192,64]{0,1:T(8,128)(2,1)} %param.10) | copy-start | bytes 3145732
  17.4 0.7 copy-start.11
  18.0 0.7 copy-start.12
  18.7 7.5 %copy-start.1 = (bf16[256,128,128]{2,1,0:T(8,128)(2,1)S(1)}, bf16[256,128,128]{2,1,0:T(8,128)(2,1)}, u32[]{:S(2)}) copy-start(bf16[256,128,128]{2,1,0:T(8,128)(2,1)} %source_ref.7) | copy-start | bytes 25165828
  18.7 7.5 %copy-start.6 = (s32[8192]{0:T(1024)S(1)}, s32[8192]{0:T(1024)}, u32[]{:S(2)}) copy-start(s32[8192]{0:T(1024)} %param.11) | copy-start | bytes 98308
  26.3 4.5 %copy-start.4 = (bf16[8192,64]{0,1:T(8,128)(2,1)S(1)}, bf16[8192,64]{0,1:T(8,128)(2,1)}, u32[]{:S(2)}) copy-start(bf16[8192,64]{0,1:T(8,128)(2,1)} %param.10) | copy-start | bytes 3145732
  26.3 4.5 %copy-start.5 = (bf16[8192,64]{0,1:T(8,128)(2,1)S(1)}, bf16[8192,64]{0,1:T(8,128)(2,1)}, u32[]{:S(2)}) copy-start(bf16[8192,64]{0,1:T(8,128)(2,1)} %param.19) | copy-start | bytes 3145732
  26.3 4.5 %copy-start.7 = (bf16[256,64]{0,1:T(8,128)(2,1)S(1)}, bf16[256,64]{0,1:T(8,128)(2,1)}, u32[]{:S(2)}) copy-start(bf16[256,64]{0,1:T(8,128)(2,1)} %param.17) | copy-start | bytes 98308
  26.3 4.5 %copy-start.8 = (bf16[256,64]{0,1:T(8,128)(2,1)S(1)}, bf16[256,64]{0,1:T(8,128)(2,1)}, u32[]{:S(2)}) copy-start(bf16[256,64]{0,1:T(8,128)(2,1)} %param.18) | copy-start | bytes 98308
  90.5 8.3 %collective-permute-start.4 = (bf16[16,64,128]{2,1,0:T(8,128)(2,1)S(1)}, bf16[16,64,128]{2,1,0:T(8,128)(2,1)S(1)}, u32[]{:S(2)}, u32[]{:S(2)}) collective-permute-start(bf16[16,64,128]{2,1,0:T(8,128)(2,1)S(1)} %get-tuple-element.30), channel_id=1, source_target_pairs={{0,4},{4,0},{8,12},{12,8},{16,20},{20,16},{24,28},{28,24},{1,5},{5... | collective-permute-start | bytes 786440 | tf_op jit(solution)/shard_map/ppermute | solution.py:23
  91.7 13.0 %collective-permute-start.5 = (bf16[16,64,128]{2,1,0:T(8,128)(2,1)S(1)}, bf16[16,64,128]{2,1,0:T(8,128)(2,1)S(1)}, u32[]{:S(2)}, u32[]{:S(2)}) collective-permute-start(bf16[16,64,128]{2,1,0:T(8,128)(2,1)S(1)} %get-tuple-element.31), channel_id=1, source_target_pairs={{0,8},{4,12},{8,0},{12,4},{16,24},{20,28},{24,16},{28,20},{1,9},{5... | collective-permute-start | bytes 786440 | tf_op jit(solution)/shard_map/ppermute | solution.py:23
  91.7 13.0 %collective-permute-start.6 = (bf16[16,64,128]{2,1,0:T(8,128)(2,1)S(1)}, bf16[16,64,128]{2,1,0:T(8,128)(2,1)S(1)}, u32[]{:S(2)}, u32[]{:S(2)}) collective-permute-start(bf16[16,64,128]{2,1,0:T(8,128)(2,1)S(1)} %get-tuple-element.32), channel_id=1, source_target_pairs={{0,16},{4,20},{8,24},{12,28},{16,0},{20,4},{24,8},{28,12},{1,17},{... | collective-permute-start | bytes 786440 | tf_op jit(solution)/shard_map/ppermute | solution.py:23
  94.3 10.5 %copy-start.10 = (s32[1,3,16]{2,0,1:T(1,128)S(1)}, s32[1,3,16]{2,0,1:T(1,128)}, u32[]{:S(2)}) copy-start(s32[1,3,16]{2,0,1:T(1,128)} %param.16) | copy-start | bytes 580

commit v5 on v4

--- a/solution.py
+++ b/solution.py
@@ -72,7 +72,11 @@
     return loads
 
 
-def pack_kernel(sends_ref, table_ref, *piece_refs):
+def pack_kernel(sends_ref, source_ref, *rest):
+    *piece_refs, table_ref, sem = rest
+    load = pltpu.make_async_copy(source_ref, table_ref, sem)
+    load.start()
+    load.wait()
     size = piece_refs[0].shape[2]
     for level, piece_ref in enumerate(piece_refs):
         for j in range(piece_ref.shape[0]):
@@ -80,9 +84,11 @@
 
 
 def gather_own_kernel(
-    own_blocks, rows_ref, cols_ref, count_ref, source_ref, table_ref,
-    total_ref, slot_list, row_list, col_list, bound_ref, weight_ref, sem,
+    own_blocks, rows_ref, cols_ref, count_ref, source_ref, table_source,
+    total_ref, slot_list, row_list, col_list, bound_ref, weight_ref, table_ref, sem, load_sem,
 ):
+    load = pltpu.make_async_copy(table_source, table_ref, load_sem.at[0])
+    load.start()
     copies = fetch(source_ref, weight_ref, sem)
     slots, size, _ = source_ref.shape
     share = slots // PARTS
@@ -122,6 +128,7 @@
     def store(slot, row, col, value):
         total_ref[:, lanes(row, size)] += value
 
+    load.wait()
     for k, copy in enumerate(copies):
         copy.wait()
         for_slots((bound_ref[0, k], bound_ref[0, k + 1]), (slot_list, row_list, col_list), product, store)
@@ -354,8 +361,11 @@
 
 
 def spread_own_kernel(
-    slot_list, row_list, col_list, bound_ref, source_ref, scaled_ref, direct_ref, total_ref, weight_ref, sem, load_sem
+    slot_list, row_list, col_list, bound_ref, source_ref, scaled_ref, direct_ref, mixed_ref,
+    total_ref, copied_ref, weight_ref, sem, load_sem,
 ):
+    copy_mixed = pltpu.make_async_copy(mixed_ref, copied_ref, load_sem.at[1])
+    copy_mixed.start()
     load = pltpu.make_async_copy(direct_ref, total_ref, load_sem.at[0])
     load.start()
     copies = fetch(source_ref, weight_ref, sem)
@@ -372,6 +382,7 @@
     for k, copy in enumerate(copies):
         copy.wait()
         for_slots((bound_ref[0, k], bound_ref[0, k + 1]), (slot_list, row_list, col_list), product, store)
+    copy_mixed.wait()
 
 
 def collect_kernel(sends_ref, total_ref, *rest):
@@ -416,9 +427,10 @@
     pieces = pl.pallas_call(
         pack_kernel,
         out_shape=[piece] * levels,
-        in_specs=[SMEM, VMEM],
+        in_specs=[SMEM, ANY],
         out_specs=[VMEM] * levels,
-        compiler_params=PARAMS,
+        scratch_shapes=[pltpu.VMEM((width, row_count), bf16), pltpu.SemaphoreType.DMA],
+        compiler_params=pltpu.CompilerParams(vmem_limit_bytes=60 * 1024 * 1024),
         name="pack",
     )(sends, own)
     arrived = [partner(pieces[level], "nodes", level) for level in reversed(range(levels))][::-1]
@@ -429,10 +441,10 @@
     total, *tables = pl.pallas_call(
         functools.partial(gather_own_kernel, own_blocks),
         out_shape=[shape((width, row_count), f32), listed, listed, listed, shape((2, PARTS + 1), i32)],
-        in_specs=[SMEM] * 3 + [ANY, VMEM],
+        in_specs=[SMEM] * 3 + [ANY, ANY],
         out_specs=[VMEM] + [SMEM] * 4,
-        scratch_shapes=[weight, sem],
-        compiler_params=PARAMS,
+        scratch_shapes=[weight, pltpu.VMEM((width, row_count), bf16), sem, load_sem],
+        compiler_params=pltpu.CompilerParams(vmem_limit_bytes=46 * 1024 * 1024),
         cost_estimate=pl.CostEstimate(flops=4 * 10**9, bytes_accessed=12 * 10**6, transcendentals=0),
         name="gather_own",
     )(block_rows, block_cols, block_counts, edge_weights, own)
@@ -500,16 +512,16 @@
         name="spread_border",
     )(*tables, edge_weights, scaled)
     returned = [partner(pieces[level], "nodes", level) for level in reversed(range(levels))][::-1]
-    total = pl.pallas_call(
+    total, mixed = pl.pallas_call(
         spread_own_kernel,
-        out_shape=shape((width, row_count), f32),
-        in_specs=[SMEM] * 4 + [ANY, VMEM, ANY],
-        out_specs=VMEM,
+        out_shape=[shape((width, row_count), f32), shape((width, row_count), bf16)],
+        in_specs=[SMEM] * 4 + [ANY, VMEM, ANY, ANY],
+        out_specs=[VMEM, ANY],
         scratch_shapes=[weight, sem, load_sem],
         compiler_params=PARAMS,
         cost_estimate=pl.CostEstimate(flops=4 * 10**9, bytes_accessed=12 * 10**6, transcendentals=0),
         name="spread_own",
-    )(*tables, edge_weights, scaled, direct)
+    )(*tables, edge_weights, scaled, direct, mixed)
     grad_features = pl.pallas_call(
         collect_kernel,
         out_shape=shape((width, row_count), bf16),

time: 109 us -> 106 us (0.972)
  local copies, waits for them, and re-layouts: 9.56 us -> 3.27 us
  Pallas kernels: 78.5 us -> 81.8 us
  waiting for transfers between devices: 5.89 us -> 7.27 us
    unnamed x27 -> x20, local copies, waits for them, and re-layouts: 8.9 us -> 2.61 us
    pallas_call x2, Pallas kernels: 4.67 us -> 7.57 us  [the longest x1 4.58 us: local(): pl.pallas_call(spread_own_kernel, out_shape=[shape((width, row_count), f3...]
    pallas_call x1, Pallas kernels: 56.3 us -> 54.2 us  [local(): pl.pallas_call(functools.partial(middle_kernel, levels, chunk), out_shape...]
    ppermute x7, waiting for transfers between devices: 5.89 us -> 7.27 us  [partner(): lax.ppermute(value, axis, [(i, i ^ 1 << apart) for i in range(lax.axis_si...]
  transfers between devices with their start and end apart: 7 -> 7, of which waited for: 1 -> 2; matrix products, arithmetic and copies ran while one was open for 1% -> 1% of each run, Pallas kernels for 15% -> 20%
where the time goes in v5:
time: 106 us
  Pallas kernels  81.8 us (77%)
  starting transfers between devices  12.1 us (11%)
  waiting for transfers between devices  7.27 us (7%)
  local copies, waits for them, and re-layouts  3.27 us (3%)
  between operations  1.46 us (1%)
    pallas_call x1, Pallas kernels, local(): pl.pallas_call(functools.partial(middle_kernel, levels, chunk), out_shape...  54.2 us
    ppermute x7, starting transfers between devices, partner(): lax.ppermute(value, axis, [(i, i ^ 1 << apart) for i in range(lax.axis_si...  12.1 us
    pallas_call x1, Pallas kernels, local(): pl.pallas_call(functools.partial(gather_own_kernel, own_blocks), out_shap...  8.37 us
    ppermute x7, waiting for transfers between devices, partner(): lax.ppermute(value, axis, [(i, i ^ 1 << apart) for i in range(lax.axis_si...  7.27 us
    pallas_call x1, Pallas kernels, local(): pl.pallas_call(gather_border_kernel, out_shape=shape((width, row_count),...  5.26 us
    pallas_call x1, Pallas kernels, local(): pl.pallas_call(spread_own_kernel, out_shape=[shape((width, row_count), f3...  4.58 us
    pallas_call x1, Pallas kernels, local(): pl.pallas_call(spread_border_kernel, out_shape=[piece] * levels, in_specs...  4.16 us
    pallas_call x1, Pallas kernels, local(): pl.pallas_call(pack_kernel, out_shape=[piece] * levels, in_specs=[SMEM, A...  2.99 us
  transfers between devices with their start and end apart: 7, of which 2 were waited for; matrix products, arithmetic and copies ran while one was open for 1% of the time, Pallas kernels for 20%

profile of v5, /device:TPU:0, one launch (start us, length us, event | category | flops | bytes accessed | tf_op | source)
XLA Modules:
  0.0 105.8 jit_solution(9296218247704339273)
XLA Ops:
  0.6 3.0 %collective-permute-start = (bf16[64,8192]{1,0:T(8,128)(2,1)}, bf16[64,8192]{1,0:T(8,128)(2,1)S(1)}, u32[]{:S(2)}, u32[]{:S(2)}) collective-permute-start(bf16[64,8192]{1,0:T(8,128)(2,1)} %bitcast.16), channel_id=1, source_target_pairs={{0,2},{1,3},{2,0},{3,1},{4,6},{5,7},{6,4},{7,5},{8,10},{9,11},{10,... | collective-permute-start | bytes 3145736 | tf_op jit(solution)/shard_map/ppermute | solution.py:23
  3.6 3.0 %pack.1 = (bf16[16,64,128]{2,1,0:T(8,128)(2,1)}, bf16[16,64,128]{2,1,0:T(8,128)(2,1)}, bf16[16,64,128]{2,1,0:T(8,128)(2,1)}) custom-call(s32[3,1,16]{2,1,0:T(1,128)} %bitcast.25, bf16[64,8192]{1,0:T(8,128)(2,1)} %bitcast.17), custom_call_target="tpu_custom_call" | custom-call | tf_op jit(solution)/shard_map/pack/pallas_call | solution.py:427
  6.6 1.6 %collective-permute-start.1 = (bf16[16,64,128]{2,1,0:T(8,128)(2,1)}, bf16[16,64,128]{2,1,0:T(8,128)(2,1)S(1)}, u32[]{:S(2)}, u32[]{:S(2)}) collective-permute-start(bf16[16,64,128]{2,1,0:T(8,128)(2,1)} %get-tuple-element.26), channel_id=1, source_target_pairs={{0,4},{4,0},{8,12},{12,8},{16,20},{20,16},{24,28},{28,24},{1,5},{5... | collective-permute-start | bytes 786440 | tf_op jit(solution)/shard_map/ppermute | solution.py:23
  8.2 1.6 %collective-permute-start.2 = (bf16[16,64,128]{2,1,0:T(8,128)(2,1)}, bf16[16,64,128]{2,1,0:T(8,128)(2,1)S(1)}, u32[]{:S(2)}, u32[]{:S(2)}) collective-permute-start(bf16[16,64,128]{2,1,0:T(8,128)(2,1)} %get-tuple-element.27), channel_id=1, source_target_pairs={{0,8},{4,12},{8,0},{12,4},{16,24},{20,28},{24,16},{28,20},{1,9},{5... | collective-permute-start | bytes 786440 | tf_op jit(solution)/shard_map/ppermute | solution.py:23
  9.8 2.6 %collective-permute-start.3 = (bf16[16,64,128]{2,1,0:T(8,128)(2,1)}, bf16[16,64,128]{2,1,0:T(8,128)(2,1)S(1)}, u32[]{:S(2)}, u32[]{:S(2)}) collective-permute-start(bf16[16,64,128]{2,1,0:T(8,128)(2,1)} %get-tuple-element.28), channel_id=1, source_target_pairs={{0,16},{4,20},{8,24},{12,28},{16,0},{20,4},{24,8},{28,12},{1,17},{... | collective-permute-start | bytes 786440 | tf_op jit(solution)/shard_map/ppermute | solution.py:23
  13.0 0.0 copy-start.1
  13.0 1.2 %copy-done.1 = bf16[8192,64]{0,1:T(8,128)(2,1)S(1)} copy-done((bf16[8192,64]{0,1:T(8,128)(2,1)S(1)}, bf16[8192,64]{0,1:T(8,128)(2,1)}, u32[]{:S(2)}) %copy-start.1) | copy-done | bytes 1048600
  14.3 0.0 copy-start.8
  14.3 0.7 copy-done.8
  14.9 0.0 copy-start.9
  14.9 0.7 copy-done.9
  15.6 0.0 copy-start
  15.6 0.0 copy-start.4
  15.6 8.4 %gather_own.1 = (f32[64,8192]{1,0:T(8,128)S(1)}, s32[544]{0:T(1024)S(1)}, s32[544]{0:T(1024)S(1)}, s32[544]{0:T(1024)S(1)}, s32[2,5]{1,0:T(2,128)S(1)}) custom-call(s32[256]{0:T(256)S(1)} %copy-done.8, s32[256]{0:T(256)S(1)} %copy-done.9, s32[1]{0:T(128)S(6)} %copy.14.count_ref, bf16[256,128,128]{2,1,0:T(8,128)(2,1)} %source_ref.7, bf16[64,8192]{1,0:T(8,128)(2,1)S(1)} %bitcast.18), custom_call_target="tpu_custom_call" | custom-call | flops 4000000000 | bytes 12000000 | tf_op jit(solution)/shard_map/gather_own/pallas_call | solution.py:441
  24.0 0.0 collective-permute-done.1.rest_0_
  24.0 0.0 collective-permute-done.2.rest_1_
  24.0 0.0 collective-permute-done.3.rest_2_
  24.0 0.0 copy-done
  24.0 0.0 copy-done.4
  24.1 0.0 copy-start.2
  24.1 0.0 copy-start.3
  24.1 0.0 copy-start.5
  24.1 0.0 copy-start.6
  24.1 5.3 %gather_border.1.agg_ref = bf16[64,8192]{1,0:T(8,128)(2,1)S(1)} custom-call(s32[544]{0:T(1024)S(1)} %get-tuple-element.21.slot_list, s32[544]{0:T(1024)S(1)} %get-tuple-element.22.row_list, s32[544]{0:T(1024)S(1)} %get-tuple-element.23.col_list, s32[2,5]{1,0:T(2,128)S(1)} %get-tuple-element.24.bound_ref, bf16[256,128,128]{2,1,0:T(8,128)(2,1)S(1)} %copy-done, ...), custom_call_target="tpu_custom_call" | custom-call | tf_op jit(solution)/shard_map/gather_border/pallas_call | solution.py:451
  29.4 0.0 collective-permute-done.cross_ref
  29.4 0.0 copy-done.2
  29.4 0.0 copy-done.3
  29.4 0.0 copy-done.5
  29.4 0.0 copy-done.6
  29.4 54.2 %middle.1 = (bf16[64,8192]{1,0:T(8,128)(2,1)S(1)}, f32[64,8192]{1,0:T(8,128)S(1)}, bf16[64,8192]{1,0:T(8,128)(2,1)S(1)}, f32[2,64,256]{2,1,0:T(8,128)S(1)}) custom-call(bf16[64,8192]{1,0:T(8,128)(2,1)S(1)} %bitcast.19, bf16[64,8192]{1,0:T(8,128)(2,1)S(1)} %collective-permute-done.cross_ref, bf16[64,8192]{1,0:T(8,128)(2,1)S(1)} %gather_border.1.agg_ref, ...), custom_call_target="tpu_custom_call" | custom-call | tf_op jit(solution)/shard_map/middle/pallas_call | solution.py:470
  83.7 4.2 %spread_border.1 = (bf16[16,64,128]{2,1,0:T(8,128)(2,1)S(1)}, bf16[16,64,128]{2,1,0:T(8,128)(2,1)S(1)}, bf16[16,64,128]{2,1,0:T(8,128)(2,1)S(1)}) custom-call(s32[544]{0:T(1024)S(1)} %get-tuple-element.21.slot_list, s32[544]{0:T(1024)S(1)} %get-tuple-element.22.row_list, s32[544]{0:T(1024)S(1)} %get-tuple-element.23.col_list, ...), custom_call_target="tpu_custom_call" | custom-call | tf_op jit(solution)/shard_map/spread_border/pallas_call | solution.py:505
  87.8 0.2 collective-permute-start.4
  88.0 1.0 collective-permute-start.5
  89.0 2.2 %collective-permute-start.6 = (bf16[16,64,128]{2,1,0:T(8,128)(2,1)S(1)}, bf16[16,64,128]{2,1,0:T(8,128)(2,1)S(1)}, u32[]{:S(2)}, u32[]{:S(2)}) collective-permute-start(bf16[16,64,128]{2,1,0:T(8,128)(2,1)S(1)} %get-tuple-element.36), channel_id=1, source_target_pairs={{0,16},{4,20},{8,24},{12,28},{16,0},{20,4},{24,8},{28,12},{1,17},{... | collective-permute-start | bytes 786440 | tf_op jit(solution)/shard_map/ppermute | solution.py:23
  91.2 0.0 copy-start.7
  91.2 4.6 %spread_own.1 = (f32[64,8192]{1,0:T(8,128)S(1)}, bf16[64,8192]{1,0:T(8,128)(2,1)}) custom-call(s32[544]{0:T(1024)S(1)} %get-tuple-element.21.slot_list, s32[544]{0:T(1024)S(1)} %get-tuple-element.22.row_list, s32[544]{0:T(1024)S(1)} %get-tuple-element.23.col_list, s32[2,5]{1,0:T(2,128)S(1)} %get-tuple-element.24.bound_ref, ...), custom_call_target="tpu_custom_call" | custom-call | flops 4000000000 | bytes 12000000 | tf_op jit(solution)/shard_map/spread_own/pallas_call | solution.py:515
  95.7 0.7 slice_bitcast_fusion
  96.4 0.0 collective-permute-done.4.rest_0_
  96.4 3.7 %collective-permute-done.5.rest_1_ = bf16[16,64,128]{2,1,0:T(8,128)(2,1)S(1)} collective-permute-done((bf16[16,64,128]{2,1,0:T(8,128)(2,1)S(1)}, bf16[16,64,128]{2,1,0:T(8,128)(2,1)S(1)}, u32[]{:S(2)}, u32[]{:S(2)}) %collective-permute-start.5) | collective-permute-done | bytes 262176 | tf_op jit(solution)/shard_map/ppermute | solution.py:23
  100.1 3.5 %collective-permute-done.6.rest_2_ = bf16[16,64,128]{2,1,0:T(8,128)(2,1)S(1)} collective-permute-done((bf16[16,64,128]{2,1,0:T(8,128)(2,1)S(1)}, bf16[16,64,128]{2,1,0:T(8,128)(2,1)S(1)}, u32[]{:S(2)}, u32[]{:S(2)}) %collective-permute-start.6) | collective-permute-done | bytes 262176 | tf_op jit(solution)/shard_map/ppermute | solution.py:23
  103.7 0.0 copy-done.7
  103.7 2.2 %collect.1 = bf16[64,8192]{1,0:T(8,128)(2,1)} custom-call(s32[3,1,16]{2,1,0:T(1,128)S(1)} %bitcast.26, f32[64,8192]{1,0:T(8,128)S(1)} %get-tuple-element.33.total_ref, bf16[16,64,128]{2,1,0:T(8,128)(2,1)S(1)} %collective-permute-done.4.rest_0_, bf16[16,64,128]{2,1,0:T(8,128)(2,1)S(1)} %collective-permute-done.5.rest_1_, ...), custom_call_target="tpu_custom_call" | custom-call | tf_op jit(solution)/shard_map/collect/pallas_call | solution.py:525
Async XLA Ops:
  0.6 28.7 %collective-permute-start = (bf16[64,8192]{1,0:T(8,128)(2,1)}, bf16[64,8192]{1,0:T(8,128)(2,1)S(1)}, u32[]{:S(2)}, u32[]{:S(2)}) collective-permute-start(bf16[64,8192]{1,0:T(8,128)(2,1)} %bitcast.16), channel_id=1, source_target_pairs={{0,2},{1,3},{2,0},{3,1},{4,6},{5,7},{6,4},{7,5},{8,10},{9,11},{10,... | collective-permute-start | bytes 3145736 | tf_op jit(solution)/shard_map/ppermute | solution.py:23
  6.6 17.4 %collective-permute-start.1 = (bf16[16,64,128]{2,1,0:T(8,128)(2,1)}, bf16[16,64,128]{2,1,0:T(8,128)(2,1)S(1)}, u32[]{:S(2)}, u32[]{:S(2)}) collective-permute-start(bf16[16,64,128]{2,1,0:T(8,128)(2,1)} %get-tuple-element.26), channel_id=1, source_target_pairs={{0,4},{4,0},{8,12},{12,8},{16,20},{20,16},{24,28},{28,24},{1,5},{5... | collective-permute-start | bytes 786440 | tf_op jit(solution)/shard_map/ppermute | solution.py:23
  8.2 15.8 %collective-permute-start.2 = (bf16[16,64,128]{2,1,0:T(8,128)(2,1)}, bf16[16,64,128]{2,1,0:T(8,128)(2,1)S(1)}, u32[]{:S(2)}, u32[]{:S(2)}) collective-permute-start(bf16[16,64,128]{2,1,0:T(8,128)(2,1)} %get-tuple-element.27), channel_id=1, source_target_pairs={{0,8},{4,12},{8,0},{12,4},{16,24},{20,28},{24,16},{28,20},{1,9},{5... | collective-permute-start | bytes 786440 | tf_op jit(solution)/shard_map/ppermute | solution.py:23
  9.8 14.2 %collective-permute-start.3 = (bf16[16,64,128]{2,1,0:T(8,128)(2,1)}, bf16[16,64,128]{2,1,0:T(8,128)(2,1)S(1)}, u32[]{:S(2)}, u32[]{:S(2)}) collective-permute-start(bf16[16,64,128]{2,1,0:T(8,128)(2,1)} %get-tuple-element.28), channel_id=1, source_target_pairs={{0,16},{4,20},{8,24},{12,28},{16,0},{20,4},{24,8},{28,12},{1,17},{... | collective-permute-start | bytes 786440 | tf_op jit(solution)/shard_map/ppermute | solution.py:23
  13.0 1.2 %copy-start.1 = (bf16[8192,64]{0,1:T(8,128)(2,1)S(1)}, bf16[8192,64]{0,1:T(8,128)(2,1)}, u32[]{:S(2)}) copy-start(bf16[8192,64]{0,1:T(8,128)(2,1)} %param.10) | copy-start | bytes 3145732
  14.3 0.7 copy-start.8
  14.9 0.7 copy-start.9
  15.6 8.4 %copy-start = (bf16[256,128,128]{2,1,0:T(8,128)(2,1)S(1)}, bf16[256,128,128]{2,1,0:T(8,128)(2,1)}, u32[]{:S(2)}) copy-start(bf16[256,128,128]{2,1,0:T(8,128)(2,1)} %source_ref.7) | copy-start | bytes 25165828
  15.6 8.4 %copy-start.4 = (s32[8192]{0:T(1024)S(1)}, s32[8192]{0:T(1024)}, u32[]{:S(2)}) copy-start(s32[8192]{0:T(1024)} %param.11) | copy-start | bytes 98308
  24.1 5.3 %copy-start.2 = (bf16[8192,64]{0,1:T(8,128)(2,1)S(1)}, bf16[8192,64]{0,1:T(8,128)(2,1)}, u32[]{:S(2)}) copy-start(bf16[8192,64]{0,1:T(8,128)(2,1)} %param.10) | copy-start | bytes 3145732
  24.1 5.3 %copy-start.3 = (bf16[8192,64]{0,1:T(8,128)(2,1)S(1)}, bf16[8192,64]{0,1:T(8,128)(2,1)}, u32[]{:S(2)}) copy-start(bf16[8192,64]{0,1:T(8,128)(2,1)} %param.19) | copy-start | bytes 3145732
  24.1 5.3 %copy-start.5 = (bf16[256,64]{0,1:T(8,128)(2,1)S(1)}, bf16[256,64]{0,1:T(8,128)(2,1)}, u32[]{:S(2)}) copy-start(bf16[256,64]{0,1:T(8,128)(2,1)} %param.17) | copy-start | bytes 98308
  24.1 5.3 %copy-start.6 = (bf16[256,64]{0,1:T(8,128)(2,1)S(1)}, bf16[256,64]{0,1:T(8,128)(2,1)}, u32[]{:S(2)}) copy-start(bf16[256,64]{0,1:T(8,128)(2,1)} %param.18) | copy-start | bytes 98308
  87.8 8.6 %collective-permute-start.4 = (bf16[16,64,128]{2,1,0:T(8,128)(2,1)S(1)}, bf16[16,64,128]{2,1,0:T(8,128)(2,1)S(1)}, u32[]{:S(2)}, u32[]{:S(2)}) collective-permute-start(bf16[16,64,128]{2,1,0:T(8,128)(2,1)S(1)} %get-tuple-element.34), channel_id=1, source_target_pairs={{0,4},{4,0},{8,12},{12,8},{16,20},{20,16},{24,28},{28,24},{1,5},{5... | collective-permute-start | bytes 786440 | tf_op jit(solution)/shard_map/ppermute | solution.py:23
  88.0 12.1 %collective-permute-start.5 = (bf16[16,64,128]{2,1,0:T(8,128)(2,1)S(1)}, bf16[16,64,128]{2,1,0:T(8,128)(2,1)S(1)}, u32[]{:S(2)}, u32[]{:S(2)}) collective-permute-start(bf16[16,64,128]{2,1,0:T(8,128)(2,1)S(1)} %get-tuple-element.35), channel_id=1, source_target_pairs={{0,8},{4,12},{8,0},{12,4},{16,24},{20,28},{24,16},{28,20},{1,9},{5... | collective-permute-start | bytes 786440 | tf_op jit(solution)/shard_map/ppermute | solution.py:23
  89.0 14.7 %collective-permute-start.6 = (bf16[16,64,128]{2,1,0:T(8,128)(2,1)S(1)}, bf16[16,64,128]{2,1,0:T(8,128)(2,1)S(1)}, u32[]{:S(2)}, u32[]{:S(2)}) collective-permute-start(bf16[16,64,128]{2,1,0:T(8,128)(2,1)S(1)} %get-tuple-element.36), channel_id=1, source_target_pairs={{0,16},{4,20},{8,24},{12,28},{16,0},{20,4},{24,8},{28,12},{1,17},{... | collective-permute-start | bytes 786440 | tf_op jit(solution)/shard_map/ppermute | solution.py:23
  91.2 12.5 %copy-start.7 = (s32[1,3,16]{2,0,1:T(1,128)S(1)}, s32[1,3,16]{2,0,1:T(1,128)}, u32[]{:S(2)}) copy-start(s32[1,3,16]{2,0,1:T(1,128)} %param.16) | copy-start | bytes 580

commit v6 on v5

--- a/solution.py
+++ b/solution.py
@@ -241,24 +241,24 @@
             barrier, inc=1, device_id={"nodes": mate}, device_id_type=pl.DeviceIdType.MESH
         )
     all_agg[rows(me), :] = agg_ref[...]
+    pl.semaphore_wait(barrier, 3 + levels)
+
+    def share_agg(step, carry):
+        share(all_agg, 0, step)
+        return carry
+
+    def share_rows(step, carry):
+        moved(whole_ref, 2, 1, me, step, near).start()
+        moved(whole_ref, 2, 2, cross, step, near).start()
+        return carry
+
+    lax.fori_loop(0, steps, share_agg, 0)
     for group in range(slab_ref.shape[0]):
         part = slice(group * width, (group + 1) * width)
         slab_ref[group, :, :width] = self_ref[:, part]
         slab_ref[group, :, width:] = neigh_ref[:, part]
     slabs[me] = slab_ref[me]
     partial_ref[0] = jnp.zeros(partial_ref.shape[1:], jnp.float32)
-    pl.semaphore_wait(barrier, 3 + levels)
-
-    def share_agg(step, carry):
-        share(all_agg, 0, step)
-        return carry
-
-    def share_rows(step, carry):
-        moved(whole_ref, 2, 1, me, step, near).start()
-        moved(whole_ref, 2, 2, cross, step, near).start()
-        return carry
-
-    lax.fori_loop(0, steps, share_agg, 0)
     for load in loads:
         load.wait()
     lax.fori_loop(0, steps, share_rows, 0)

time: 106 us -> 106 us (level)
  transfers between devices with their start and end apart: 7 -> 7, of which waited for: 2 -> 2; matrix products, arithmetic and copies ran while one was open for 1% -> 1% of each run, Pallas kernels for 20% -> 19%
where the time goes in v6:
time: 106 us; the launch traced here: 105 us
  Pallas kernels  80.9 us (76%)
  starting transfers between devices  13.1 us (12%)
  waiting for transfers between devices  6.57 us (6%)
  local copies, waits for them, and re-layouts  3.27 us (3%)
  between operations  1.46 us (1%)
    pallas_call x1, Pallas kernels, local(): pl.pallas_call(functools.partial(middle_kernel, levels, chunk), out_shape...  54.6 us
    ppermute x7, starting transfers between devices, partner(): lax.ppermute(value, axis, [(i, i ^ 1 << apart) for i in range(lax.axis_si...  13.1 us
    pallas_call x1, Pallas kernels, local(): pl.pallas_call(functools.partial(gather_own_kernel, own_blocks), out_shap...  8.15 us
    ppermute x7, waiting for transfers between devices, partner(): lax.ppermute(value, axis, [(i, i ^ 1 << apart) for i in range(lax.axis_si...  6.57 us
    pallas_call x1, Pallas kernels, local(): pl.pallas_call(gather_border_kernel, out_shape=shape((width, row_count),...  4.88 us
    pallas_call x1, Pallas kernels, local(): pl.pallas_call(spread_own_kernel, out_shape=[shape((width, row_count), f3...  4.37 us
    pallas_call x1, Pallas kernels, local(): pl.pallas_call(spread_border_kernel, out_shape=[piece] * levels, in_specs...  3.75 us
    pallas_call x1, Pallas kernels, local(): pl.pallas_call(pack_kernel, out_shape=[piece] * levels, in_specs=[SMEM, A...  2.99 us
  transfers between devices with their start and end apart: 7, of which 2 were waited for; matrix products, arithmetic and copies ran while one was open for 1% of the time, Pallas kernels for 19%

profile of v6, /device:TPU:0, one launch (start us, length us, event | category | flops | bytes accessed | tf_op | source)
XLA Modules:
  0.0 105.3 jit_solution(2896619912783208621)
XLA Ops:
  0.6 3.0 %collective-permute-start = (bf16[64,8192]{1,0:T(8,128)(2,1)}, bf16[64,8192]{1,0:T(8,128)(2,1)S(1)}, u32[]{:S(2)}, u32[]{:S(2)}) collective-permute-start(bf16[64,8192]{1,0:T(8,128)(2,1)} %bitcast.16), channel_id=1, source_target_pairs={{0,2},{1,3},{2,0},{3,1},{4,6},{5,7},{6,4},{7,5},{8,10},{9,11},{10,... | collective-permute-start | bytes 3145736 | tf_op jit(solution)/shard_map/ppermute | solution.py:23
  3.6 3.0 %pack.1 = (bf16[16,64,128]{2,1,0:T(8,128)(2,1)}, bf16[16,64,128]{2,1,0:T(8,128)(2,1)}, bf16[16,64,128]{2,1,0:T(8,128)(2,1)}) custom-call(s32[3,1,16]{2,1,0:T(1,128)} %bitcast.25, bf16[64,8192]{1,0:T(8,128)(2,1)} %bitcast.17), custom_call_target="tpu_custom_call" | custom-call | tf_op jit(solution)/shard_map/pack/pallas_call | solution.py:427
  6.6 1.6 %collective-permute-start.1 = (bf16[16,64,128]{2,1,0:T(8,128)(2,1)}, bf16[16,64,128]{2,1,0:T(8,128)(2,1)S(1)}, u32[]{:S(2)}, u32[]{:S(2)}) collective-permute-start(bf16[16,64,128]{2,1,0:T(8,128)(2,1)} %get-tuple-element.26), channel_id=1, source_target_pairs={{0,4},{4,0},{8,12},{12,8},{16,20},{20,16},{24,28},{28,24},{1,5},{5... | collective-permute-start | bytes 786440 | tf_op jit(solution)/shard_map/ppermute | solution.py:23
  8.2 1.6 %collective-permute-start.2 = (bf16[16,64,128]{2,1,0:T(8,128)(2,1)}, bf16[16,64,128]{2,1,0:T(8,128)(2,1)S(1)}, u32[]{:S(2)}, u32[]{:S(2)}) collective-permute-start(bf16[16,64,128]{2,1,0:T(8,128)(2,1)} %get-tuple-element.27), channel_id=1, source_target_pairs={{0,8},{4,12},{8,0},{12,4},{16,24},{20,28},{24,16},{28,20},{1,9},{5... | collective-permute-start | bytes 786440 | tf_op jit(solution)/shard_map/ppermute | solution.py:23
  9.8 2.6 %collective-permute-start.3 = (bf16[16,64,128]{2,1,0:T(8,128)(2,1)}, bf16[16,64,128]{2,1,0:T(8,128)(2,1)S(1)}, u32[]{:S(2)}, u32[]{:S(2)}) collective-permute-start(bf16[16,64,128]{2,1,0:T(8,128)(2,1)} %get-tuple-element.28), channel_id=1, source_target_pairs={{0,16},{4,20},{8,24},{12,28},{16,0},{20,4},{24,8},{28,12},{1,17},{... | collective-permute-start | bytes 786440 | tf_op jit(solution)/shard_map/ppermute | solution.py:23
  13.0 0.0 copy-start.1
  13.0 1.2 %copy-done.1 = bf16[8192,64]{0,1:T(8,128)(2,1)S(1)} copy-done((bf16[8192,64]{0,1:T(8,128)(2,1)S(1)}, bf16[8192,64]{0,1:T(8,128)(2,1)}, u32[]{:S(2)}) %copy-start.1) | copy-done | bytes 1048600
  14.3 0.0 copy-start.8
  14.3 0.7 copy-done.8
  14.9 0.0 copy-start.9
  14.9 0.7 copy-done.9
  15.6 0.0 copy-start
  15.6 0.0 copy-start.4
  15.6 8.2 %gather_own.1 = (f32[64,8192]{1,0:T(8,128)S(1)}, s32[544]{0:T(1024)S(1)}, s32[544]{0:T(1024)S(1)}, s32[544]{0:T(1024)S(1)}, s32[2,5]{1,0:T(2,128)S(1)}) custom-call(s32[256]{0:T(256)S(1)} %copy-done.8, s32[256]{0:T(256)S(1)} %copy-done.9, s32[1]{0:T(128)S(6)} %copy.14.count_ref, bf16[256,128,128]{2,1,0:T(8,128)(2,1)} %source_ref.7, bf16[64,8192]{1,0:T(8,128)(2,1)S(1)} %bitcast.18), custom_call_target="tpu_custom_call" | custom-call | flops 4000000000 | bytes 12000000 | tf_op jit(solution)/shard_map/gather_own/pallas_call | solution.py:441
  23.8 0.0 collective-permute-done.1.rest_0_
  23.8 0.0 collective-permute-done.2.rest_1_
  23.8 0.0 collective-permute-done.3.rest_2_
  23.8 0.0 copy-done
  23.8 0.0 copy-done.4
  23.8 0.0 copy-start.2
  23.9 0.0 copy-start.3
  23.9 0.0 copy-start.5
  23.9 0.0 copy-start.6
  23.9 4.9 %gather_border.1.agg_ref = bf16[64,8192]{1,0:T(8,128)(2,1)S(1)} custom-call(s32[544]{0:T(1024)S(1)} %get-tuple-element.21.slot_list, s32[544]{0:T(1024)S(1)} %get-tuple-element.22.row_list, s32[544]{0:T(1024)S(1)} %get-tuple-element.23.col_list, s32[2,5]{1,0:T(2,128)S(1)} %get-tuple-element.24.bound_ref, bf16[256,128,128]{2,1,0:T(8,128)(2,1)S(1)} %copy-done, ...), custom_call_target="tpu_custom_call" | custom-call | tf_op jit(solution)/shard_map/gather_border/pallas_call | solution.py:451
  28.8 0.0 collective-permute-done.cross_ref
  28.8 0.0 copy-done.2
  28.8 0.0 copy-done.3
  28.8 0.0 copy-done.5
  28.8 0.0 copy-done.6
  28.8 54.6 %middle.1 = (bf16[64,8192]{1,0:T(8,128)(2,1)S(1)}, f32[64,8192]{1,0:T(8,128)S(1)}, bf16[64,8192]{1,0:T(8,128)(2,1)S(1)}, f32[2,64,256]{2,1,0:T(8,128)S(1)}) custom-call(bf16[64,8192]{1,0:T(8,128)(2,1)S(1)} %bitcast.19, bf16[64,8192]{1,0:T(8,128)(2,1)S(1)} %collective-permute-done.cross_ref, bf16[64,8192]{1,0:T(8,128)(2,1)S(1)} %gather_border.1.agg_ref, ...), custom_call_target="tpu_custom_call" | custom-call | tf_op jit(solution)/shard_map/middle/pallas_call | solution.py:470
  83.4 3.7 %spread_border.1 = (bf16[16,64,128]{2,1,0:T(8,128)(2,1)S(1)}, bf16[16,64,128]{2,1,0:T(8,128)(2,1)S(1)}, bf16[16,64,128]{2,1,0:T(8,128)(2,1)S(1)}) custom-call(s32[544]{0:T(1024)S(1)} %get-tuple-element.21.slot_list, s32[544]{0:T(1024)S(1)} %get-tuple-element.22.row_list, s32[544]{0:T(1024)S(1)} %get-tuple-element.23.col_list, ...), custom_call_target="tpu_custom_call" | custom-call | tf_op jit(solution)/shard_map/spread_border/pallas_call | solution.py:505
  87.2 1.1 %collective-permute-start.4 = (bf16[16,64,128]{2,1,0:T(8,128)(2,1)S(1)}, bf16[16,64,128]{2,1,0:T(8,128)(2,1)S(1)}, u32[]{:S(2)}, u32[]{:S(2)}) collective-permute-start(bf16[16,64,128]{2,1,0:T(8,128)(2,1)S(1)} %get-tuple-element.34), channel_id=1, source_target_pairs={{0,4},{4,0},{8,12},{12,8},{16,20},{20,16},{24,28},{28,24},{1,5},{5... | collective-permute-start | bytes 786440 | tf_op jit(solution)/shard_map/ppermute | solution.py:23
  88.3 0.0 collective-permute-start.5
  88.3 3.3 %collective-permute-start.6 = (bf16[16,64,128]{2,1,0:T(8,128)(2,1)S(1)}, bf16[16,64,128]{2,1,0:T(8,128)(2,1)S(1)}, u32[]{:S(2)}, u32[]{:S(2)}) collective-permute-start(bf16[16,64,128]{2,1,0:T(8,128)(2,1)S(1)} %get-tuple-element.36), channel_id=1, source_target_pairs={{0,16},{4,20},{8,24},{12,28},{16,0},{20,4},{24,8},{28,12},{1,17},{... | collective-permute-start | bytes 786440 | tf_op jit(solution)/shard_map/ppermute | solution.py:23
  91.6 0.0 copy-start.7
  91.6 4.4 %spread_own.1 = (f32[64,8192]{1,0:T(8,128)S(1)}, bf16[64,8192]{1,0:T(8,128)(2,1)}) custom-call(s32[544]{0:T(1024)S(1)} %get-tuple-element.21.slot_list, s32[544]{0:T(1024)S(1)} %get-tuple-element.22.row_list, s32[544]{0:T(1024)S(1)} %get-tuple-element.23.col_list, s32[2,5]{1,0:T(2,128)S(1)} %get-tuple-element.24.bound_ref, ...), custom_call_target="tpu_custom_call" | custom-call | flops 4000000000 | bytes 12000000 | tf_op jit(solution)/shard_map/spread_own/pallas_call | solution.py:515
  95.9 0.7 slice_bitcast_fusion
  96.6 0.0 collective-permute-done.4.rest_0_
  96.6 4.8 %collective-permute-done.5.rest_1_ = bf16[16,64,128]{2,1,0:T(8,128)(2,1)S(1)} collective-permute-done((bf16[16,64,128]{2,1,0:T(8,128)(2,1)S(1)}, bf16[16,64,128]{2,1,0:T(8,128)(2,1)S(1)}, u32[]{:S(2)}, u32[]{:S(2)}) %collective-permute-start.5) | collective-permute-done | bytes 262176 | tf_op jit(solution)/shard_map/ppermute | solution.py:23
  101.4 1.7 %collective-permute-done.6.rest_2_ = bf16[16,64,128]{2,1,0:T(8,128)(2,1)S(1)} collective-permute-done((bf16[16,64,128]{2,1,0:T(8,128)(2,1)S(1)}, bf16[16,64,128]{2,1,0:T(8,128)(2,1)S(1)}, u32[]{:S(2)}, u32[]{:S(2)}) %collective-permute-start.6) | collective-permute-done | bytes 262176 | tf_op jit(solution)/shard_map/ppermute | solution.py:23
  103.2 0.0 copy-done.7
  103.2 2.2 %collect.1 = bf16[64,8192]{1,0:T(8,128)(2,1)} custom-call(s32[3,1,16]{2,1,0:T(1,128)S(1)} %bitcast.26, f32[64,8192]{1,0:T(8,128)S(1)} %get-tuple-element.33.total_ref, bf16[16,64,128]{2,1,0:T(8,128)(2,1)S(1)} %collective-permute-done.4.rest_0_, bf16[16,64,128]{2,1,0:T(8,128)(2,1)S(1)} %collective-permute-done.5.rest_1_, ...), custom_call_target="tpu_custom_call" | custom-call | tf_op jit(solution)/shard_map/collect/pallas_call | solution.py:525
Async XLA Ops:
  0.6 28.2 %collective-permute-start = (bf16[64,8192]{1,0:T(8,128)(2,1)}, bf16[64,8192]{1,0:T(8,128)(2,1)S(1)}, u32[]{:S(2)}, u32[]{:S(2)}) collective-permute-start(bf16[64,8192]{1,0:T(8,128)(2,1)} %bitcast.16), channel_id=1, source_target_pairs={{0,2},{1,3},{2,0},{3,1},{4,6},{5,7},{6,4},{7,5},{8,10},{9,11},{10,... | collective-permute-start | bytes 3145736 | tf_op jit(solution)/shard_map/ppermute | solution.py:23
  6.6 17.2 %collective-permute-start.1 = (bf16[16,64,128]{2,1,0:T(8,128)(2,1)}, bf16[16,64,128]{2,1,0:T(8,128)(2,1)S(1)}, u32[]{:S(2)}, u32[]{:S(2)}) collective-permute-start(bf16[16,64,128]{2,1,0:T(8,128)(2,1)} %get-tuple-element.26), channel_id=1, source_target_pairs={{0,4},{4,0},{8,12},{12,8},{16,20},{20,16},{24,28},{28,24},{1,5},{5... | collective-permute-start | bytes 786440 | tf_op jit(solution)/shard_map/ppermute | solution.py:23
  8.2 15.6 %collective-permute-start.2 = (bf16[16,64,128]{2,1,0:T(8,128)(2,1)}, bf16[16,64,128]{2,1,0:T(8,128)(2,1)S(1)}, u32[]{:S(2)}, u32[]{:S(2)}) collective-permute-start(bf16[16,64,128]{2,1,0:T(8,128)(2,1)} %get-tuple-element.27), channel_id=1, source_target_pairs={{0,8},{4,12},{8,0},{12,4},{16,24},{20,28},{24,16},{28,20},{1,9},{5... | collective-permute-start | bytes 786440 | tf_op jit(solution)/shard_map/ppermute | solution.py:23
  9.8 14.0 %collective-permute-start.3 = (bf16[16,64,128]{2,1,0:T(8,128)(2,1)}, bf16[16,64,128]{2,1,0:T(8,128)(2,1)S(1)}, u32[]{:S(2)}, u32[]{:S(2)}) collective-permute-start(bf16[16,64,128]{2,1,0:T(8,128)(2,1)} %get-tuple-element.28), channel_id=1, source_target_pairs={{0,16},{4,20},{8,24},{12,28},{16,0},{20,4},{24,8},{28,12},{1,17},{... | collective-permute-start | bytes 786440 | tf_op jit(solution)/shard_map/ppermute | solution.py:23
  13.0 1.2 %copy-start.1 = (bf16[8192,64]{0,1:T(8,128)(2,1)S(1)}, bf16[8192,64]{0,1:T(8,128)(2,1)}, u32[]{:S(2)}) copy-start(bf16[8192,64]{0,1:T(8,128)(2,1)} %param.10) | copy-start | bytes 3145732
  14.3 0.7 copy-start.8
  14.9 0.7 copy-start.9
  15.6 8.2 %copy-start = (bf16[256,128,128]{2,1,0:T(8,128)(2,1)S(1)}, bf16[256,128,128]{2,1,0:T(8,128)(2,1)}, u32[]{:S(2)}) copy-start(bf16[256,128,128]{2,1,0:T(8,128)(2,1)} %source_ref.7) | copy-start | bytes 25165828
  15.6 8.2 %copy-start.4 = (s32[8192]{0:T(1024)S(1)}, s32[8192]{0:T(1024)}, u32[]{:S(2)}) copy-start(s32[8192]{0:T(1024)} %param.11) | copy-start | bytes 98308
  23.8 5.0 %copy-start.2 = (bf16[8192,64]{0,1:T(8,128)(2,1)S(1)}, bf16[8192,64]{0,1:T(8,128)(2,1)}, u32[]{:S(2)}) copy-start(bf16[8192,64]{0,1:T(8,128)(2,1)} %param.10) | copy-start | bytes 3145732
  23.9 4.9 %copy-start.3 = (bf16[8192,64]{0,1:T(8,128)(2,1)S(1)}, bf16[8192,64]{0,1:T(8,128)(2,1)}, u32[]{:S(2)}) copy-start(bf16[8192,64]{0,1:T(8,128)(2,1)} %param.19) | copy-start | bytes 3145732
  23.9 4.9 %copy-start.5 = (bf16[256,64]{0,1:T(8,128)(2,1)S(1)}, bf16[256,64]{0,1:T(8,128)(2,1)}, u32[]{:S(2)}) copy-start(bf16[256,64]{0,1:T(8,128)(2,1)} %param.17) | copy-start | bytes 98308
  23.9 4.9 %copy-start.6 = (bf16[256,64]{0,1:T(8,128)(2,1)S(1)}, bf16[256,64]{0,1:T(8,128)(2,1)}, u32[]{:S(2)}) copy-start(bf16[256,64]{0,1:T(8,128)(2,1)} %param.18) | copy-start | bytes 98308
  87.2 9.4 %collective-permute-start.4 = (bf16[16,64,128]{2,1,0:T(8,128)(2,1)S(1)}, bf16[16,64,128]{2,1,0:T(8,128)(2,1)S(1)}, u32[]{:S(2)}, u32[]{:S(2)}) collective-permute-start(bf16[16,64,128]{2,1,0:T(8,128)(2,1)S(1)} %get-tuple-element.34), channel_id=1, source_target_pairs={{0,4},{4,0},{8,12},{12,8},{16,20},{20,16},{24,28},{28,24},{1,5},{5... | collective-permute-start | bytes 786440 | tf_op jit(solution)/shard_map/ppermute | solution.py:23
  88.3 13.1 %collective-permute-start.5 = (bf16[16,64,128]{2,1,0:T(8,128)(2,1)S(1)}, bf16[16,64,128]{2,1,0:T(8,128)(2,1)S(1)}, u32[]{:S(2)}, u32[]{:S(2)}) collective-permute-start(bf16[16,64,128]{2,1,0:T(8,128)(2,1)S(1)} %get-tuple-element.35), channel_id=1, source_target_pairs={{0,8},{4,12},{8,0},{12,4},{16,24},{20,28},{24,16},{28,20},{1,9},{5... | collective-permute-start | bytes 786440 | tf_op jit(solution)/shard_map/ppermute | solution.py:23
  88.3 14.9 %collective-permute-start.6 = (bf16[16,64,128]{2,1,0:T(8,128)(2,1)S(1)}, bf16[16,64,128]{2,1,0:T(8,128)(2,1)S(1)}, u32[]{:S(2)}, u32[]{:S(2)}) collective-permute-start(bf16[16,64,128]{2,1,0:T(8,128)(2,1)S(1)} %get-tuple-element.36), channel_id=1, source_target_pairs={{0,16},{4,20},{8,24},{12,28},{16,0},{20,4},{24,8},{28,12},{1,17},{... | collective-permute-start | bytes 786440 | tf_op jit(solution)/shard_map/ppermute | solution.py:23
  91.6 11.6 %copy-start.7 = (s32[1,3,16]{2,0,1:T(1,128)S(1)}, s32[1,3,16]{2,0,1:T(1,128)}, u32[]{:S(2)}) copy-start(s32[1,3,16]{2,0,1:T(1,128)} %param.16) | copy-start | bytes 580
